TPU v7x, 32 devices: a whole 2x2x4 slice. The times are simulated.
32 devices in a mesh: wide: 8 (over z, x), narrow: 4 (over y, core).
Axes of the slice: x: 2, y: 2, z: 4, core: 2. Of those that a mesh axis runs over, the one named last changes fastest.
Arguments:
- block_in: bfloat16 [128, 208, 768], P(('wide', 'narrow')), may hold values from -6 to 6
- out_grad: bfloat16 [128, 208, 768], P(('wide', 'narrow')), may hold values from -6 to 6
- lengths: int32 [128], P(('wide', 'narrow')), may hold values from 10 to 202, as said below
- feature_proj: float32 [12, 32, 64], replicated, may hold values from -5 to 5
- attn_in: float32 [3, 768, 768], P(None, 'wide'), may hold values from -0.21875 to 0.21875
- attn_out: float32 [768, 768], P('wide'), may hold values from -1.75 to 1.75
- ffn_in: float32 [768, 3072], P('wide'), may hold values from -0.21875 to 0.21875
- ffn_out: float32 [3072, 768], P('wide'), may hold values from -0.109375 to 0.109375
- norm_params: float32 [4, 768], P(None, 'wide')
- bias_in: float32 [3072], P('wide'), may hold values from -4 to 4
- bias_out: float32 [768], P('wide'), may hold values from -4 to 4
- mom_attn_in: float32 [3, 768, 768], P(None, 'wide', 'narrow')
- mom_attn_out: float32 [768, 768], P('wide', 'narrow')
- mom_ffn_in: float32 [768, 3072], P('wide', 'narrow')
- mom_ffn_out: float32 [3072, 768], P('wide', 'narrow')
- first_norms: float32 [4, 768], P(None, ('wide', 'narrow'))
- first_bias_in: float32 [3072], P(('wide', 'narrow'))
- first_bias_out: float32 [768], P(('wide', 'narrow'))
- second_norms: float32 [4, 768], P(None, ('wide', 'narrow'))
- second_bias_in: float32 [3072], P(('wide', 'narrow'))
- second_bias_out: float32 [768], P(('wide', 'narrow'))
Outputs:
- block_out: float32 [128, 208, 768], P(('wide', 'narrow'))
- input_grad: float32 [128, 208, 768], P(('wide', 'narrow'))
- grad_attn_in: float32 [3, 768, 768], P(None, 'wide', 'narrow')
- grad_attn_out: float32 [768, 768], P('wide', 'narrow')
- grad_ffn_in: float32 [768, 3072], P('wide', 'narrow')
- grad_ffn_out: float32 [3072, 768], P('wide', 'narrow')
- grad_norms: float32 [4, 768], P(None, ('wide', 'narrow'))
- grad_bias_in: float32 [3072], P(('wide', 'narrow'))
- grad_bias_out: float32 [768], P(('wide', 'narrow'))
- new_mom_attn_in: float32 [3, 768, 768], P(None, 'wide', 'narrow')
- new_mom_attn_out: float32 [768, 768], P('wide', 'narrow')
- new_mom_ffn_in: float32 [768, 3072], P('wide', 'narrow')
- new_mom_ffn_out: float32 [3072, 768], P('wide', 'narrow')
- new_attn_in: float32 [3, 768, 768], P(None, 'wide', 'narrow')
- new_attn_out: float32 [768, 768], P('wide', 'narrow')
- new_ffn_in: float32 [768, 3072], P('wide', 'narrow')
- new_ffn_out: float32 [3072, 768], P('wide', 'narrow')
- new_first_norms: float32 [4, 768], P(None, ('wide', 'narrow'))
- new_first_bias_in: float32 [3072], P(('wide', 'narrow'))
- new_first_bias_out: float32 [768], P(('wide', 'narrow'))
- new_second_norm_one: float32 [2, 768], P(None, ('wide', 'narrow'))
- new_second_norm_two: float32 [2, 768], P(None, ('wide', 'narrow'))
- new_second_bias_in: float32 [3072], P(('wide', 'narrow'))
- new_second_bias_out: float32 [768], P(('wide', 'narrow'))
- new_norm_params: float32 [4, 768], P(None, ('wide', 'narrow'))
- new_bias_in: float32 [3072], P(('wide', 'narrow'))
- new_bias_out: float32 [768], P(('wide', 'narrow'))
Inputs may be any that keep to these rules, and one draw needn't show every extreme that they name: `lengths`: in each aligned group of four consecutive molecules (0 to 3, 4 to 7 and so on) at least one molecule has 202 tokens.
All inputs are finite; a program needn't handle non-finite values.
Results may differ from a plain program's by a relative error of at most 0.014.
The roundings to bfloat16 on the way count: a program that leaves them out, or rounds other values in their place, can miss the bound.
Values may be sent and summed in bfloat16 or wider, within the bound.
No kernel may reach another device: no remote copies, remote signals or barrier semaphores. Data moves between devices by JAX's collectives and lax.ppermute only.
A program may use at most 192 MiB of HBM per device.

v0:
```python
from functools import partial
import math

import jax
import jax.numpy as jnp
from jax import lax
from jax.sharding import PartitionSpec as P

D = 768
FF = 3072
HEADS = 12
HDIM = 64
NS_ITERS = 5
ADAM_STEP = 10


PRECISE = lax.Precision.HIGHEST
NORM_EPS = 1e-05
ORTHO_EPS = 1e-07
ADAM_EPS = 1e-08
LINEAR_COEF = 3.4445
CUBIC_COEF = -4.775
QUINTIC_COEF = 2.0315
MOMENT_DECAY = 0.5
FIRST_DECAY = 0.5
SECOND_DECAY = 0.5
MUON_SCALE = 0.6
WEIGHT_DECAY = 0.01
VECTOR_RATE = 0.4


def layer_norm_apply(row_vals, gain_vals, shift_vals):
    centered = row_vals - jnp.mean(row_vals, axis=-1, keepdims=True)
    inverse = lax.rsqrt(jnp.mean(centered * centered, axis=-1, keepdims=True) + NORM_EPS)
    return centered * inverse * gain_vals + shift_vals


def rotary_tables(length, head_width):
    half_width = head_width // 2
    frequency = jnp.exp(
        jnp.arange(half_width, dtype=jnp.float32) * (-2.0 * math.log(10000.0) / head_width)
    )
    angles = jnp.arange(length, dtype=jnp.float32)[:, None] * frequency[None, :]
    return (jnp.cos(angles), jnp.sin(angles))


def rotate_heads(tensor, cosine_table, sine_table):
    half_width = tensor.shape[-1] // 2
    leading = tensor[..., :half_width]
    trailing = tensor[..., half_width:]
    cosine_wide = cosine_table[None, :, None, :]
    sine_wide = sine_table[None, :, None, :]
    return jnp.concatenate(
        [
            leading * cosine_wide - trailing * sine_wide,
            trailing * cosine_wide + leading * sine_wide,
        ],
        axis=-1,
    )


def feature_map(rotated, feature_proj):
    unit_heads = rotated * rotated.shape[-1] ** (-0.25)
    projected = jnp.einsum("slhe,hfe->slhf", unit_heads, feature_proj, precision=PRECISE)
    squared = 0.5 * jnp.sum(unit_heads * unit_heads, axis=-1, keepdims=True)
    return jnp.exp(projected - squared) * feature_proj.shape[1] ** (-0.5)


def rotate_features(head_vals, cosine_table, sine_table, feature_proj):
    return feature_map(rotate_heads(head_vals, cosine_table, sine_table), feature_proj)


def forward(params, flat_in, live_mask, cosine_table, sine_table, feature_proj):
    w_qkv, w_out, w_in, w_back, norm_low, bias_inner_low, bias_final_low = params
    seq_count, length = live_mask.shape
    head_shape = (seq_count, length, HEADS, HDIM)
    norm_vals = norm_low.astype(jnp.float32)
    hidden_one = layer_norm_apply(flat_in, norm_vals[0], norm_vals[1]).astype(jnp.bfloat16)
    projected = jnp.einsum("td,jde->jte", hidden_one, w_qkv, preferred_element_type=jnp.float32)
    query_feats = rotate_features(
        projected[0].reshape(head_shape), cosine_table, sine_table, feature_proj
    )
    key_feats = rotate_features(
        projected[1].reshape(head_shape), cosine_table, sine_table, feature_proj
    )
    query_low = query_feats.astype(jnp.bfloat16)
    key_low = key_feats.astype(jnp.bfloat16) * live_mask[:, :, None, None].astype(jnp.bfloat16)
    value_low = projected[2].astype(jnp.bfloat16).reshape(head_shape)
    kv_state = jnp.einsum("slhf,slhe->shfe", key_low, value_low, preferred_element_type=jnp.float32)
    state_low = kv_state.astype(jnp.bfloat16)
    key_total = jnp.sum(key_low.astype(jnp.float32), axis=1)
    numerator = jnp.einsum(
        "slhf,shfe->slhe", query_low, state_low, preferred_element_type=jnp.float32
    )
    denominator = jnp.einsum(
        "slhf,shf->slh", query_low.astype(jnp.float32), key_total, precision=PRECISE
    )
    attended = numerator / denominator[..., None]
    mixed_low = attended.reshape(seq_count * length, D).astype(jnp.bfloat16)
    middle = flat_in + jnp.dot(mixed_low, w_out, preferred_element_type=jnp.float32)
    hidden_two = layer_norm_apply(middle, norm_vals[2], norm_vals[3]).astype(jnp.bfloat16)
    inner_pre = jnp.dot(
        hidden_two, w_in, preferred_element_type=jnp.float32
    ) + bias_inner_low.astype(jnp.float32)
    act_low = jax.nn.gelu(inner_pre, approximate=False).astype(jnp.bfloat16)
    result = middle + (
        jnp.dot(act_low, w_back, preferred_element_type=jnp.float32)
        + bias_final_low.astype(jnp.float32)
    )
    kept_values = (
        hidden_one,
        projected,
        query_low,
        key_low,
        value_low,
        state_low,
        key_total,
        denominator,
        attended,
        mixed_low,
        middle,
        hidden_two,
        inner_pre,
        act_low,
    )
    return (result, kept_values)


def backward(
    params, kept_values, flat_in, grad_final, live_mask, cosine_table, sine_table, feature_proj
):
    w_qkv, w_out, w_in, w_back, norm_low, bias_inner_low, bias_final_low = params
    (
        hidden_one,
        projected,
        query_low,
        key_low,
        value_low,
        state_low,
        key_total,
        denominator,
        attended,
        mixed_low,
        middle,
        hidden_two,
        inner_pre,
        act_low,
    ) = kept_values
    seq_count, length = live_mask.shape
    head_shape = (seq_count, length, HEADS, HDIM)
    norm_vals = norm_low.astype(jnp.float32)
    grad_bias_final = jnp.sum(grad_final.astype(jnp.float32), axis=0)
    grad_w_back = jnp.einsum("tf,td->fd", act_low, grad_final, preferred_element_type=jnp.float32)
    grad_act = jnp.einsum("td,fd->tf", grad_final, w_back, preferred_element_type=jnp.float32)
    unused_gelu, gelu_pull = jax.vjp(partial(jax.nn.gelu, approximate=False), inner_pre)
    grad_inner = gelu_pull(grad_act)[0].astype(jnp.bfloat16)
    grad_bias_inner = jnp.sum(grad_inner.astype(jnp.float32), axis=0)
    grad_w_in = jnp.einsum("td,tf->df", hidden_two, grad_inner, preferred_element_type=jnp.float32)
    grad_hidden_two = jnp.einsum("tf,df->td", grad_inner, w_in, preferred_element_type=jnp.float32)
    unused_two, norm_two_pull = jax.vjp(layer_norm_apply, middle, norm_vals[2], norm_vals[3])
    grad_mid_part, grad_gain_two, grad_shift_two = norm_two_pull(grad_hidden_two)
    grad_middle = grad_final.astype(jnp.float32) + grad_mid_part
    grad_branch = grad_middle.astype(jnp.bfloat16)
    grad_w_out = jnp.einsum("td,te->de", mixed_low, grad_branch, preferred_element_type=jnp.float32)
    grad_attended = jnp.einsum(
        "te,de->td", grad_branch, w_out, preferred_element_type=jnp.float32
    ).reshape(attended.shape)
    grad_numer = grad_attended / denominator[..., None]
    grad_denom = -jnp.sum(grad_attended * attended, axis=-1) / denominator
    query_vals = query_low.astype(jnp.float32)
    state_vals = state_low.astype(jnp.float32)
    grad_qfeat = (
        jnp.einsum("slhe,shfe->slhf", grad_numer, state_vals, precision=PRECISE)
        + grad_denom[..., None] * key_total[:, None]
    )
    grad_state = jnp.einsum("slhf,slhe->shfe", query_vals, grad_numer, precision=PRECISE)
    grad_total = jnp.einsum("slhf,slh->shf", query_vals, grad_denom, precision=PRECISE)
    grad_kfeat = (
        jnp.einsum("shfe,slhe->slhf", grad_state, value_low.astype(jnp.float32), precision=PRECISE)
        + grad_total[:, None]
    ) * live_mask[:, :, None, None]
    grad_values = jnp.einsum(
        "slhf,shfe->slhe", key_low.astype(jnp.float32), grad_state, precision=PRECISE
    )
    feature_fn = partial(
        rotate_features, cosine_table=cosine_table, sine_table=sine_table, feature_proj=feature_proj
    )
    unused_query, query_pull = jax.vjp(feature_fn, projected[0].reshape(head_shape))
    unused_key, key_pull = jax.vjp(feature_fn, projected[1].reshape(head_shape))
    grad_queries = query_pull(grad_qfeat)[0]
    grad_keys = key_pull(grad_kfeat)[0]
    row_total = seq_count * length
    grad_projected = jnp.stack(
        [
            grad_queries.reshape(row_total, D),
            grad_keys.reshape(row_total, D),
            grad_values.reshape(row_total, D),
        ]
    ).astype(jnp.bfloat16)
    grad_w_qkv = jnp.einsum(
        "td,jte->jde", hidden_one, grad_projected, preferred_element_type=jnp.float32
    )
    grad_hidden_one = jnp.einsum(
        "jte,jde->td", grad_projected, w_qkv, preferred_element_type=jnp.float32
    )
    unused_one, norm_one_pull = jax.vjp(layer_norm_apply, flat_in, norm_vals[0], norm_vals[1])
    grad_in_part, grad_gain_one, grad_shift_one = norm_one_pull(grad_hidden_one)
    grad_input = grad_middle + grad_in_part
    grad_norm_vals = jnp.stack([grad_gain_one, grad_shift_one, grad_gain_two, grad_shift_two])
    return (
        grad_input,
        (
            grad_w_qkv,
            grad_w_out,
            grad_w_in,
            grad_w_back,
            grad_norm_vals,
            grad_bias_inner,
            grad_bias_final,
        ),
    )


def gram_of(matrices):
    return jnp.einsum("brc,bsc->brs", matrices, matrices, precision=PRECISE)


def ortho_step(iterate, gram_mat):
    poly_mat = CUBIC_COEF * gram_mat + QUINTIC_COEF * jnp.einsum(
        "brs,bst->brt", gram_mat, gram_mat, precision=PRECISE
    )
    return LINEAR_COEF * iterate + jnp.einsum("brs,bsc->brc", poly_mat, iterate, precision=PRECISE)


def adam_update(param, earlier_first, earlier_second, gradient):
    first_new = FIRST_DECAY * earlier_first + (1.0 - FIRST_DECAY) * gradient
    second_new = SECOND_DECAY * earlier_second + (1.0 - SECOND_DECAY) * gradient * gradient
    first_fix = 1.0 - FIRST_DECAY**ADAM_STEP
    second_fix = 1.0 - SECOND_DECAY**ADAM_STEP
    direction = first_new / first_fix / (jnp.sqrt(second_new / second_fix) + ADAM_EPS)
    return (first_new, second_new, param - VECTOR_RATE * (direction + WEIGHT_DECAY * param))


def per_device(
    block_in,
    out_grad,
    lengths,
    feature_proj,
    attn_in,
    attn_out,
    ffn_in,
    ffn_out,
    norm_params,
    bias_in,
    bias_out,
    mom_attn_in,
    mom_attn_out,
    mom_ffn_in,
    mom_ffn_out,
    first_norms,
    first_bias_in,
    first_bias_out,
    second_norms,
    second_bias_in,
    second_bias_out,
):
    seq_count, length, model_width = block_in.shape
    row_total = seq_count * length
    positions = jnp.arange(length, dtype=jnp.int32)
    live_mask = (positions[None, :] < lengths[:, None]).astype(jnp.float32)
    cosine_table, sine_table = rotary_tables(length, HDIM)
    flat_in = block_in.reshape(row_total, model_width).astype(jnp.float32)
    low_qkv = attn_in.astype(jnp.bfloat16)
    low_out = attn_out.astype(jnp.bfloat16)
    low_in = ffn_in.astype(jnp.bfloat16)
    low_back_w = ffn_out.astype(jnp.bfloat16)
    low_norms = norm_params.astype(jnp.bfloat16)
    low_bias_in = bias_in.astype(jnp.bfloat16)
    low_bias_out = bias_out.astype(jnp.bfloat16)
    params = (
        lax.all_gather(low_qkv, "wide", axis=1, tiled=True),
        lax.all_gather(low_out, "wide", axis=0, tiled=True),
        lax.all_gather(low_in, "wide", axis=0, tiled=True),
        lax.all_gather(low_back_w, "wide", axis=0, tiled=True),
        lax.all_gather(low_norms, "wide", axis=1, tiled=True),
        lax.all_gather(low_bias_in, "wide", axis=0, tiled=True),
        lax.all_gather(low_bias_out, "wide", axis=0, tiled=True),
    )
    result, kept_values = forward(
        params, flat_in, live_mask, cosine_table, sine_table, feature_proj
    )
    params_back = (
        lax.all_gather(low_qkv, "wide", axis=1, tiled=True),
        lax.all_gather(low_out, "wide", axis=0, tiled=True),
        lax.all_gather(low_in, "wide", axis=0, tiled=True),
        lax.all_gather(low_back_w, "wide", axis=0, tiled=True),
        lax.all_gather(low_norms, "wide", axis=1, tiled=True),
        lax.all_gather(low_bias_in, "wide", axis=0, tiled=True),
        lax.all_gather(low_bias_out, "wide", axis=0, tiled=True),
    )
    unused_result, kept_values = forward(
        params_back, flat_in, live_mask, cosine_table, sine_table, feature_proj
    )
    grad_input, gradients = backward(
        params_back,
        kept_values,
        flat_in,
        out_grad.reshape(row_total, model_width),
        live_mask,
        cosine_table,
        sine_table,
        feature_proj,
    )
    narrow_size = lax.axis_size("narrow")
    wide_sums = (
        lax.psum_scatter(gradients[0], "wide", scatter_dimension=1, tiled=True),
        lax.psum_scatter(gradients[1], "wide", scatter_dimension=0, tiled=True),
        lax.psum_scatter(gradients[2], "wide", scatter_dimension=0, tiled=True),
        lax.psum_scatter(gradients[3], "wide", scatter_dimension=0, tiled=True),
        lax.psum_scatter(gradients[4], "wide", scatter_dimension=1, tiled=True),
        lax.psum_scatter(gradients[5], "wide", scatter_dimension=0, tiled=True),
        lax.psum_scatter(gradients[6], "wide", scatter_dimension=0, tiled=True),
    )
    owned = (
        lax.psum_scatter(wide_sums[0], "narrow", scatter_dimension=2, tiled=True),
        lax.psum_scatter(wide_sums[1], "narrow", scatter_dimension=1, tiled=True),
        lax.psum_scatter(wide_sums[2], "narrow", scatter_dimension=1, tiled=True),
        lax.psum_scatter(wide_sums[3], "narrow", scatter_dimension=1, tiled=True),
        lax.psum_scatter(wide_sums[4], "narrow", scatter_dimension=1, tiled=True),
        lax.psum_scatter(wide_sums[5], "narrow", scatter_dimension=0, tiled=True),
        lax.psum_scatter(wide_sums[6], "narrow", scatter_dimension=0, tiled=True),
    )
    (
        grad_qkv,
        grad_out_w,
        grad_in_w,
        grad_back_w,
        grad_norm_vals,
        grad_bias_inner,
        grad_bias_final,
    ) = owned
    column = lax.axis_index("narrow")

    def own_columns(weight):
        block_width = weight.shape[-1] // narrow_size
        return lax.dynamic_slice_in_dim(
            weight, column * block_width, block_width, axis=weight.ndim - 1
        )

    mom_qkv_new = MOMENT_DECAY * mom_attn_in + grad_qkv
    mom_out_new = MOMENT_DECAY * mom_attn_out + grad_out_w
    mom_in_new = MOMENT_DECAY * mom_ffn_in + grad_in_w
    mom_back_new = MOMENT_DECAY * mom_ffn_out + grad_back_w
    stacks = (mom_qkv_new, mom_out_new[None], mom_in_new[None], mom_back_new[None])
    squares = lax.psum(
        (
            jnp.sum(stacks[0] * stacks[0], axis=(1, 2)),
            jnp.sum(stacks[1] * stacks[1], axis=(1, 2)),
            jnp.sum(stacks[2] * stacks[2], axis=(1, 2)),
            jnp.sum(stacks[3] * stacks[3], axis=(1, 2)),
        ),
        "narrow",
    )
    iterates = tuple(
        (
            matrices / (jnp.sqrt(square_sum)[:, None, None] + ORTHO_EPS)
            for matrices, square_sum in zip(stacks, squares)
        )
    )
    gram_mats = lax.psum(
        (gram_of(iterates[0]), gram_of(iterates[1]), gram_of(iterates[2]), gram_of(iterates[3])),
        "narrow",
    )
    iterates = tuple(
        (ortho_step(iterate, gram_mat) for iterate, gram_mat in zip(iterates, gram_mats))
    )
    for sweep_index in range(NS_ITERS - 1):
        gram_mats = lax.psum(
            (
                gram_of(iterates[0]),
                gram_of(iterates[1]),
                gram_of(iterates[2]),
                gram_of(iterates[3]),
            ),
            "narrow",
        )
        iterates = tuple(
            (ortho_step(iterate, gram_mat) for iterate, gram_mat in zip(iterates, gram_mats))
        )
    rate_qkv = MUON_SCALE
    rate_out = MUON_SCALE * math.sqrt(D / (D // 64))
    rate_in = MUON_SCALE * math.sqrt(FF / D)
    rate_back = MUON_SCALE * math.sqrt(D / FF)
    new_qkv = own_columns(attn_in) * (1.0 - rate_qkv * WEIGHT_DECAY) - rate_qkv * iterates[0]
    new_out = own_columns(attn_out) * (1.0 - rate_out * WEIGHT_DECAY) - rate_out * iterates[1][0]
    new_in = own_columns(ffn_in) * (1.0 - rate_in * WEIGHT_DECAY) - rate_in * iterates[2][0]
    new_back = own_columns(ffn_out) * (1.0 - rate_back * WEIGHT_DECAY) - rate_back * iterates[3][0]
    norm_first, norm_second, norm_new = adam_update(
        own_columns(norm_params), first_norms, second_norms, grad_norm_vals
    )
    inner_first, inner_second, inner_new = adam_update(
        own_columns(bias_in), first_bias_in, second_bias_in, grad_bias_inner
    )
    final_first, final_second, final_new = adam_update(
        own_columns(bias_out), first_bias_out, second_bias_out, grad_bias_final
    )
    return (
        result.reshape(seq_count, length, model_width),
        grad_input.reshape(seq_count, length, model_width),
        grad_qkv,
        grad_out_w,
        grad_in_w,
        grad_back_w,
        grad_norm_vals,
        grad_bias_inner,
        grad_bias_final,
        mom_qkv_new,
        mom_out_new,
        mom_in_new,
        mom_back_new,
        new_qkv,
        new_out,
        new_in,
        new_back,
        norm_first,
        inner_first,
        final_first,
        norm_second[:2],
        norm_second[2:],
        inner_second,
        final_second,
        norm_new,
        inner_new,
        final_new,
    )


def solution(mesh):
    in_specs = (
        P(("wide", "narrow"), None, None),
        P(("wide", "narrow"), None, None),
        P(("wide", "narrow")),
        P(),
        P(None, "wide", None),
        P("wide", None),
        P("wide", None),
        P("wide", None),
        P(None, "wide"),
        P("wide"),
        P("wide"),
        P(None, "wide", "narrow"),
        P("wide", "narrow"),
        P("wide", "narrow"),
        P("wide", "narrow"),
        P(None, ("wide", "narrow")),
        P(("wide", "narrow")),
        P(("wide", "narrow")),
        P(None, ("wide", "narrow")),
        P(("wide", "narrow")),
        P(("wide", "narrow")),
    )
    out_specs = (
        P(("wide", "narrow"), None, None),
        P(("wide", "narrow"), None, None),
        P(None, "wide", "narrow"),
        P("wide", "narrow"),
        P("wide", "narrow"),
        P("wide", "narrow"),
        P(None, ("wide", "narrow")),
        P(("wide", "narrow")),
        P(("wide", "narrow")),
        P(None, "wide", "narrow"),
        P("wide", "narrow"),
        P("wide", "narrow"),
        P("wide", "narrow"),
        P(None, "wide", "narrow"),
        P("wide", "narrow"),
        P("wide", "narrow"),
        P("wide", "narrow"),
        P(None, ("wide", "narrow")),
        P(("wide", "narrow")),
        P(("wide", "narrow")),
        P(None, ("wide", "narrow")),
        P(None, ("wide", "narrow")),
        P(("wide", "narrow")),
        P(("wide", "narrow")),
        P(None, ("wide", "narrow")),
        P(("wide", "narrow")),
        P(("wide", "narrow")),
    )
    return jax.shard_map(
        per_device, mesh=mesh, in_specs=in_specs, out_specs=out_specs, check_vma=False
    )
```

profile of v0, /device:TPU:0, one launch (start us, length us, event | category | flops | bytes accessed | tf_op | source)
XLA Modules:
  0.0 1424.3 jit_solution(12844586551339965919)
XLA Ops:
  16.1 22.4 %all-gather = bf16[8,96,4]{1,2,0:T(4,128)(2,1)S(1)} all-gather(bf16[1,96,4]{1,2,0:T(4,128)(2,1)S(1)} %convert_bitcast_fusion), channel_id=1, replica_groups=mesh['wide'=8,'narrow'=4] {'wide'}, dimensions={0}, use_global_device_ids=true | all-gather | bytes 6912 | tf_op jit(solution)/shard_map/all_gather | solution.py:285
  38.6 26.4 %all-gather.1 = bf16[8,1,384]{2,1,0:T(2,128)(2,1)S(1)} all-gather(bf16[1,1,384]{2,1,0:T(2,128)(2,1)S(1)} %reshape.629), channel_id=1, replica_groups=mesh['wide'=8,'narrow'=4] {'wide'}, dimensions={0}, use_global_device_ids=true | all-gather | bytes 6912 | tf_op jit(solution)/shard_map/all_gather | solution.py:286
  66.5 12.6 all-gather.7.cloned.1.call-done
  79.0 5.1 convolution_bitcast_fusion
  94.8 5.5 reshape.663
  104.2 11.9 fusion.170
  125.8 12.0 fusion.169
  137.7 5.8 copy.302
  143.5 6.1 copy.301
  173.4 28.8 %all-gather.11.cloned.1.call-done = bf16[768,3072]{1,0:T(8,128)(2,1)} async-done(((bf16[96,3072]{1,0:T(8,128)(2,1)}), bf16[768,3072]{1,0:T(8,128)(2,1)}) %all-gather.11.cloned.1.call-update) | async-done | bytes 4718608 | tf_op jit(solution)/shard_map/all_gather | solution.py:283
  202.2 9.5 fusion.161
  211.6 70.6 %all-gather.13.cloned.1.call-done = bf16[3072,768]{1,0:T(8,128)(2,1)} async-done(((bf16[384,768]{1,0:T(8,128)(2,1)}), bf16[3072,768]{1,0:T(8,128)(2,1)}) %all-gather.13.cloned.1.call-update) | async-done | bytes 4718608 | tf_op jit(solution)/shard_map/all_gather | solution.py:284
  282.2 33.0 %convert_reduce_fusion = (f32[3072]{0:T(1024)}, bf16[832,3072]{1,0:T(8,128)(2,1)S(1)}, f32[832,3072]{1,0:T(8,128)}) fusion(f32[832,3072]{1,0:T(8,128)} %fusion.161, f32[3072]{0:T(1024)S(1)} %bitcast.492, bf16[832,768]{1,0:T(8,128)(2,1)} %bitcast.474, bf16[3072,768]{1,0:T(8,128)(2,1)} %all-gather.13.cloned.1.call-done), kind=kOutput, calls=%fused_computation.2 | convolution fusion | flops 4117558272 | bytes 31580160 | tf_op jit(solution)/shard_map/td,fd->tf/dot_general | solution.py:154
  326.8 10.7 fusion.160
  342.3 5.6 reshape.587
  362.2 31.8 %reduce-scatter.21.cloned.1.call-done = f32[96,768]{1,0:T(8,128)} async-done(((f32[768,768]{1,0:T(8,128)}), f32[96,768]{1,0:T(8,128)}) %reduce-scatter.21.cloned.1.call-update) | async-done | bytes 294928 | tf_op jit(solution)/shard_map/reduce_scatter | solution.py:317
  397.0 7.9 fusion.6
  404.9 155.2 %reduce-scatter.23.cloned.1.call-done = f32[96,3072]{1,0:T(8,128)} async-done(((f32[768,3072]{1,0:T(8,128)}), f32[96,3072]{1,0:T(8,128)}) %reduce-scatter.23.cloned.1.call-update) | async-done | bytes 1179664 | tf_op jit(solution)/shard_map/reduce_scatter | solution.py:318
  561.0 6.6 fusion.7
  571.9 5.2 copy.274
  577.1 5.4 reshape.642
  585.8 5.2 copy.276
  591.0 5.4 reshape.643
  600.1 5.2 copy.277
  605.3 5.4 reshape.644
  618.9 7.5 all-reduce.16
  630.0 9.3 convolution_bitcast_fusion.1
  639.3 11.0 copy.278
  650.3 8.3 copy.304
  658.6 11.7 multiply_convert_fusion
  676.7 9.7 fusion.177
  687.1 8.8 fusion.14
  696.9 95.1 %reduce-scatter.29.cloned.1.call-done = f32[96,2304]{1,0:T(8,128)} async-done(((f32[768,2304]{1,0:T(8,128)}), f32[96,2304]{1,0:T(8,128)}) %reduce-scatter.29.cloned.1.call-update) | async-done | bytes 884752
  804.8 19.5 %all-reduce.4 = bf16[768]{0:T(1024)(128)(2,1)S(1)} all-reduce(bf16[768]{0:T(1024)(128)(2,1)S(1)} %dynamic-update-slice), channel_id=1, replica_groups=mesh['wide'=8,'narrow'=4] {'wide'}, use_global_device_ids=true, to_apply=%add.4 | all-reduce | flops 768 | bytes 3072
  834.5 35.7 %all-reduce.10 = (f32[3072]{0:T(1024)S(1)}, f32[768]{0:T(1024)S(1)}) all-reduce(f32[3072]{0:T(1024)S(1)} %copy-done.71, f32[768]{0:T(1024)S(1)} %convert_reduce_fusion.1), channel_id=12, replica_groups=mesh['wide'=8,'narrow'=4] {'wide'}, use_global_device_ids=true, to_apply=%region_29.0.clone | all-reduce | flops 3840 | bytes 30720
  871.4 121.5 %reduce-scatter.27.cloned.1.call-done = f32[384,768]{1,0:T(8,128)} async-done(((f32[3072,768]{1,0:T(8,128)}), f32[384,768]{1,0:T(8,128)}) %reduce-scatter.27.cloned.1.call-update) | async-done | bytes 1179664 | tf_op jit(solution)/shard_map/reduce_scatter | solution.py:319
  995.8 9.5 add_add_fusion.4
  1005.3 51.4 %reduce-scatter.37.cloned.1.call-done = f32[96,4]{1,0:T(8,128)} async-done(((f32[768,4]{1,0:T(8,128)}), f32[96,4]{1,0:T(8,128)}) %reduce-scatter.37.cloned.1.call-update) | async-done | bytes 1552
  1057.6 26.4 %reduce-scatter.31.cloned.1.call-done = f32[192,288]{1,0:T(8,128)} async-done(((f32[768,288]{1,0:T(8,128)}), f32[192,288]{1,0:T(8,128)}) %reduce-scatter.31.cloned.1.call-update) | async-done | bytes 221200
  1086.6 32.3 %all-reduce.35.cloned.1.call-done = (f32[1,96,96]{2,1,0:T(8,128)}, f32[1,96,96]{2,1,0:T(8,128)}) async-done(((f32[1,96,96]{2,1,0:T(8,128)}, f32[1,96,96]{2,1,0:T(8,128)}), (f32[1,96,96]{2,1,0:T(8,128)}, f32[1,96,96]{2,1,0:T(8,128)})) %all-reduce.35.cloned.1.call-update) | async-done | bytes 73744 | tf_op jit(solution)/shard_map/psum | solution.py:378
  1123.7 23.9 %reduce-scatter.35.cloned.1.call-done = f32[192,384]{1,0:T(8,128)} async-done(((f32[768,384]{1,0:T(8,128)}), f32[192,384]{1,0:T(8,128)}) %reduce-scatter.35.cloned.1.call-update) | async-done | bytes 294928
  1149.3 33.2 %all-reduce.33.cloned.1.call-done = (f32[1,96,96]{2,1,0:T(8,128)}, f32[1,96,96]{2,1,0:T(8,128)}) async-done(((f32[1,96,96]{2,1,0:T(8,128)}, f32[1,96,96]{2,1,0:T(8,128)}), (f32[1,96,96]{2,1,0:T(8,128)}, f32[1,96,96]{2,1,0:T(8,128)})) %all-reduce.33.cloned.1.call-update) | async-done | bytes 73744 | tf_op jit(solution)/shard_map/psum | solution.py:378
  1186.0 12.3 all-reduce.50
  1205.2 31.5 %all-reduce.49.cloned.1.call-done = (f32[3,96,96]{2,1,0:T(8,128)}, f32[1,384,384]{2,1,0:T(8,128)}) async-done(((f32[3,96,96]{2,1,0:T(8,128)}, f32[1,384,384]{2,1,0:T(8,128)}), (f32[3,96,96]{2,1,0:T(8,128)}, f32[1,384,384]{2,1,0:T(8,128)})) %all-reduce.49.cloned.1.call-update) | async-done | bytes 700432 | tf_op jit(solution)/shard_map/psum | solution.py:370
  1251.3 29.7 %all-reduce.47.cloned.1.call-done = (f32[3,96,96]{2,1,0:T(8,128)}, f32[1,384,384]{2,1,0:T(8,128)}) async-done(((f32[3,96,96]{2,1,0:T(8,128)}, f32[1,384,384]{2,1,0:T(8,128)}), (f32[3,96,96]{2,1,0:T(8,128)}, f32[1,384,384]{2,1,0:T(8,128)})) %all-reduce.47.cloned.1.call-update) | async-done | bytes 700432 | tf_op jit(solution)/shard_map/psum | solution.py:378
  1290.7 33.1 %all-reduce.45.cloned.1.call-done = (f32[3,96,96]{2,1,0:T(8,128)}, f32[1,384,384]{2,1,0:T(8,128)}) async-done(((f32[3,96,96]{2,1,0:T(8,128)}, f32[1,384,384]{2,1,0:T(8,128)}), (f32[3,96,96]{2,1,0:T(8,128)}, f32[1,384,384]{2,1,0:T(8,128)})) %all-reduce.45.cloned.1.call-update) | async-done | bytes 700432 | tf_op jit(solution)/shard_map/psum | solution.py:378
  1335.3 31.2 %all-reduce.43.cloned.1.call-done = (f32[3,96,96]{2,1,0:T(8,128)}, f32[1,384,384]{2,1,0:T(8,128)}) async-done(((f32[3,96,96]{2,1,0:T(8,128)}, f32[1,384,384]{2,1,0:T(8,128)}), (f32[3,96,96]{2,1,0:T(8,128)}, f32[1,384,384]{2,1,0:T(8,128)})) %all-reduce.43.cloned.1.call-update) | async-done | bytes 700432 | tf_op jit(solution)/shard_map/psum | solution.py:378
  1376.9 32.3 %all-reduce.41.cloned.1.call-done = (f32[3,96,96]{2,1,0:T(8,128)}, f32[1,384,384]{2,1,0:T(8,128)}) async-done(((f32[3,96,96]{2,1,0:T(8,128)}, f32[1,384,384]{2,1,0:T(8,128)}), (f32[3,96,96]{2,1,0:T(8,128)}, f32[1,384,384]{2,1,0:T(8,128)})) %all-reduce.41.cloned.1.call-update) | async-done | bytes 700432 | tf_op jit(solution)/shard_map/psum | solution.py:378
  (408 shorter events, 218.5 us)
Async XLA Ops:
  7.2 148.4 %copy-start = (f32[12,32,64]{2,1,0:T(8,128)S(1)}, f32[12,32,64]{2,1,0:T(8,128)}, u32[]{:S(2)}) copy-start(f32[12,32,64]{2,1,0:T(8,128)} %param.24) | copy-start | bytes 294916
  7.2 71.8 %all-gather.7.cloned.1.call-start = ((), (), s32[]{:S(2)}) async-start(), calls=%async_computation.9 | async-start | bytes 3981312 | tf_op jit(solution)/shard_map/all_gather | solution.py:281
  9.4 160.1 %all-gather.9.cloned.1.call-start = ((), (), s32[]{:S(2)}) async-start(), calls=%async_computation.10 | async-start | bytes 1327104 | tf_op jit(solution)/shard_map/all_gather | solution.py:282
  11.2 191.0 %all-gather.11.cloned.1.call-start = ((), (), s32[]{:S(2)}) async-start(), calls=%async_computation.11 | async-start | bytes 5308416 | tf_op jit(solution)/shard_map/all_gather | solution.py:283
  13.5 51.6 %copy-start.90 = (s32[4]{0:T(128)S(1)}, s32[4]{0:T(128)}, u32[]{:S(2)}) copy-start(s32[4]{0:T(128)} %param.23) | copy-start | bytes 52
  13.5 268.8 %all-gather.13.cloned.1.call-start = ((), (), s32[]{:S(2)}) async-start(), calls=%async_computation.12 | async-start | bytes 5308416 | tf_op jit(solution)/shard_map/all_gather | solution.py:284
  14.5 379.6 %reduce-scatter.21.cloned.1.call-start = ((), (), s32[]{:S(2)}) async-start(), calls=%async_computation.13 | async-start | bytes 2654208 | tf_op jit(solution)/shard_map/reduce_scatter | solution.py:317
  14.9 69.3 %copy-start.63 = (f32[832]{0:T(1024)}, f32[832]{0:T(1024)S(1)}, u32[]{:S(2)}) copy-start(f32[832]{0:T(1024)S(1)} %div.139) | copy-start | bytes 9988
  16.1 68.1 %copy-start.65 = (f32[832]{0:T(1024)}, f32[832]{0:T(1024)S(1)}, u32[]{:S(2)}) copy-start(f32[832]{0:T(1024)S(1)} %rsqrt.24) | copy-start | bytes 9988
  38.6 45.6 %copy-start.61 = (f32[768]{0:T(1024)}, f32[768]{0:T(1024)S(1)}, u32[]{:S(2)}) copy-start(f32[768]{0:T(1024)S(1)} %get-tuple-element.171) | copy-start | bytes 9220
  38.6 163.5 %copy-start.54 = (f32[768]{0:T(1024)}, f32[768]{0:T(1024)S(1)}, u32[]{:S(2)}) copy-start(f32[768]{0:T(1024)S(1)} %get-tuple-element.169) | copy-start | bytes 9220
  65.9 83.8 %copy-start.42 = (f32[208,32]{0,1:T(8,128)}, f32[208,32]{0,1:T(8,128)S(1)}, u32[]{:S(2)}) copy-start(f32[208,32]{0,1:T(8,128)S(1)} %get-tuple-element.260) | copy-start | bytes 79876
  65.9 83.8 %copy-start.44 = (f32[208,32]{0,1:T(8,128)}, f32[208,32]{0,1:T(8,128)S(1)}, u32[]{:S(2)}) copy-start(f32[208,32]{0,1:T(8,128)S(1)} %get-tuple-element.261) | copy-start | bytes 79876
  66.4 12.6 copy-start.26
  173.4 38.2 %copy-start.67 = (f32[832]{0:T(1024)}, f32[832]{0:T(1024)S(1)}, u32[]{:S(2)}) copy-start(f32[832]{0:T(1024)S(1)} %multiply_reduce_fusion.6) | copy-start | bytes 9988
  282.2 33.1 %copy-start.91 = (bf16[768,3072]{1,0:T(8,128)(2,1)S(1)}, bf16[768,3072]{1,0:T(8,128)(2,1)}, u32[]{:S(2)}) copy-start(bf16[768,3072]{1,0:T(8,128)(2,1)} %all-gather.11.cloned.1.call-done) | copy-start | bytes 14155780
  326.8 233.3 %reduce-scatter.23.cloned.1.call-start = ((), (), s32[]{:S(2)}) async-start(), calls=%async_computation.14 | async-start | bytes 10616832 | tf_op jit(solution)/shard_map/reduce_scatter | solution.py:318
  337.6 278.0 %reduce-scatter.33.cloned.1.call-start = ((), (), s32[]{:S(2)}) async-start(), calls=%async_computation.19 | async-start | bytes 491520
  396.0 221.2 %reduce-scatter.25.cloned.1.call-start = ((), (), s32[]{:S(2)}) async-start(), calls=%async_computation.15 | async-start | bytes 1474560 | tf_op jit(solution)/shard_map/reduce_scatter | solution.py:327
  560.1 110.3 %all-reduce.39.cloned.1.call-start = ((), (), s32[]{:S(2)}) async-start(), calls=%async_computation.25 | async-start | bytes 196608 | tf_op jit(solution)/shard_map/psum | solution.py:370
  616.6 22.7 %copy-start.37 = (f32[96,192]{1,0:T(8,128)}, f32[96,192]{1,0:T(8,128)S(1)}, u32[]{:S(2)}) copy-start(f32[96,192]{1,0:T(8,128)S(1)} %copy.283) | copy-start | bytes 221188
  617.2 55.4 %copy-start.57 = (f32[96,192]{1,0:T(8,128)}, f32[96,192]{1,0:T(8,128)S(1)}, u32[]{:S(2)}) copy-start(f32[96,192]{1,0:T(8,128)S(1)} %get-tuple-element.218) | copy-start | bytes 221188
  618.9 20.4 %copy-start.48 = (f32[96,768]{1,0:T(8,128)}, f32[96,768]{1,0:T(8,128)S(1)}, u32[]{:S(2)}) copy-start(f32[96,768]{1,0:T(8,128)S(1)} %get-tuple-element.216) | copy-start | bytes 884740
  629.7 162.3 %reduce-scatter.29.cloned.1.call-start = ((), (), s32[]{:S(2)}) async-start(), calls=%async_computation.17 | async-start | bytes 7962624
  658.6 171.1 %all-reduce.37.cloned.1.call-start = ((), (), s32[]{:S(2)}) async-start(), calls=%async_computation.24 | async-start | bytes 196608 | tf_op jit(solution)/shard_map/psum | solution.py:378
  676.2 316.7 %reduce-scatter.27.cloned.1.call-start = ((), (), s32[]{:S(2)}) async-start(), calls=%async_computation.16 | async-start | bytes 10616832 | tf_op jit(solution)/shard_map/reduce_scatter | solution.py:319
  686.4 370.4 %reduce-scatter.37.cloned.1.call-start = ((), (), s32[]{:S(2)}) async-start(), calls=%async_computation.21 | async-start | bytes 442368
  696.9 387.1 %reduce-scatter.31.cloned.1.call-start = ((), (), s32[]{:S(2)}) async-start(), calls=%async_computation.18 | async-start | bytes 1474560
  797.0 6.9 copy-start.83
  800.0 34.5 %copy-start.70 = (f32[832]{0:T(1024)S(1)}, f32[832]{0:T(1024)}, u32[]{:S(2)}) copy-start(f32[832]{0:T(1024)} %copy-done.69) | copy-start | bytes 9988
  800.0 34.5 %copy-start.71 = (f32[3072]{0:T(1024)S(1)}, f32[3072]{0:T(1024)}, u32[]{:S(2)}) copy-start(f32[3072]{0:T(1024)} %get-tuple-element.221) | copy-start | bytes 36868
  800.0 318.8 %all-reduce.35.cloned.1.call-start = ((), (), s32[]{:S(2)}) async-start(), calls=%async_computation.23 | async-start | bytes 196608 | tf_op jit(solution)/shard_map/psum | solution.py:378
  834.4 313.2 %reduce-scatter.35.cloned.1.call-start = ((), (), s32[]{:S(2)}) async-start(), calls=%async_computation.20 | async-start | bytes 1474560
  995.6 186.9 %all-reduce.33.cloned.1.call-start = ((), (), s32[]{:S(2)}) async-start(), calls=%async_computation.22 | async-start | bytes 196608 | tf_op jit(solution)/shard_map/psum | solution.py:378
  1005.3 142.3 %copy-start.47 = (f32[384,192]{0,1:T(8,128)S(1)}, f32[384,192]{0,1:T(8,128)}, u32[]{:S(2)}) copy-start(f32[384,192]{0,1:T(8,128)} %param.35) | copy-start | bytes 884740
  1085.3 34.6 %copy-start.28 = (f32[3,96,192]{2,1,0:T(8,128)}, f32[3,96,192]{2,1,0:T(8,128)S(1)}, u32[]{:S(2)}) copy-start(f32[3,96,192]{2,1,0:T(8,128)S(1)} %copy.281) | copy-start | bytes 663556
  1086.6 113.7 %copy-start.49 = (f32[3,96,192]{2,1,0:T(8,128)}, f32[3,96,192]{2,1,0:T(8,128)S(1)}, u32[]{:S(2)}) copy-start(f32[3,96,192]{2,1,0:T(8,128)S(1)} %get-tuple-element.220) | copy-start | bytes 663556
  1086.6 99.4 %copy-start.74 = (f32[384]{0:T(512)S(1)}, f32[384]{0:T(512)}, u32[]{:S(2)}) copy-start(f32[384]{0:T(512)} %dynamic-slice.4) | copy-start | bytes 4612
  1086.6 99.5 %copy-start.82 = (f32[96]{0:T(128)S(1)}, f32[96]{0:T(128)}, u32[]{:S(2)}) copy-start(f32[96]{0:T(128)} %dynamic-slice.8) | copy-start | bytes 1156
  1123.6 113.1 %all-reduce.49.cloned.1.call-start = ((), (), s32[]{:S(2)}) async-start(), calls=%async_computation.30 | async-start | bytes 1474560 | tf_op jit(solution)/shard_map/psum | solution.py:370
  1149.3 53.0 %copy-start.50 = (f32[384,192]{0,1:T(8,128)}, f32[384,192]{0,1:T(8,128)S(1)}, u32[]{:S(2)}) copy-start(f32[384,192]{0,1:T(8,128)S(1)} %get-tuple-element.214) | copy-start | bytes 884740
  1202.0 79.0 %all-reduce.47.cloned.1.call-start = ((), (), s32[]{:S(2)}) async-start(), calls=%async_computation.29 | async-start | bytes 1474560 | tf_op jit(solution)/shard_map/psum | solution.py:378
  1205.0 34.7 %copy-start.7 = (f32[832,768]{1,0:T(8,128)}, f32[832,768]{1,0:T(8,128)S(1)}, u32[]{:S(2)}) copy-start(f32[832,768]{1,0:T(8,128)S(1)} %add_add_fusion) | copy-start | bytes 7667716
  1246.4 77.4 %all-reduce.45.cloned.1.call-start = ((), (), s32[]{:S(2)}) async-start(), calls=%async_computation.28 | async-start | bytes 1474560 | tf_op jit(solution)/shard_map/psum | solution.py:378
  1250.5 36.0 %copy-start.23 = (f32[384,192]{0,1:T(8,128)S(1)}, f32[384,192]{0,1:T(8,128)}, u32[]{:S(2)}) copy-start(f32[384,192]{0,1:T(8,128)} %copy-done.22) | copy-start | bytes 884740
  1289.1 77.4 %all-reduce.43.cloned.1.call-start = ((), (), s32[]{:S(2)}) async-start(), calls=%async_computation.27 | async-start | bytes 1474560 | tf_op jit(solution)/shard_map/psum | solution.py:378
  1331.9 77.3 %all-reduce.41.cloned.1.call-start = ((), (), s32[]{:S(2)}) async-start(), calls=%async_computation.26 | async-start | bytes 1474560 | tf_op jit(solution)/shard_map/psum | solution.py:378
  1372.9 42.6 %copy-start.29 = (f32[384,192]{0,1:T(8,128)S(1)}, f32[384,192]{0,1:T(8,128)}, u32[]{:S(2)}) copy-start(f32[384,192]{0,1:T(8,128)} %copy.303) | copy-start | bytes 884740
  (68 other events, 252.3 us)
Sparse Core Ops, SparseCore 0:
  10.8 68.1 all-gather.6
  81.8 39.4 all-gather.8
  123.5 78.6 all-gather.10
  204.2 78.0 all-gather.12
  326.9 67.1 reduce-scatter.20
  397.5 162.5 reduce-scatter.22
  562.6 19.8 reduce-scatter.32
  585.6 25.7 reduce-scatter.24
  629.9 29.6 all-reduce.38
  663.0 128.9 reduce-scatter.28
  795.7 30.4 all-reduce.36
  829.6 163.2 reduce-scatter.26
  996.2 60.5 reduce-scatter.36
  1059.2 24.7 reduce-scatter.30
  1087.4 31.4 all-reduce.34
  1121.9 25.7 reduce-scatter.34
  1151.0 31.4 all-reduce.32
  1202.1 34.5 all-reduce.48
  1246.5 34.4 all-reduce.46
  1289.3 34.4 all-reduce.44
  1332.0 34.4 all-reduce.42
  1374.8 34.4 all-reduce.40
where the time goes:
time: 1440 us; the launch traced here: 1420 us
  waiting for transfers between devices  841 us (58%)
  matrix products  217 us (15%)
  local copies, waits for them, and re-layouts  160 us (11%)
  blocking collectives  124 us (9%)
  other arithmetic  58 us (4%)
  between operations  21.6 us (2%)
    psum x9, waiting for transfers between devices, per_device(): lax.psum((gram_of(iterates[0]), gram_of(iterates[1]), gram_of(iterates[2]...  223 us
    unnamed x27, waiting for transfers between devices  197 us
    reduce_scatter x1, waiting for transfers between devices, per_device(): lax.psum_scatter(gradients[2], 'wide', scatter_dimension=0, tiled=True)  155 us
    reduce_scatter x1, waiting for transfers between devices, per_device(): lax.psum_scatter(gradients[3], 'wide', scatter_dimension=0, tiled=True)  122 us
    unnamed x214, local copies, waits for them, and re-layouts  74 us
    all_gather x1, waiting for transfers between devices, per_device(): lax.all_gather(low_back_w, 'wide', axis=0, tiled=True)  70.6 us
    unnamed x3, blocking collectives  67.4 us
    dot_general x1, matrix products, backward(): jnp.einsum('td,fd->tf', grad_final, w_back, preferred_element_type=jnp.fl...  33 us
  transfers between devices with their start and end apart: 22, of which 17 were waited for; matrix products, arithmetic and copies ran while one was open for 23% of the time, Pallas kernels for 0%

commit v1 on v0

--- a/solution.py
+++ b/solution.py
@@ -221,15 +221,91 @@
     )
 
 
+def xor_pairs(size, mask):
+    return [(index, index ^ mask) for index in range(size)]
+
+
+def swap(value, axis_name, mask):
+    return lax.ppermute(value, axis_name, xor_pairs(lax.axis_size(axis_name), mask))
+
+
+def gather_rows(piece):
+    wide_size = lax.axis_size("wide")
+    narrow_size = lax.axis_size("narrow")
+    block = jnp.stack([piece] + [swap(piece, "wide", 2 * m) for m in range(1, wide_size // 2)])
+    block = jnp.stack([block, swap(block, "wide", 1)])
+    block = jnp.stack([block] + [swap(block, "narrow", 2 * m) for m in range(1, narrow_size // 2)])
+    block = jnp.stack([block, swap(block, "narrow", 1)])
+    flat = block.reshape((wide_size * narrow_size,) + piece.shape)
+    my_wide = lax.axis_index("wide")
+    my_narrow = lax.axis_index("narrow")
+    ordered = []
+    for wide_index in range(wide_size):
+        for narrow_index in range(narrow_size):
+            wide_mask = wide_index ^ my_wide
+            narrow_mask = narrow_index ^ my_narrow
+            place = (narrow_mask & 1) * (narrow_size // 2) + (narrow_mask >> 1)
+            place = (place * 2 + (wide_mask & 1)) * (wide_size // 2) + (wide_mask >> 1)
+            ordered.append(lax.dynamic_index_in_dim(flat, place, 0, keepdims=False))
+    return jnp.concatenate(ordered, axis=0)
+
+
+def pick(value, index, axis):
+    return lax.dynamic_index_in_dim(value, index, axis, keepdims=False)
+
+
+def fold(value, axis_name, masks, shift):
+    place = lax.axis_index(axis_name)
+    here = pick(value, (place >> shift) & (value.shape[0] - 1), 0).astype(jnp.float32)
+    for mask in masks:
+        other = ((place ^ mask) >> shift) & (value.shape[0] - 1)
+        here = here + swap(pick(value, other, 0), axis_name, mask).astype(jnp.float32)
+    return here
+
+
+def scatter_blocks(parts, wire):
+    wide_size = lax.axis_size("wide")
+    narrow_size = lax.axis_size("narrow")
+    rest = parts.shape[2:]
+    value = parts.astype(wire).reshape((narrow_size // 2, 2, wide_size) + rest).swapaxes(0, 1)
+    value = fold(value, "narrow", [1], 0).astype(wire)
+    value = fold(value, "narrow", [2 * m for m in range(1, narrow_size // 2)], 1).astype(wire)
+    value = value.reshape((wide_size // 2, 2) + rest).swapaxes(0, 1)
+    value = fold(value, "wide", [1], 0).astype(wire)
+    return fold(value, "wide", [2 * m for m in range(1, wide_size // 2)], 1)
+
+
+def narrow_sum(value):
+    mask = 1
+    while mask < lax.axis_size("narrow"):
+        value = value + swap(value, "narrow", mask)
+        mask *= 2
+    return value
+
+
 def gram_of(matrices):
     return jnp.einsum("brc,bsc->brs", matrices, matrices, precision=PRECISE)
 
 
-def ortho_step(iterate, gram_mat):
-    poly_mat = CUBIC_COEF * gram_mat + QUINTIC_COEF * jnp.einsum(
-        "brs,bst->brt", gram_mat, gram_mat, precision=PRECISE
-    )
-    return LINEAR_COEF * iterate + jnp.einsum("brs,bsc->brc", poly_mat, iterate, precision=PRECISE)
+def bmm(left, right):
+    return jnp.einsum("brs,bst->brt", left, right, precision=PRECISE)
+
+
+def ortho_factor(gram_mat):
+    count = gram_mat.shape[-1]
+    identity = jnp.eye(count, dtype=jnp.float32)
+    square_sum = jnp.trace(gram_mat, axis1=-2, axis2=-1)
+    scale = (1.0 / (jnp.sqrt(square_sum) + ORTHO_EPS))[:, None, None]
+    gram_mat = gram_mat * scale * scale
+    factor = None
+    for sweep_index in range(NS_ITERS):
+        poly_mat = (
+            LINEAR_COEF * identity + CUBIC_COEF * gram_mat + QUINTIC_COEF * bmm(gram_mat, gram_mat)
+        )
+        factor = poly_mat if factor is None else bmm(poly_mat, factor)
+        if sweep_index < NS_ITERS - 1:
+            gram_mat = bmm(poly_mat, bmm(gram_mat, poly_mat))
+    return factor * scale
 
 
 def adam_update(param, earlier_first, earlier_second, gradient):
@@ -277,11 +353,20 @@
     low_norms = norm_params.astype(jnp.bfloat16)
     low_bias_in = bias_in.astype(jnp.bfloat16)
     low_bias_out = bias_out.astype(jnp.bfloat16)
+    narrow_size = lax.axis_size("narrow")
+    wide_size = lax.axis_size("wide")
+    column = lax.axis_index("narrow")
+
+    def quarter(rows):
+        part = rows.shape[0] // narrow_size
+        return lax.dynamic_slice_in_dim(rows, column * part, part, axis=0)
+
+    qkv_rows = low_qkv.transpose(1, 0, 2).reshape(-1, 3 * D)
     params = (
-        lax.all_gather(low_qkv, "wide", axis=1, tiled=True),
-        lax.all_gather(low_out, "wide", axis=0, tiled=True),
-        lax.all_gather(low_in, "wide", axis=0, tiled=True),
-        lax.all_gather(low_back_w, "wide", axis=0, tiled=True),
+        gather_rows(quarter(qkv_rows)).reshape(D, 3, D).transpose(1, 0, 2),
+        gather_rows(quarter(low_out)),
+        gather_rows(quarter(low_in)),
+        gather_rows(quarter(low_back_w)),
         lax.all_gather(low_norms, "wide", axis=1, tiled=True),
         lax.all_gather(low_bias_in, "wide", axis=0, tiled=True),
         lax.all_gather(low_bias_out, "wide", axis=0, tiled=True),
@@ -289,20 +374,8 @@
     result, kept_values = forward(
         params, flat_in, live_mask, cosine_table, sine_table, feature_proj
     )
-    params_back = (
-        lax.all_gather(low_qkv, "wide", axis=1, tiled=True),
-        lax.all_gather(low_out, "wide", axis=0, tiled=True),
-        lax.all_gather(low_in, "wide", axis=0, tiled=True),
-        lax.all_gather(low_back_w, "wide", axis=0, tiled=True),
-        lax.all_gather(low_norms, "wide", axis=1, tiled=True),
-        lax.all_gather(low_bias_in, "wide", axis=0, tiled=True),
-        lax.all_gather(low_bias_out, "wide", axis=0, tiled=True),
-    )
-    unused_result, kept_values = forward(
-        params_back, flat_in, live_mask, cosine_table, sine_table, feature_proj
-    )
     grad_input, gradients = backward(
-        params_back,
+        params,
         kept_values,
         flat_in,
         out_grad.reshape(row_total, model_width),
@@ -311,35 +384,27 @@
         sine_table,
         feature_proj,
     )
-    narrow_size = lax.axis_size("narrow")
-    wide_sums = (
-        lax.psum_scatter(gradients[0], "wide", scatter_dimension=1, tiled=True),
-        lax.psum_scatter(gradients[1], "wide", scatter_dimension=0, tiled=True),
-        lax.psum_scatter(gradients[2], "wide", scatter_dimension=0, tiled=True),
-        lax.psum_scatter(gradients[3], "wide", scatter_dimension=0, tiled=True),
-        lax.psum_scatter(gradients[4], "wide", scatter_dimension=1, tiled=True),
-        lax.psum_scatter(gradients[5], "wide", scatter_dimension=0, tiled=True),
-        lax.psum_scatter(gradients[6], "wide", scatter_dimension=0, tiled=True),
-    )
-    owned = (
-        lax.psum_scatter(wide_sums[0], "narrow", scatter_dimension=2, tiled=True),
-        lax.psum_scatter(wide_sums[1], "narrow", scatter_dimension=1, tiled=True),
-        lax.psum_scatter(wide_sums[2], "narrow", scatter_dimension=1, tiled=True),
-        lax.psum_scatter(wide_sums[3], "narrow", scatter_dimension=1, tiled=True),
-        lax.psum_scatter(wide_sums[4], "narrow", scatter_dimension=1, tiled=True),
-        lax.psum_scatter(wide_sums[5], "narrow", scatter_dimension=0, tiled=True),
-        lax.psum_scatter(wide_sums[6], "narrow", scatter_dimension=0, tiled=True),
-    )
-    (
-        grad_qkv,
-        grad_out_w,
-        grad_in_w,
-        grad_back_w,
-        grad_norm_vals,
-        grad_bias_inner,
-        grad_bias_final,
-    ) = owned
-    column = lax.axis_index("narrow")
+    def blocks_of(gradient):
+        rows, columns = gradient.shape
+        shape = (wide_size, rows // wide_size, narrow_size, columns // narrow_size)
+        return gradient.astype(jnp.bfloat16).reshape(shape).transpose(2, 0, 1, 3)
+
+    grad_back_w = scatter_blocks(blocks_of(gradients[3]), jnp.bfloat16)
+    grad_in_w = scatter_blocks(blocks_of(gradients[2]), jnp.bfloat16)
+    grad_out_w = scatter_blocks(blocks_of(gradients[1]), jnp.bfloat16)
+    grad_qkv = scatter_blocks(
+        jnp.stack([blocks_of(gradients[0][j]) for j in range(3)], axis=2), jnp.bfloat16
+    )
+    norm_sums, inner_sums, final_sums = lax.psum(gradients[4:], ("wide", "narrow"))
+    place = lax.axis_index("wide") * narrow_size + column
+
+    def own_part(vector):
+        width = vector.shape[-1] // (wide_size * narrow_size)
+        return lax.dynamic_slice_in_dim(vector, place * width, width, axis=vector.ndim - 1)
+
+    grad_norm_vals = own_part(norm_sums)
+    grad_bias_inner = own_part(inner_sums)
+    grad_bias_final = own_part(final_sums)
 
     def own_columns(weight):
         block_width = weight.shape[-1] // narrow_size
@@ -352,41 +417,16 @@
     mom_in_new = MOMENT_DECAY * mom_ffn_in + grad_in_w
     mom_back_new = MOMENT_DECAY * mom_ffn_out + grad_back_w
     stacks = (mom_qkv_new, mom_out_new[None], mom_in_new[None], mom_back_new[None])
-    squares = lax.psum(
-        (
-            jnp.sum(stacks[0] * stacks[0], axis=(1, 2)),
-            jnp.sum(stacks[1] * stacks[1], axis=(1, 2)),
-            jnp.sum(stacks[2] * stacks[2], axis=(1, 2)),
-            jnp.sum(stacks[3] * stacks[3], axis=(1, 2)),
-        ),
-        "narrow",
-    )
-    iterates = tuple(
-        (
-            matrices / (jnp.sqrt(square_sum)[:, None, None] + ORTHO_EPS)
-            for matrices, square_sum in zip(stacks, squares)
-        )
-    )
-    gram_mats = lax.psum(
-        (gram_of(iterates[0]), gram_of(iterates[1]), gram_of(iterates[2]), gram_of(iterates[3])),
-        "narrow",
-    )
-    iterates = tuple(
-        (ortho_step(iterate, gram_mat) for iterate, gram_mat in zip(iterates, gram_mats))
-    )
-    for sweep_index in range(NS_ITERS - 1):
-        gram_mats = lax.psum(
-            (
-                gram_of(iterates[0]),
-                gram_of(iterates[1]),
-                gram_of(iterates[2]),
-                gram_of(iterates[3]),
-            ),
-            "narrow",
-        )
-        iterates = tuple(
-            (ortho_step(iterate, gram_mat) for iterate, gram_mat in zip(iterates, gram_mats))
-        )
+    small = jnp.concatenate([gram_of(stacks[0]), gram_of(stacks[1]), gram_of(stacks[2])], axis=0)
+    large = gram_of(stacks[3])
+    small_factor = ortho_factor(narrow_sum(small))
+    large_factor = ortho_factor(narrow_sum(large))
+    iterates = (
+        bmm(small_factor[:3], stacks[0]),
+        bmm(small_factor[3:4], stacks[1]),
+        bmm(small_factor[4:5], stacks[2]),
+        bmm(large_factor, stacks[3]),
+    )
     rate_qkv = MUON_SCALE
     rate_out = MUON_SCALE * math.sqrt(D / (D // 64))
     rate_in = MUON_SCALE * math.sqrt(FF / D)

time: 1440 us -> 792 us (0.55)
  waiting for transfers between devices: 841 us -> 166 us
  local copies, waits for them, and re-layouts: 160 us -> 226 us
  matrix products: 217 us -> 158 us
  starting transfers between devices: 2.34 us -> 58.8 us
  blocking collectives: 124 us -> 102 us
  between operations: 21.6 us -> 5.57 us
    reduce_scatter x4 -> x0, waiting for transfers between devices: 309 us -> none  [the longest x1 155 us: per_device(): lax.psum_scatter(gradients[2], 'wide', scatter_dimension=0, tiled=True)]
    psum x9 -> x0, waiting for transfers between devices: 223 us -> none  [per_device(): lax.psum((gram_of(iterates[0]), gram_of(iterates[1]), gram_of(iterates[2]...]
    unnamed x27 -> x0, waiting for transfers between devices: 197 us -> none
    ppermute x0 -> x52, waiting for transfers between devices: none -> 166 us  [swap(): lax.ppermute(value, axis_name, xor_pairs(lax.axis_size(axis_name), mask))]
    all_gather x4 -> x0, waiting for transfers between devices: 112 us -> none  [the longest x1 70.6 us: per_device(): lax.all_gather(low_back_w, 'wide', axis=0, tiled=True)]
    ppermute x0 -> x52, starting transfers between devices: none -> 58.8 us  [swap(): lax.ppermute(value, axis_name, xor_pairs(lax.axis_size(axis_name), mask))]
    unnamed x3 -> x1, blocking collectives: 67.4 us -> 17.7 us
    psum x1, blocking collectives: 7.51 us -> 39.5 us  [per_device(): lax.psum(gradients[4:], ('wide', 'narrow'))]
  transfers between devices with their start and end apart: 22 -> 52, of which waited for: 17 -> 21; matrix products, arithmetic and copies ran while one was open for 23% -> 28% of each run, Pallas kernels for 0% -> 0%
where the time goes in v1:
time: 792 us; the launch traced here: 786 us
  local copies, waits for them, and re-layouts  226 us (29%)
  waiting for transfers between devices  166 us (21%)
  matrix products  158 us (20%)
  blocking collectives  102 us (13%)
  other arithmetic  71.3 us (9%)
  starting transfers between devices  58.8 us (7%)
    ppermute x52, waiting for transfers between devices, swap(): lax.ppermute(value, axis_name, xor_pairs(lax.axis_size(axis_name), mask))  166 us
    ppermute x52, starting transfers between devices, swap(): lax.ppermute(value, axis_name, xor_pairs(lax.axis_size(axis_name), mask))  58.8 us
    unnamed x376, local copies, waits for them, and re-layouts  52.5 us
    psum x1, blocking collectives, per_device(): lax.psum(gradients[4:], ('wide', 'narrow'))  39.5 us
    dot_general x38, matrix products, bmm(): return jnp.einsum('brs,bst->brt', left, right, precision=PRECISE)  36.4 us
    another operation x7, local copies, waits for them, and re-layouts, backward(): jnp.stack([grad_queries.reshape(row_total, D), grad_keys.reshape(row_tota...  30.7 us
    dot_general x1, matrix products, forward(): jnp.dot(hidden_two, w_in, preferred_element_type=jnp.float32)  29.7 us
    all_gather x1, blocking collectives, per_device(): lax.all_gather(low_bias_in, 'wide', axis=0, tiled=True)  26.7 us
  transfers between devices with their start and end apart: 52, of which 21 were waited for; matrix products, arithmetic and copies ran while one was open for 28% of the time, Pallas kernels for 0%

profile of v1, /device:TPU:0, one launch (start us, length us, event | category | flops | bytes accessed | tf_op | source)
XLA Modules:
  0.0 786.4 jit_solution(9232988488916835631)
XLA Ops:
  25.2 17.7 %all-gather = bf16[8,96,4]{1,2,0:T(4,128)(2,1)S(1)} all-gather(bf16[1,96,4]{1,2,0:T(4,128)(2,1)S(1)} %convert_bitcast_fusion.2), channel_id=1, replica_groups=mesh['wide'=8,'narrow'=4] {'wide'}, dimensions={0}, use_global_device_ids=true | all-gather | bytes 6912 | tf_op jit(solution)/shard_map/all_gather | solution.py:370
  48.4 17.7 %all-reduce.4 = bf16[768]{0:T(1024)(128)(2,1)S(1)} all-reduce(bf16[768]{0:T(1024)(128)(2,1)S(1)} %dynamic-update-slice), channel_id=1, replica_groups=mesh['wide'=8,'narrow'=4] {'wide'}, use_global_device_ids=true, to_apply=%add.4 | all-reduce | flops 768 | bytes 3072
  66.7 26.7 %all-gather.1 = bf16[8,1,384]{2,1,0:T(2,128)(2,1)S(1)} all-gather(bf16[1,1,384]{2,1,0:T(2,128)(2,1)S(1)} %reshape.683), channel_id=1, replica_groups=mesh['wide'=8,'narrow'=4] {'wide'}, dimensions={0}, use_global_device_ids=true | all-gather | bytes 6912 | tf_op jit(solution)/shard_map/all_gather | solution.py:371
  94.5 4.2 collective-permute-start.2
  114.7 4.2 collective-permute-done.10
  126.5 4.6 collective-permute-done.15
  133.3 8.4 %collective-permute-done.4 = bf16[2,4,24,2304]{3,2,1,0:T(8,128)(2,1)S(1)} collective-permute-done((bf16[2,4,24,2304]{3,2,1,0:T(8,128)(2,1)S(1)}, bf16[2,4,24,2304]{3,2,1,0:T(8,128)(2,1)S(1)}, u32[]{:S(2)}, u32[]{:S(2)}) %collective-permute-start.4) | collective-permute-done | bytes 884768 | tf_op jit(solution)/shard_map/ppermute | solution.py:229
  142.3 24.7 %collective-permute-done.22 = bf16[2,4,96,768]{3,2,1,0:T(8,128)(2,1)S(1)} collective-permute-done((bf16[2,4,96,768]{3,2,1,0:T(8,128)(2,1)S(1)}, bf16[2,4,96,768]{3,2,1,0:T(8,128)(2,1)S(1)}, u32[]{:S(2)}, u32[]{:S(2)}) %collective-permute-start.22) | collective-permute-done | bytes 1179680 | tf_op jit(solution)/shard_map/ppermute | solution.py:229
  169.5 22.4 %collective-permute-done.16 = bf16[2,4,24,3072]{3,2,1,0:T(8,128)(2,1)S(1)} collective-permute-done((bf16[2,4,24,3072]{3,2,1,0:T(8,128)(2,1)S(1)}, bf16[2,4,24,3072]{3,2,1,0:T(8,128)(2,1)S(1)}, u32[]{:S(2)}, u32[]{:S(2)}) %collective-permute-start.16) | collective-permute-done | bytes 1179680 | tf_op jit(solution)/shard_map/ppermute | solution.py:229
  226.4 5.7 reshape.700
  232.1 5.5 reshape.699
  237.6 11.9 %fusion.206 = (f32[4,208,12,32]{3,2,1,0:T(8,128)}, f32[4,208,12,32]{3,2,1,0:T(8,128)}) fusion(f32[4,208,12,64]{3,2,1,0:T(8,128)} %reshape.699), kind=kLoop, calls=%fused_computation.593 | loop fusion | bytes 5111808 | tf_op jit(solution)/shard_map/slice | solution.py:50
  249.5 5.8 copy.368
  255.3 5.8 copy.367
  261.1 11.8 %fusion.205 = (f32[4,208,12,32]{3,2,1,0:T(8,128)}, f32[4,208,12,32]{3,2,1,0:T(8,128)}) fusion(f32[4,208,12,64]{3,2,1,0:T(8,128)} %reshape.700), kind=kLoop, calls=%fused_computation.592 | loop fusion | bytes 5111808 | tf_op jit(solution)/shard_map/slice | solution.py:50
  272.9 5.8 copy.370
  278.7 6.0 copy.369
  300.2 5.0 convert_element_type.353
  305.2 4.9 convert_reduce_fusion.2
  315.9 4.6 convert_element_type.358
  332.9 29.7 %multiply_convert_fusion = (bf16[832,3072]{1,0:T(8,128)(2,1)}, f32[832,3072]{1,0:T(8,128)}, f32[832,3072]{1,0:T(8,128)}) fusion(f32[3072]{0:T(1024)S(1)} %bitcast.910, bf16[768,3072]{1,0:T(8,128)(2,1)S(1)} %constant_dynamic-update-slice_fusion.64, f32[832,768]{1,0:T(8,128)S(1)} %get-tuple-element.179, f32[768]{0:T(1024)S(1)} %copy-done.90, ...), kind=kOutput, calls=%fused_computation.12 | convolution fusion | flops 4097753088 | bytes 32858624 | tf_op jit(solution)/shard_map/dot_general | solution.py:102
  362.7 13.3 %convert_reduce_fusion = (f32[3072]{0:T(1024)S(1)}, bf16[832,3072]{1,0:T(8,128)(2,1)}) fusion(f32[832,3072]{1,0:T(8,128)} %get-tuple-element.67, bf16[3072,768]{1,0:T(8,128)(2,1)S(1)} %constant_dynamic-update-slice_fusion.96, bf16[832,768]{1,0:T(8,128)(2,1)S(1)} %bitcast.835, f32[832,3072]{1,0:T(8,128)} %get-tuple-element.180, f32[3072]{0:T(1024)} %bitcast.911), kind=kOutput, calls=%fused_computation.11 | convolution fusion | flops 3969315840 | bytes 31580160 | tf_op jit(solution)/shard_map/td,fd->tf/dot_general | solution.py:154
  376.0 7.9 %multiply_reduce_fusion.3 = (f32[768]{0:T(1024)S(1)}, f32[832]{0:T(1024)S(1)}, f32[768]{0:T(1024)}, f32[832,768]{1,0:T(8,128)S(1)}) fusion(f32[832,768]{1,0:T(8,128)S(1)} %get-tuple-element.179, f32[832]{0:T(1024)S(1)} %fusion.167, f32[832]{0:T(1024)S(1)} %broadcast_multiply_fusion.2, f32[768]{0:T(1024)S(1)} %get-tuple-element.33, ...), kind=kOutput, calls=%fused_computation.71 | convolution fusion | flops 3930978048 | bytes 14961408 | tf_op jit(solution)/shard_map/tf,df->td/dot_general | solution.py:159
  383.9 7.7 convolution_convert_fusion.1
  400.3 5.7 reshape.641
  429.3 5.3 copy.356
  434.5 5.3 reshape.696
  443.2 5.3 copy.358
  448.4 5.4 reshape.697
  457.8 5.4 reshape.698
  467.0 5.1 fusion.31
  472.1 5.6 convert_bitcast_fusion
  477.7 6.9 convolution_convert_fusion
  484.7 5.6 add_add_fusion.4
  490.3 6.7 copy.341
  503.6 9.7 %reshape.647 = bf16[8,96,4,768]{3,2,1,0:T(4,128)(2,1)} reshape(bf16[768,3072]{1,0:T(8,128)(2,1)} %convolution_convert_fusion.1) | data formatting | bytes 9437184 | tf_op jit(solution)/shard_map/reshape | solution.py:390
  513.3 5.5 copy.340
  561.4 39.5 %all-reduce.5 = (f32[4,768]{1,0:T(4,128)S(1)}, f32[3072]{0:T(1024)S(1)}, f32[768]{0:T(1024)S(1)}) all-reduce(f32[4,768]{1,0:T(4,128)S(1)} %pad_maximum_fusion.22, f32[3072]{0:T(1024)S(1)} %get-tuple-element.187, f32[768]{0:T(1024)S(1)} %copy-done.84), channel_id=1, replica_groups=mesh['wide'=8,'narrow'=4] {'wide','narrow'}, use_global_device_ids=true, to_apply=%region_18.19 | all-reduce | flops 6912 | bytes 55296 | tf_op jit(solution)/shard_map/psum | solution.py:398
  601.0 4.6 add_add_fusion.2
  611.3 7.3 collective-permute-done.31
  638.2 18.1 %collective-permute-done.25 = bf16[8,3,96,192]{3,2,0,1:T(8,128)(2,1)S(1)} collective-permute-done((bf16[8,3,96,192]{3,2,0,1:T(8,128)(2,1)S(1)}, bf16[8,3,96,192]{3,2,0,1:T(8,128)(2,1)S(1)}, u32[]{:S(2)}, u32[]{:S(2)}) %collective-permute-start.25) | collective-permute-done | bytes 884768 | tf_op jit(solution)/shard_map/ppermute | solution.py:229
  660.3 6.5 collective-permute-done.26
  670.6 11.0 %collective-permute-done.37 = bf16[8,96,768]{2,1,0:T(8,128)(2,1)S(1)} collective-permute-done((bf16[8,96,768]{2,1,0:T(8,128)(2,1)S(1)}, bf16[8,96,768]{2,1,0:T(8,128)(2,1)S(1)}, u32[]{:S(2)}, u32[]{:S(2)}) %collective-permute-start.37) | collective-permute-done | bytes 1179680 | tf_op jit(solution)/shard_map/ppermute | solution.py:229
  684.5 18.7 %collective-permute-done.43 = bf16[8,384,192]{1,2,0:T(8,128)(2,1)S(1)} collective-permute-done((bf16[8,384,192]{1,2,0:T(8,128)(2,1)S(1)}, bf16[8,384,192]{1,2,0:T(8,128)(2,1)S(1)}, u32[]{:S(2)}, u32[]{:S(2)}) %collective-permute-start.43) | collective-permute-done | bytes 1179680 | tf_op jit(solution)/shard_map/ppermute | solution.py:229
  709.2 4.1 collective-permute-done.39
  713.3 4.3 collective-permute-done.40
  729.1 7.1 collective-permute-done.46
  751.6 9.3 %collective-permute-done.51 = f32[1,384,384]{2,1,0:T(8,128)S(1)} collective-permute-done((f32[1,384,384]{2,1,0:T(8,128)S(1)}, f32[1,384,384]{2,1,0:T(8,128)S(1)}, u32[]{:S(2)}, u32[]{:S(2)}) %collective-permute-start.51) | collective-permute-done | bytes 589856 | tf_op jit(solution)/shard_map/ppermute | solution.py:229
  (702 shorter events, 310.9 us)
Async XLA Ops:
  2.4 91.9 %collective-permute-start.6 = (bf16[24,768]{1,0:T(8,128)(2,1)}, bf16[24,768]{1,0:T(8,128)(2,1)}, u32[]{:S(2)}, u32[]{:S(2)}) collective-permute-start(bf16[24,768]{1,0:T(8,128)(2,1)} %dynamic-slice_convert_fusion.2), channel_id=1, source_target_pairs={{0,8},{4,12},{8,0},{12,4},{16,24},{20,28},{24,16},{28,20},{1,9},{5... | collective-permute-start | bytes 110600 | tf_op jit(solution)/shard_map/ppermute | solution.py:229
  5.4 88.9 %collective-permute-start.7 = (bf16[24,768]{1,0:T(8,128)(2,1)}, bf16[24,768]{1,0:T(8,128)(2,1)}, u32[]{:S(2)}, u32[]{:S(2)}) collective-permute-start(bf16[24,768]{1,0:T(8,128)(2,1)} %dynamic-slice_convert_fusion.2), channel_id=1, source_target_pairs={{0,16},{4,20},{8,24},{12,28},{16,0},{20,4},{24,8},{28,12},{1,17},{... | collective-permute-start | bytes 110600 | tf_op jit(solution)/shard_map/ppermute | solution.py:229
  8.0 86.5 %collective-permute-start.8 = (bf16[24,768]{1,0:T(8,128)(2,1)}, bf16[24,768]{1,0:T(8,128)(2,1)}, u32[]{:S(2)}, u32[]{:S(2)}) collective-permute-start(bf16[24,768]{1,0:T(8,128)(2,1)} %dynamic-slice_convert_fusion.2), channel_id=1, source_target_pairs={{0,24},{4,28},{8,16},{12,20},{16,8},{20,12},{24,0},{28,4},{1,25},{... | collective-permute-start | bytes 110600 | tf_op jit(solution)/shard_map/ppermute | solution.py:229
  8.7 95.8 %collective-permute-start.18 = (bf16[96,768]{1,0:T(8,128)(2,1)}, bf16[96,768]{1,0:T(8,128)(2,1)}, u32[]{:S(2)}, u32[]{:S(2)}) collective-permute-start(bf16[96,768]{1,0:T(8,128)(2,1)} %dynamic-slice_convert_fusion), channel_id=1, source_target_pairs={{0,8},{4,12},{8,0},{12,4},{16,24},{20,28},{24,16},{28,20},{1,9},{5... | collective-permute-start | bytes 442376 | tf_op jit(solution)/shard_map/ppermute | solution.py:229
  9.6 97.4 %collective-permute-start.19 = (bf16[96,768]{1,0:T(8,128)(2,1)}, bf16[96,768]{1,0:T(8,128)(2,1)}, u32[]{:S(2)}, u32[]{:S(2)}) collective-permute-start(bf16[96,768]{1,0:T(8,128)(2,1)} %dynamic-slice_convert_fusion), channel_id=1, source_target_pairs={{0,16},{4,20},{8,24},{12,28},{16,0},{20,4},{24,8},{28,12},{1,17},{... | collective-permute-start | bytes 442376 | tf_op jit(solution)/shard_map/ppermute | solution.py:229
  94.3 7.9 collective-permute-start
  94.5 8.4 %collective-permute-start.2 = (bf16[24,2304]{1,0:T(8,128)(2,1)}, bf16[24,2304]{1,0:T(8,128)(2,1)S(1)}, u32[]{:S(2)}, u32[]{:S(2)}) collective-permute-start(bf16[24,2304]{1,0:T(8,128)(2,1)} %constant_dynamic-slice_fusion.67), channel_id=1, source_target_pairs={{0,24},{4,28},{8,16},{12,20},{16,8},{20,12},{24,0},{28,4},{1,25},{... | collective-permute-start | bytes 331784 | tf_op jit(solution)/shard_map/ppermute | solution.py:229
  100.9 8.0 %collective-permute-start.20 = (bf16[96,768]{1,0:T(8,128)(2,1)}, bf16[96,768]{1,0:T(8,128)(2,1)S(1)}, u32[]{:S(2)}, u32[]{:S(2)}) collective-permute-start(bf16[96,768]{1,0:T(8,128)(2,1)} %dynamic-slice_convert_fusion), channel_id=1, source_target_pairs={{0,24},{4,28},{8,16},{12,20},{16,8},{20,12},{24,0},{28,4},{1,25},{... | collective-permute-start | bytes 442376 | tf_op jit(solution)/shard_map/ppermute | solution.py:229
  102.2 10.0 %collective-permute-start.12 = (bf16[24,3072]{1,0:T(8,128)(2,1)}, bf16[24,3072]{1,0:T(8,128)(2,1)S(1)}, u32[]{:S(2)}, u32[]{:S(2)}) collective-permute-start(bf16[24,3072]{1,0:T(8,128)(2,1)} %dynamic-slice_convert_fusion.1), channel_id=1, source_target_pairs={{0,8},{4,12},{8,0},{12,4},{16,24},{20,28},{24,16},{28,20},{1,9},{5... | collective-permute-start | bytes 442376 | tf_op jit(solution)/shard_map/ppermute | solution.py:229
  102.9 7.9 collective-permute-start.9
  104.5 9.2 %collective-permute-start.13 = (bf16[24,3072]{1,0:T(8,128)(2,1)S(1)}, bf16[24,3072]{1,0:T(8,128)(2,1)S(1)}, u32[]{:S(2)}, u32[]{:S(2)}) collective-permute-start(bf16[24,3072]{1,0:T(8,128)(2,1)S(1)} %copy-done.72), channel_id=1, source_target_pairs={{0,16},{4,20},{8,24},{12,28},{16,0},{20,4},{24,8},{28,12},{1,17},{... | collective-permute-start | bytes 442376 | tf_op jit(solution)/shard_map/ppermute | solution.py:229
  107.0 7.0 collective-permute-start.14
  108.9 10.2 %collective-permute-start.3 = (bf16[4,24,2304]{2,1,0:T(8,128)(2,1)S(1)}, bf16[4,24,2304]{2,1,0:T(8,128)(2,1)S(1)}, u32[]{:S(2)}, u32[]{:S(2)}) collective-permute-start(bf16[4,24,2304]{2,1,0:T(8,128)(2,1)S(1)} %get-tuple-element.149), channel_id=1, source_target_pairs={{0,4},{4,0},{8,12},{12,8},{16,20},{20,16},{24,28},{28,24},{1,5},{5... | collective-permute-start | bytes 1327112 | tf_op jit(solution)/shard_map/ppermute | solution.py:229
  110.8 14.0 %collective-permute-start.21 = (bf16[4,96,768]{2,1,0:T(8,128)(2,1)S(1)}, bf16[4,96,768]{2,1,0:T(8,128)(2,1)S(1)}, u32[]{:S(2)}, u32[]{:S(2)}) collective-permute-start(bf16[4,96,768]{2,1,0:T(8,128)(2,1)S(1)} %get-tuple-element.143), channel_id=1, source_target_pairs={{0,4},{4,0},{8,12},{12,8},{16,20},{20,16},{24,28},{28,24},{1,5},{5... | collective-permute-start | bytes 1769480 | tf_op jit(solution)/shard_map/ppermute | solution.py:229
  112.1 6.8 collective-permute-start.10
  114.1 16.9 %collective-permute-start.15 = (bf16[4,24,3072]{2,1,0:T(8,128)(2,1)S(1)}, bf16[4,24,3072]{2,1,0:T(8,128)(2,1)S(1)}, u32[]{:S(2)}, u32[]{:S(2)}) collective-permute-start(bf16[4,24,3072]{2,1,0:T(8,128)(2,1)S(1)} %get-tuple-element.145), channel_id=1, source_target_pairs={{0,4},{4,0},{8,12},{12,8},{16,20},{20,16},{24,28},{28,24},{1,5},{5... | collective-permute-start | bytes 1769480 | tf_op jit(solution)/shard_map/ppermute | solution.py:229
  119.0 13.8 %collective-permute-start.11 = (bf16[2,2,4,24,768]{4,3,2,1,0:T(8,128)(2,1)S(1)}, bf16[2,2,4,24,768]{4,3,2,1,0:T(8,128)(2,1)S(1)}, u32[]{:S(2)}, u32[]{:S(2)}) collective-permute-start(bf16[2,2,4,24,768]{4,3,2,1,0:T(8,128)(2,1)S(1)} %get-tuple-element.147), channel_id=1, source_target_pairs={{0,1},{1,0},{2,3},{3,2},{4,5},{5,4},{6,7},{7,6},{8,9},{9,8},{10,11... | collective-permute-start | bytes 1769480 | tf_op jit(solution)/shard_map/ppermute | solution.py:229
  119.2 22.5 %collective-permute-start.4 = (bf16[2,4,24,2304]{3,2,1,0:T(8,128)(2,1)S(1)}, bf16[2,4,24,2304]{3,2,1,0:T(8,128)(2,1)S(1)}, u32[]{:S(2)}, u32[]{:S(2)}) collective-permute-start(bf16[2,4,24,2304]{3,2,1,0:T(8,128)(2,1)S(1)} %get-tuple-element.132), channel_id=1, source_target_pairs={{0,2},{1,3},{2,0},{3,1},{4,6},{5,7},{6,4},{7,5},{8,10},{9,11},{10,... | collective-permute-start | bytes 2654216 | tf_op jit(solution)/shard_map/ppermute | solution.py:229
  124.9 42.1 %collective-permute-start.22 = (bf16[2,4,96,768]{3,2,1,0:T(8,128)(2,1)S(1)}, bf16[2,4,96,768]{3,2,1,0:T(8,128)(2,1)S(1)}, u32[]{:S(2)}, u32[]{:S(2)}) collective-permute-start(bf16[2,4,96,768]{3,2,1,0:T(8,128)(2,1)S(1)} %get-tuple-element.128), channel_id=1, source_target_pairs={{0,2},{1,3},{2,0},{3,1},{4,6},{5,7},{6,4},{7,5},{8,10},{9,11},{10,... | collective-permute-start | bytes 3538952 | tf_op jit(solution)/shard_map/ppermute | solution.py:229
  131.2 60.7 %collective-permute-start.16 = (bf16[2,4,24,3072]{3,2,1,0:T(8,128)(2,1)S(1)}, bf16[2,4,24,3072]{3,2,1,0:T(8,128)(2,1)S(1)}, u32[]{:S(2)}, u32[]{:S(2)}) collective-permute-start(bf16[2,4,24,3072]{3,2,1,0:T(8,128)(2,1)S(1)} %get-tuple-element.130), channel_id=1, source_target_pairs={{0,2},{1,3},{2,0},{3,1},{4,6},{5,7},{6,4},{7,5},{8,10},{9,11},{10,... | collective-permute-start | bytes 3538952 | tf_op jit(solution)/shard_map/ppermute | solution.py:229
  142.0 52.3 %collective-permute-start.5 = (bf16[2,2,4,24,2304]{4,3,2,1,0:T(8,128)(2,1)S(1)}, bf16[2,2,4,24,2304]{4,3,2,1,0:T(8,128)(2,1)S(1)}, u32[]{:S(2)}, u32[]{:S(2)}) collective-permute-start(bf16[2,2,4,24,2304]{4,3,2,1,0:T(8,128)(2,1)S(1)} %get-tuple-element.126), channel_id=1, source_target_pairs={{0,1},{1,0},{2,3},{3,2},{4,5},{5,4},{6,7},{7,6},{8,9},{9,8},{10,11... | collective-permute-start | bytes 5308424 | tf_op jit(solution)/shard_map/ppermute | solution.py:229
  169.5 159.3 %collective-permute-start.23 = (bf16[2,2,4,96,768]{4,3,2,1,0:T(8,128)(2,1)}, bf16[2,2,4,96,768]{4,3,2,1,0:T(8,128)(2,1)}, u32[]{:S(2)}, u32[]{:S(2)}) collective-permute-start(bf16[2,2,4,96,768]{4,3,2,1,0:T(8,128)(2,1)} %get-tuple-element.122), channel_id=1, source_target_pairs={{0,1},{1,0},{2,3},{3,2},{4,5},{5,4},{6,7},{7,6},{8,9},{9,8},{10,11... | collective-permute-start | bytes 7077896 | tf_op jit(solution)/shard_map/ppermute | solution.py:229
  194.3 129.4 %collective-permute-start.17 = (bf16[2,2,4,24,3072]{4,3,2,1,0:T(8,128)(2,1)}, bf16[2,2,4,24,3072]{4,3,2,1,0:T(8,128)(2,1)}, u32[]{:S(2)}, u32[]{:S(2)}) collective-permute-start(bf16[2,2,4,24,3072]{4,3,2,1,0:T(8,128)(2,1)} %get-tuple-element.124), channel_id=1, source_target_pairs={{0,1},{1,0},{2,3},{3,2},{4,5},{5,4},{6,7},{7,6},{8,9},{9,8},{10,11... | collective-permute-start | bytes 7077896 | tf_op jit(solution)/shard_map/ppermute | solution.py:229
  525.3 81.0 %collective-permute-start.30 = (bf16[2,8,96,192]{3,2,1,0:T(8,128)(2,1)}, bf16[2,8,96,192]{3,2,1,0:T(8,128)(2,1)}, u32[]{:S(2)}, u32[]{:S(2)}) collective-permute-start(bf16[2,8,96,192]{3,2,1,0:T(8,128)(2,1)} %dynamic-slice_bitcast_fusion.6), channel_id=1, source_target_pairs={{0,1},{1,0},{2,3},{3,2},{4,5},{5,4},{6,7},{7,6},{8,9},{9,8},{10,11... | collective-permute-start | bytes 1769480 | tf_op jit(solution)/shard_map/ppermute | solution.py:229
  531.0 104.5 %collective-permute-start.42 = (bf16[2,8,384,192]{2,3,1,0:T(8,128)(2,1)}, bf16[2,8,384,192]{2,3,1,0:T(8,128)(2,1)}, u32[]{:S(2)}, u32[]{:S(2)}) collective-permute-start(bf16[2,8,384,192]{2,3,1,0:T(8,128)(2,1)} %dynamic-slice_bitcast_fusion), channel_id=1, source_target_pairs={{0,1},{1,0},{2,3},{3,2},{4,5},{5,4},{6,7},{7,6},{8,9},{9,8},{10,11... | collective-permute-start | bytes 7077896 | tf_op jit(solution)/shard_map/ppermute | solution.py:229
  531.0 101.2 %collective-permute-start.36 = (bf16[2,8,96,768]{3,2,1,0:T(8,128)(2,1)}, bf16[2,8,96,768]{3,2,1,0:T(8,128)(2,1)}, u32[]{:S(2)}, u32[]{:S(2)}) collective-permute-start(bf16[2,8,96,768]{3,2,1,0:T(8,128)(2,1)} %dynamic-slice_bitcast_fusion.1), channel_id=1, source_target_pairs={{0,1},{1,0},{2,3},{3,2},{4,5},{5,4},{6,7},{7,6},{8,9},{9,8},{10,11... | collective-permute-start | bytes 7077896 | tf_op jit(solution)/shard_map/ppermute | solution.py:229
  561.3 63.2 %collective-permute-start.24 = (bf16[2,8,3,96,192]{4,3,1,0,2:T(8,128)(2,1)}, bf16[2,8,3,96,192]{4,3,1,0,2:T(8,128)(2,1)}, u32[]{:S(2)}, u32[]{:S(2)}) collective-permute-start(bf16[2,8,3,96,192]{4,3,1,0,2:T(8,128)(2,1)} %dynamic-slice_bitcast_fusion.2), channel_id=1, source_target_pairs={{0,1},{1,0},{2,3},{3,2},{4,5},{5,4},{6,7},{7,6},{8,9},{9,8},{10,11... | collective-permute-start | bytes 5308424 | tf_op jit(solution)/shard_map/ppermute | solution.py:229
  607.8 10.8 %collective-permute-start.31 = (bf16[8,96,192]{2,1,0:T(8,128)(2,1)S(1)}, bf16[8,96,192]{2,1,0:T(8,128)(2,1)S(1)}, u32[]{:S(2)}, u32[]{:S(2)}) collective-permute-start(bf16[8,96,192]{2,1,0:T(8,128)(2,1)S(1)} %dynamic-slice_bitcast_fusion.10), channel_id=1, source_target_pairs={{0,2},{1,3},{2,0},{3,1},{4,6},{5,7},{6,4},{7,5},{8,10},{9,11},{10,... | collective-permute-start | bytes 884744 | tf_op jit(solution)/shard_map/ppermute | solution.py:229
  627.4 29.0 %collective-permute-start.25 = (bf16[8,3,96,192]{3,2,0,1:T(8,128)(2,1)S(1)}, bf16[8,3,96,192]{3,2,0,1:T(8,128)(2,1)S(1)}, u32[]{:S(2)}, u32[]{:S(2)}) collective-permute-start(bf16[8,3,96,192]{3,2,0,1:T(8,128)(2,1)S(1)} %dynamic-slice_bitcast_fusion.5), channel_id=1, source_target_pairs={{0,2},{1,3},{2,0},{3,1},{4,6},{5,7},{6,4},{7,5},{8,10},{9,11},{10,... | collective-permute-start | bytes 2654216 | tf_op jit(solution)/shard_map/ppermute | solution.py:229
  629.2 29.6 %collective-permute-start.33 = (bf16[96,192]{1,0:T(8,128)(2,1)S(1)}, bf16[96,192]{1,0:T(8,128)(2,1)S(1)}, u32[]{:S(2)}, u32[]{:S(2)}) collective-permute-start(bf16[96,192]{1,0:T(8,128)(2,1)S(1)} %get-tuple-element.152), channel_id=1, source_target_pairs={{0,8},{4,12},{8,0},{12,4},{16,24},{20,28},{24,16},{28,20},{1,9},{5... | collective-permute-start | bytes 110600 | tf_op jit(solution)/shard_map/ppermute | solution.py:229
  630.3 29.1 %collective-permute-start.35 = (bf16[96,192]{1,0:T(8,128)(2,1)S(1)}, bf16[96,192]{1,0:T(8,128)(2,1)S(1)}, u32[]{:S(2)}, u32[]{:S(2)}) collective-permute-start(bf16[96,192]{1,0:T(8,128)(2,1)S(1)} %get-tuple-element.153), channel_id=1, source_target_pairs={{0,24},{4,28},{8,16},{12,20},{16,8},{20,12},{24,0},{28,4},{1,25},{... | collective-permute-start | bytes 110600 | tf_op jit(solution)/shard_map/ppermute | solution.py:229
  632.2 27.2 %collective-permute-start.34 = (bf16[96,192]{1,0:T(8,128)(2,1)S(1)}, bf16[96,192]{1,0:T(8,128)(2,1)S(1)}, u32[]{:S(2)}, u32[]{:S(2)}) collective-permute-start(bf16[96,192]{1,0:T(8,128)(2,1)S(1)} %get-tuple-element.154), channel_id=1, source_target_pairs={{0,16},{4,20},{8,24},{12,28},{16,0},{20,4},{24,8},{28,12},{1,17},{... | collective-permute-start | bytes 110600 | tf_op jit(solution)/shard_map/ppermute | solution.py:229
  635.5 46.1 %collective-permute-start.37 = (bf16[8,96,768]{2,1,0:T(8,128)(2,1)S(1)}, bf16[8,96,768]{2,1,0:T(8,128)(2,1)S(1)}, u32[]{:S(2)}, u32[]{:S(2)}) collective-permute-start(bf16[8,96,768]{2,1,0:T(8,128)(2,1)S(1)} %dynamic-slice_bitcast_fusion.4), channel_id=1, source_target_pairs={{0,2},{1,3},{2,0},{3,1},{4,6},{5,7},{6,4},{7,5},{8,10},{9,11},{10,... | collective-permute-start | bytes 3538952 | tf_op jit(solution)/shard_map/ppermute | solution.py:229
  656.9 9.9 %collective-permute-start.26 = (bf16[4,3,96,192]{3,2,1,0:T(8,128)(2,1)S(1)}, bf16[4,3,96,192]{3,2,1,0:T(8,128)(2,1)S(1)}, u32[]{:S(2)}, u32[]{:S(2)}) collective-permute-start(bf16[4,3,96,192]{3,2,1,0:T(8,128)(2,1)S(1)} %dynamic-slice_bitcast_fusion.9), channel_id=1, source_target_pairs={{0,4},{4,0},{8,12},{12,8},{16,20},{20,16},{24,28},{28,24},{1,5},{5... | collective-permute-start | bytes 1327112 | tf_op jit(solution)/shard_map/ppermute | solution.py:229
  658.8 44.5 %collective-permute-start.43 = (bf16[8,384,192]{1,2,0:T(8,128)(2,1)S(1)}, bf16[8,384,192]{1,2,0:T(8,128)(2,1)S(1)}, u32[]{:S(2)}, u32[]{:S(2)}) collective-permute-start(bf16[8,384,192]{1,2,0:T(8,128)(2,1)S(1)} %dynamic-slice_bitcast_fusion.3), channel_id=1, source_target_pairs={{0,2},{1,3},{2,0},{3,1},{4,6},{5,7},{6,4},{7,5},{8,10},{9,11},{10,... | collective-permute-start | bytes 3538952 | tf_op jit(solution)/shard_map/ppermute | solution.py:229
  667.1 16.6 %collective-permute-start.27 = (bf16[3,96,192]{2,1,0:T(8,128)(2,1)S(1)}, bf16[3,96,192]{2,1,0:T(8,128)(2,1)S(1)}, u32[]{:S(2)}, u32[]{:S(2)}) collective-permute-start(bf16[3,96,192]{2,1,0:T(8,128)(2,1)S(1)} %get-tuple-element.139), channel_id=1, source_target_pairs={{0,8},{4,12},{8,0},{12,4},{16,24},{20,28},{24,16},{28,20},{1,9},{5... | collective-permute-start | bytes 331784 | tf_op jit(solution)/shard_map/ppermute | solution.py:229
  668.1 15.6 %collective-permute-start.29 = (bf16[3,96,192]{2,1,0:T(8,128)(2,1)S(1)}, bf16[3,96,192]{2,1,0:T(8,128)(2,1)S(1)}, u32[]{:S(2)}, u32[]{:S(2)}) collective-permute-start(bf16[3,96,192]{2,1,0:T(8,128)(2,1)S(1)} %get-tuple-element.140), channel_id=1, source_target_pairs={{0,24},{4,28},{8,16},{12,20},{16,8},{20,12},{24,0},{28,4},{1,25},{... | collective-permute-start | bytes 331784 | tf_op jit(solution)/shard_map/ppermute | solution.py:229
  670.0 13.7 %collective-permute-start.28 = (bf16[3,96,192]{2,1,0:T(8,128)(2,1)S(1)}, bf16[3,96,192]{2,1,0:T(8,128)(2,1)S(1)}, u32[]{:S(2)}, u32[]{:S(2)}) collective-permute-start(bf16[3,96,192]{2,1,0:T(8,128)(2,1)S(1)} %get-tuple-element.141), channel_id=1, source_target_pairs={{0,16},{4,20},{8,24},{12,28},{16,0},{20,4},{24,8},{28,12},{1,17},{... | collective-permute-start | bytes 331784 | tf_op jit(solution)/shard_map/ppermute | solution.py:229
  682.0 23.1 %collective-permute-start.38 = (bf16[4,96,768]{2,1,0:T(8,128)(2,1)S(1)}, bf16[4,96,768]{2,1,0:T(8,128)(2,1)S(1)}, u32[]{:S(2)}, u32[]{:S(2)}) collective-permute-start(bf16[4,96,768]{2,1,0:T(8,128)(2,1)S(1)} %dynamic-slice_bitcast_fusion.8), channel_id=1, source_target_pairs={{0,4},{4,0},{8,12},{12,8},{16,20},{20,16},{24,28},{28,24},{1,5},{5... | collective-permute-start | bytes 1769480 | tf_op jit(solution)/shard_map/ppermute | solution.py:229
  703.6 15.3 %collective-permute-start.44 = (bf16[4,384,192]{1,2,0:T(8,128)(2,1)S(1)}, bf16[4,384,192]{1,2,0:T(8,128)(2,1)S(1)}, u32[]{:S(2)}, u32[]{:S(2)}) collective-permute-start(bf16[4,384,192]{1,2,0:T(8,128)(2,1)S(1)} %dynamic-slice_bitcast_fusion.7), channel_id=1, source_target_pairs={{0,4},{4,0},{8,12},{12,8},{16,20},{20,16},{24,28},{28,24},{1,5},{5... | collective-permute-start | bytes 1769480 | tf_op jit(solution)/shard_map/ppermute | solution.py:229
  705.3 8.1 %collective-permute-start.39 = (bf16[96,768]{1,0:T(8,128)(2,1)S(1)}, bf16[96,768]{1,0:T(8,128)(2,1)S(1)}, u32[]{:S(2)}, u32[]{:S(2)}) collective-permute-start(bf16[96,768]{1,0:T(8,128)(2,1)S(1)} %get-tuple-element.136), channel_id=1, source_target_pairs={{0,8},{4,12},{8,0},{12,4},{16,24},{20,28},{24,16},{28,20},{1,9},{5... | collective-permute-start | bytes 442376 | tf_op jit(solution)/shard_map/ppermute | solution.py:229
  706.1 7.2 collective-permute-start.41
  708.0 9.6 %collective-permute-start.40 = (bf16[96,768]{1,0:T(8,128)(2,1)S(1)}, bf16[96,768]{1,0:T(8,128)(2,1)S(1)}, u32[]{:S(2)}, u32[]{:S(2)}) collective-permute-start(bf16[96,768]{1,0:T(8,128)(2,1)S(1)} %get-tuple-element.138), channel_id=1, source_target_pairs={{0,16},{4,20},{8,24},{12,28},{16,0},{20,4},{24,8},{28,12},{1,17},{... | collective-permute-start | bytes 442376 | tf_op jit(solution)/shard_map/ppermute | solution.py:229
  719.3 9.8 %collective-permute-start.47 = (bf16[384,192]{0,1:T(8,128)(2,1)S(1)}, bf16[384,192]{0,1:T(8,128)(2,1)S(1)}, u32[]{:S(2)}, u32[]{:S(2)}) collective-permute-start(bf16[384,192]{0,1:T(8,128)(2,1)S(1)} %get-tuple-element.134), channel_id=1, source_target_pairs={{0,24},{4,28},{8,16},{12,20},{16,8},{20,12},{24,0},{28,4},{1,25},{... | collective-permute-start | bytes 442376 | tf_op jit(solution)/shard_map/ppermute | solution.py:229
  721.2 15.0 %collective-permute-start.46 = (bf16[384,192]{0,1:T(8,128)(2,1)S(1)}, bf16[384,192]{0,1:T(8,128)(2,1)S(1)}, u32[]{:S(2)}, u32[]{:S(2)}) collective-permute-start(bf16[384,192]{0,1:T(8,128)(2,1)S(1)} %get-tuple-element.135), channel_id=1, source_target_pairs={{0,16},{4,20},{8,24},{12,28},{16,0},{20,4},{24,8},{28,12},{1,17},{... | collective-permute-start | bytes 442376 | tf_op jit(solution)/shard_map/ppermute | solution.py:229
  722.8 15.2 %collective-permute-start.49 = (f32[5,96,96]{2,1,0:T(8,128)S(1)}, f32[5,96,96]{2,1,0:T(8,128)S(1)}, u32[]{:S(2)}, u32[]{:S(2)}) collective-permute-start(f32[5,96,96]{2,1,0:T(8,128)S(1)} %fusion.180), channel_id=1, source_target_pairs={{0,2},{1,3},{2,0},{3,1},{4,6},{5,7},{6,4},{7,5},{8,10},{9,11},{10,... | collective-permute-start | bytes 552968 | tf_op jit(solution)/shard_map/ppermute | solution.py:229
  737.8 7.2 collective-permute-start.50
  745.2 15.8 %collective-permute-start.51 = (f32[1,384,384]{2,1,0:T(8,128)S(1)}, f32[1,384,384]{2,1,0:T(8,128)S(1)}, u32[]{:S(2)}, u32[]{:S(2)}) collective-permute-start(f32[1,384,384]{2,1,0:T(8,128)S(1)} %add.1365), channel_id=1, source_target_pairs={{0,2},{1,3},{2,0},{3,1},{4,6},{5,7},{6,4},{7,5},{8,10},{9,11},{10,... | collective-permute-start | bytes 1769480 | tf_op jit(solution)/shard_map/ppermute | solution.py:229
  (124 other events, 1682.1 us)

commit v2 on v1

v2 whole, which is shorter than its diff:
```python
from functools import partial
import math

import jax
import jax.numpy as jnp
from jax import lax
from jax.experimental import pallas as pl
from jax.experimental.pallas import tpu as pltpu
from jax.sharding import PartitionSpec as P

D = 768
FF = 3072
HEADS = 12
HDIM = 64
FEAT = 32
NS_ITERS = 5
ADAM_STEP = 10


PRECISE = lax.Precision.HIGHEST
NORM_EPS = 1e-05
ORTHO_EPS = 1e-07
ADAM_EPS = 1e-08
LINEAR_COEF = 3.4445
CUBIC_COEF = -4.775
QUINTIC_COEF = 2.0315
MOMENT_DECAY = 0.5
FIRST_DECAY = 0.5
SECOND_DECAY = 0.5
MUON_SCALE = 0.6
WEIGHT_DECAY = 0.01
VECTOR_RATE = 0.4
GROUP = 4
GROUPS = HEADS // GROUP
GE = GROUP * HDIM
GF = GROUP * FEAT


def mm(left, right):
    return jnp.dot(left, right, preferred_element_type=jnp.float32)


def mm_nt(left, right):
    return lax.dot_general(left, right, (((1,), (1,)), ((), ())), preferred_element_type=jnp.float32)


def mm_tn(left, right):
    return lax.dot_general(left, right, (((0,), (0,)), ((), ())), preferred_element_type=jnp.float32)


def halves(value):
    high = value.astype(jnp.bfloat16)
    return high, (value - high.astype(jnp.float32)).astype(jnp.bfloat16)


def normalise(rows):
    centered = rows - jnp.mean(rows, axis=-1, keepdims=True)
    inverse = lax.rsqrt(jnp.mean(centered * centered, axis=-1, keepdims=True) + NORM_EPS)
    return centered * inverse, inverse


def norm_pull(normed, inverse, grad, gain):
    scaled = grad * gain
    mean_plain = jnp.mean(scaled, axis=-1, keepdims=True)
    mean_prod = jnp.mean(scaled * normed, axis=-1, keepdims=True)
    return inverse * (scaled - mean_plain - normed * mean_prod)


def partner_of(values):
    lane = lax.broadcasted_iota(jnp.int32, (values.shape[0], 128), 1)
    first = (lane & (HDIM - 1)) < HDIM // 2
    parts = []
    for at in range(0, values.shape[1], 128):
        block = values[:, at : at + 128]
        ahead = pltpu.roll(block, 128 - HDIM // 2, 1)
        behind = pltpu.roll(block, HDIM // 2, 1)
        parts.append(jnp.where(first, ahead, behind))
    return jnp.concatenate(parts, axis=1)


def head_mask(rows, columns, row_width, column_width):
    row = lax.broadcasted_iota(jnp.int32, (rows, columns), 0) // row_width
    column = lax.broadcasted_iota(jnp.int32, (rows, columns), 1) // column_width
    return row == column


def store_columns(ref, values):
    width = ref.shape[3]
    for n in range(ref.shape[0]):
        ref[n, 0] = values[:, width * n : width * (n + 1)].astype(ref.dtype)


def load_columns(ref):
    return jnp.concatenate([ref[n, 0] for n in range(ref.shape[0])], axis=1)


def attend_kernel(
    lengths_ref, x_ref, w_ref, vec_ref, proj_ref, cos_ref, sin_ref,
    middle_ref, h1_ref, h2_ref, wq_ref, wk_ref, pq_ref, pk_ref, v_ref, state_ref, total_ref, att_ref, rden_ref, mixed_ref,
):
    rows = x_ref.shape[1]
    x = x_ref[0].astype(jnp.float32)
    h1 = (normalise(x)[0] * vec_ref[0:1, :] + vec_ref[1:2, :]).astype(jnp.bfloat16)
    h1_ref[0] = h1
    live = (lax.broadcasted_iota(jnp.int32, (rows, 1), 0) < lengths_ref[pl.program_id(0)]).astype(jnp.float32)
    cosine = jnp.concatenate([cos_ref[...]] * (D // 128), axis=1)
    sine = jnp.concatenate([sin_ref[...]] * (D // 128), axis=1)
    values = mm(h1, w_ref[2]).astype(jnp.bfloat16)
    v_ref[0] = values
    feats = []
    for j, (w_out, p_out) in enumerate(((wq_ref, pq_ref), (wk_ref, pk_ref))):
        heads = mm(h1, w_ref[j])
        unit = (heads * cosine + partner_of(heads) * sine) * HDIM ** (-0.25)
        w_out[0] = unit
        high, low = halves(unit)
        sq_high, sq_low = halves(unit * unit)
        parts = []
        for g in range(GROUPS):
            cut = slice(GE * g, GE * (g + 1))
            left = jnp.concatenate([high[:, cut], low[:, cut], high[:, cut], sq_high[:, cut], sq_low[:, cut]], axis=1)
            parts.append(jnp.exp(mm(left, proj_ref[g])) * FEAT ** (-0.5))
        phi = jnp.concatenate(parts, axis=1)
        p_out[0] = phi
        feats.append(phi)
    query_low = feats[0].astype(jnp.bfloat16)
    key_vals = feats[1].astype(jnp.bfloat16).astype(jnp.float32) * live
    key_low = key_vals.astype(jnp.bfloat16)
    total_ref[0] = jnp.sum(key_vals, axis=0, keepdims=True)
    mask = head_mask(GF, GE, FEAT, HDIM)
    ones = jnp.ones((rows, GE), jnp.bfloat16)
    attended, inverse_den = [], []
    for g in range(GROUPS):
        cut = slice(GE * g, GE * (g + 1))
        fcut = slice(GF * g, GF * (g + 1))
        both = mm_tn(key_low[:, fcut], jnp.concatenate([values[:, cut], ones], axis=1))
        state = jnp.where(mask, both[:, :GE], 0.0).astype(jnp.bfloat16)
        state_ref[0, g] = state
        tot_high, tot_low = halves(jnp.where(mask, both[:, GE:], 0.0))
        query = query_low[:, fcut]
        numer = mm(query, state)
        denom = mm(jnp.concatenate([query, query], axis=1), jnp.concatenate([tot_high, tot_low], axis=0))
        inverse = 1.0 / denom
        attended.append(numer * inverse)
        inverse_den.append(inverse)
    attended = jnp.concatenate(attended, axis=1)
    att_ref[0] = attended
    rden_ref[0] = jnp.concatenate(inverse_den, axis=1)
    mixed = attended.astype(jnp.bfloat16)
    mixed_ref[0] = mixed
    middle = x + mm(mixed, w_ref[3])
    middle_ref[0] = middle
    h2_ref[0] = (normalise(middle)[0] * vec_ref[2:3, :] + vec_ref[3:4, :]).astype(jnp.bfloat16)


def attend_back_kernel(
    lengths_ref, og_ref, gh2_ref, ffn_ref, middle_ref, w_ref, vec_ref, projt_ref, cos_ref, sin_ref,
    wq_ref, wk_ref, pq_ref, pk_ref, v_ref, state_ref, total_ref, att_ref, rden_ref,
    out_ref, gm_ref, gb_ref, gq_ref, gk_ref, gv_ref, sums_ref,
):
    rows = og_ref.shape[1]
    og = og_ref[0].astype(jnp.float32)
    middle = middle_ref[0]
    out_ref[0] = middle + (ffn_ref[0] + vec_ref[4:5, :])
    grad_h2 = gh2_ref[0]
    normed, inverse = normalise(middle)
    grad_middle = og + norm_pull(normed, inverse, grad_h2, vec_ref[2:3, :])
    gm_ref[0] = grad_middle

    @pl.when(pl.program_id(0) == 0)
    def _():
        sums_ref[...] = jnp.zeros_like(sums_ref)

    sums_ref[0:1, :] += jnp.sum(grad_h2 * normed, axis=0, keepdims=True)
    sums_ref[1:2, :] += jnp.sum(grad_h2, axis=0, keepdims=True)
    sums_ref[2:3, :] += jnp.sum(og, axis=0, keepdims=True)
    branch = grad_middle.astype(jnp.bfloat16)
    store_columns(gb_ref, grad_middle)
    grad_numer = mm_nt(branch, w_ref[3]) * rden_ref[0]
    gn_high, gn_low = halves(grad_numer)
    pr_high, pr_low = halves(grad_numer * att_ref[0])
    live = (lax.broadcasted_iota(jnp.int32, (rows, 1), 0) < lengths_ref[pl.program_id(0)]).astype(jnp.float32)
    query_low = pq_ref[0].astype(jnp.bfloat16)
    key_low = (pk_ref[0].astype(jnp.bfloat16).astype(jnp.float32) * live).astype(jnp.bfloat16)
    mask = head_mask(GF, GE, FEAT, HDIM)
    spread = head_mask(GE, GF, HDIM, FEAT).astype(jnp.float32).astype(jnp.bfloat16)
    spread2 = jnp.concatenate([spread, spread], axis=0)
    gather = mask.astype(jnp.float32).astype(jnp.bfloat16)
    gather2 = jnp.concatenate([gather, gather], axis=0)
    grad_u = ([], [])
    grad_v = []
    for g in range(GROUPS):
        cut = slice(GE * g, GE * (g + 1))
        fcut = slice(GF * g, GF * (g + 1))
        query, key, values = query_low[:, fcut], key_low[:, fcut], v_ref[0, :, cut]
        state = state_ref[0, g]
        grad_denom = -mm(jnp.concatenate([pr_high[:, cut], pr_low[:, cut]], axis=1), spread2)
        two = jnp.concatenate([gn_high[:, cut], gn_low[:, cut]], axis=1)
        grad_qfeat = mm_nt(two, jnp.concatenate([state, state], axis=1)) + grad_denom * total_ref[0, :, fcut]
        pair = mm_tn(query, two)
        grad_state = jnp.where(mask, pair[:, :GE] + pair[:, GE:], 0.0)
        grad_total = jnp.sum(grad_denom * query.astype(jnp.float32), axis=0, keepdims=True)
        gs_high, gs_low = halves(grad_state)
        grad_kfeat = mm_nt(
            jnp.concatenate([values, values], axis=1), jnp.concatenate([gs_high, gs_low], axis=1)
        )
        grad_kfeat = (grad_kfeat + grad_total) * live
        grad_v.append(mm(jnp.concatenate([key, key], axis=1), jnp.concatenate([gs_high, gs_low], axis=0)))
        for j, (grad_feat, p_in, w_in) in enumerate(((grad_qfeat, pq_ref, wq_ref), (grad_kfeat, pk_ref, wk_ref))):
            t_high, t_low = halves(grad_feat * p_in[0, :, fcut])
            pulled = mm(jnp.concatenate([t_high, t_low, t_high], axis=1), projt_ref[g])
            weight = mm(jnp.concatenate([t_high, t_low], axis=1), gather2)
            grad_u[j].append((pulled - weight * w_in[0, :, cut]) * HDIM ** (-0.25))
    cosine = jnp.concatenate([cos_ref[...]] * (D // 128), axis=1)
    sine = jnp.concatenate([sin_ref[...]] * (D // 128), axis=1)
    for grads, ref in zip(grad_u, (gq_ref, gk_ref)):
        turned = jnp.concatenate(grads, axis=1)
        store_columns(ref, turned * cosine - partner_of(turned) * sine)
    store_columns(gv_ref, jnp.concatenate(grad_v, axis=1))


def input_back_kernel(x_ref, gm_ref, gq_ref, gk_ref, gv_ref, w_ref, vec_ref, out_ref, sums_ref):
    grad_h1 = sum(mm_nt(load_columns(ref), w_ref[j]) for j, ref in enumerate((gq_ref, gk_ref, gv_ref)))
    normed, inverse = normalise(x_ref[0].astype(jnp.float32))
    out_ref[0] = gm_ref[0] + norm_pull(normed, inverse, grad_h1, vec_ref[0:1, :])

    @pl.when(pl.program_id(0) == 0)
    def _():
        sums_ref[...] = jnp.zeros_like(sums_ref)

    sums_ref[0:1, :] += jnp.sum(grad_h1 * normed, axis=0, keepdims=True)
    sums_ref[1:2, :] += jnp.sum(grad_h1, axis=0, keepdims=True)


def attn_weight_kernel(h1_ref, mixed_ref, gq_ref, gk_ref, gv_ref, gb_ref, out_ref):
    wide, rows = out_ref.shape[1], out_ref.shape[2] // 2
    h1 = h1_ref[...]
    left = mm_tn(h1, jnp.concatenate([gq_ref[...], gk_ref[...]], axis=1)).astype(jnp.bfloat16)
    right = jnp.concatenate([mm_tn(h1, gv_ref[...]), mm_tn(mixed_ref[...], gb_ref[...])], axis=1).astype(jnp.bfloat16)
    for w in range(wide):
        out_ref[0, w, :rows, :] = left[rows * w : rows * (w + 1)]
        out_ref[0, w, rows:, :] = right[rows * w : rows * (w + 1)]


def ffn_kernel(has_past, blocks, h2_ref, og_ref, win_ref, wback_ref, bias_ref, *rest):
    if has_past:
        out_past_ref, gh2_past_ref, out_ref, gh2_ref, gw_ref, bsum_ref, act_ref, gi_ref = rest
    else:
        out_ref, gh2_ref, gw_ref, bsum_ref, act_ref, gi_ref = rest
    seqs, rows = out_ref.shape[0], out_ref.shape[1]
    step = pl.program_id(0)
    win, wback = win_ref[...], wback_ref[...]
    bias = bias_ref[...]

    def part(s, carry):
        span = pl.ds(pl.multiple_of(s * rows, rows), rows)
        inner = mm(h2_ref[s], win) + bias
        grad_act = mm_nt(og_ref[s], wback)
        cdf = 0.5 * (1.0 + lax.erf(inner * (2.0**-0.5)))
        pdf = jnp.exp(-0.5 * inner * inner) * (2.0 * math.pi) ** -0.5
        act = (inner * cdf).astype(jnp.bfloat16)
        grad_inner = (grad_act * (cdf + inner * pdf)).astype(jnp.bfloat16)
        act_ref[span, :] = act
        gi_ref[span, :] = grad_inner
        out_part = mm(act, wback)
        gh2_part = mm_nt(grad_inner, win)

        @pl.when(step == 0)
        def _():
            if has_past:
                out_ref[s] = out_past_ref[s] + out_part
                gh2_ref[s] = gh2_past_ref[s] + gh2_part
            else:
                out_ref[s] = out_part
                gh2_ref[s] = gh2_part

        @pl.when(step > 0)
        def _():
            out_ref[s] += out_part
            gh2_ref[s] += gh2_part

        return carry + jnp.sum(grad_inner.astype(jnp.float32), axis=0, keepdims=True)

    bsum_ref[...] = lax.fori_loop(0, seqs, part, jnp.zeros(bias.shape, jnp.float32))
    h2 = h2_ref[...].reshape(seqs * rows, D)
    og = og_ref[...].reshape(seqs * rows, D)
    grad_in = mm_tn(h2, gi_ref[...]).astype(jnp.bfloat16)
    grad_back = mm_tn(og, act_ref[...]).astype(jnp.bfloat16)
    if not blocks:
        gw_ref[0] = grad_in
        gw_ref[1] = grad_back
        return
    narrow, wide = gw_ref.shape[0], gw_ref.shape[1]
    in_rows, in_cols = D // wide, gw_ref.shape[3]
    width = grad_in.shape[1]
    for k in range(width // in_cols):
        for w in range(wide):
            gw_ref[step * (width // in_cols) + k, w, :in_rows, :] = grad_in[
                in_rows * w : in_rows * (w + 1), in_cols * k : in_cols * (k + 1)
            ]
    back_rows = D // narrow
    half = back_rows // 2
    for k in range(width // 128):
        for n in range(narrow):
            for h in range(2):
                gw_ref[n, step * (width // 128) + k, in_rows:, 128 * h : 128 * (h + 1)] = grad_back[
                    back_rows * n + half * h : back_rows * n + half * (h + 1), 128 * k : 128 * (k + 1)
                ]


def spec(shape, index):
    return pl.BlockSpec(shape, index)


LIMIT = 60 * 1024 * 1024


def estimate(flops, moved, transcendentals=0):
    return pl.CostEstimate(flops=int(flops), bytes_accessed=int(moved), transcendentals=int(transcendentals))


def whole(array):
    rank = array.ndim
    return pl.BlockSpec(array.shape, lambda *unused: (0,) * rank)


def by_seq(shape):
    rank = len(shape)
    return pl.BlockSpec((1,) + tuple(shape[1:]), lambda s, *unused: (s,) + (0,) * (rank - 1))


def by_seq_second(shape):
    rank = len(shape)
    return pl.BlockSpec((shape[0], 1) + tuple(shape[2:]), lambda s, *unused: (0, s) + (0,) * (rank - 2))


def attend(lengths, x, weights, vectors, proj, cosine, sine):
    seqs, rows, unused_width = x.shape
    bf, f4 = jnp.bfloat16, jnp.float32
    shapes = [
        ((seqs, rows, D), f4), ((seqs, rows, D), bf), ((seqs, rows, D), bf), ((seqs, rows, D), f4), ((seqs, rows, D), f4),
        ((seqs, rows, HEADS * FEAT), f4), ((seqs, rows, HEADS * FEAT), f4), ((seqs, rows, D), bf),
        ((seqs, GROUPS, GF, GE), bf), ((seqs, 1, HEADS * FEAT), f4), ((seqs, rows, D), f4), ((seqs, rows, D), f4),
        ((seqs, rows, D), bf),
    ]
    return pl.pallas_call(
        attend_kernel,
        grid_spec=pltpu.PrefetchScalarGridSpec(
            num_scalar_prefetch=1,
            grid=(seqs,),
            in_specs=[by_seq(x.shape)] + [whole(a) for a in (weights, vectors, proj, cosine, sine)],
            out_specs=[by_seq(shape) for shape, unused in shapes],
        ),
        out_shape=[jax.ShapeDtypeStruct(shape, dtype) for shape, dtype in shapes],
        compiler_params=pltpu.CompilerParams(vmem_limit_bytes=LIMIT),
        cost_estimate=estimate(seqs * rows * D * D * 12, 40e6),
        name="attend",
    )(lengths, x, weights, vectors, proj, cosine, sine)


def attend_back(lengths, og, grad_h2, ffn, middle, weights, vectors, projt, cosine, sine, kept, narrow_size):
    seqs, rows, unused_width = og.shape
    bf, f4 = jnp.bfloat16, jnp.float32
    blocked = (narrow_size, seqs, rows, D // narrow_size)
    outs = [((seqs, rows, D), f4, by_seq), ((seqs, rows, D), f4, by_seq)]
    outs += [(blocked, bf, by_seq_second)] + [((seqs, rows, D), bf, by_seq)] * 0
    outs += [(blocked, bf, by_seq_second)] * 3
    out_shapes = [jax.ShapeDtypeStruct(shape, dtype) for shape, dtype, unused in outs]
    out_specs = [make(shape) for shape, unused, make in outs]
    out_shapes.append(jax.ShapeDtypeStruct((8, D), f4))
    out_specs.append(pl.BlockSpec((8, D), lambda s, *unused: (0, 0)))
    return pl.pallas_call(
        attend_back_kernel,
        grid_spec=pltpu.PrefetchScalarGridSpec(
            num_scalar_prefetch=1,
            grid=(seqs,),
            in_specs=[by_seq(a.shape) for a in (og, grad_h2, ffn, middle)]
            + [whole(a) for a in (weights, vectors, projt, cosine, sine)]
            + [by_seq(a.shape) for a in kept],
            out_specs=out_specs,
        ),
        out_shape=out_shapes,
        compiler_params=pltpu.CompilerParams(vmem_limit_bytes=LIMIT),
        cost_estimate=estimate(seqs * rows * D * D * 8, 50e6),
        name="attend_back",
    )(lengths, og, grad_h2, ffn, middle, weights, vectors, projt, cosine, sine, *kept)


def input_back(x, grad_middle, grads, weights, vectors):
    seqs, rows, unused_width = x.shape
    return pl.pallas_call(
        input_back_kernel,
        grid=(seqs,),
        in_specs=[by_seq(x.shape), by_seq(x.shape)] + [by_seq_second(a.shape) for a in grads] + [whole(weights), whole(vectors)],
        out_specs=[by_seq(x.shape), pl.BlockSpec((8, D), lambda s: (0, 0))],
        out_shape=[jax.ShapeDtypeStruct(x.shape, jnp.float32), jax.ShapeDtypeStruct((8, D), jnp.float32)],
        compiler_params=pltpu.CompilerParams(vmem_limit_bytes=LIMIT),
        cost_estimate=estimate(seqs * rows * D * D * 6, 15e6),
        name="input_back",
    )(x, grad_middle, *grads, weights, vectors)


def attn_weights(h1, mixed, grads, wide_size):
    narrow_size, seqs, rows, width = grads[0].shape
    tokens = seqs * rows
    flat = [a.reshape(narrow_size, tokens, width) for a in grads]
    h1, mixed = h1.reshape(tokens, D), mixed.reshape(tokens, D)
    shape = (narrow_size, wide_size, 2 * D // wide_size, 2 * width)
    return pl.pallas_call(
        attn_weight_kernel,
        grid=(narrow_size,),
        in_specs=[whole(h1), whole(mixed)] + [pl.BlockSpec((None, tokens, width), lambda n: (n, 0, 0))] * 4,
        out_specs=pl.BlockSpec((1,) + shape[1:], lambda n: (n, 0, 0, 0)),
        out_shape=jax.ShapeDtypeStruct(shape, jnp.bfloat16),
        compiler_params=pltpu.CompilerParams(vmem_limit_bytes=LIMIT),
        cost_estimate=estimate(tokens * D * D * 8, 15e6),
        name="attn_weights",
    )(h1, mixed, *flat)


def ffn_tile(tile, h2, og, w_in, w_back, bias, past, wide_size, narrow_size, blocks):
    seqs, rows, unused_width = h2.shape
    width = w_in.shape[2]
    step = 512 if width % 512 == 0 else width
    if blocks:
        shape = (narrow_size, wide_size, 2 * D // wide_size, width // narrow_size)
        gw_spec = pl.BlockSpec(shape, lambda i: (0, 0, 0, 0))
    else:
        shape = (2, D, width)
        gw_spec = pl.BlockSpec((2, D, step), lambda i: (0, 0, i))
    tokens = jax.ShapeDtypeStruct(h2.shape, jnp.float32)
    return pl.pallas_call(
        partial(ffn_kernel, past is not None, blocks),
        grid=(width // step,),
        in_specs=[
            whole(h2),
            whole(og),
            pl.BlockSpec((None, D, step), lambda i: (tile, 0, i)),
            pl.BlockSpec((None, step, D), lambda i: (tile, i, 0)),
            pl.BlockSpec((None, 1, step), lambda i: (tile, 0, i)),
        ]
        + [whole(a) for a in past or ()],
        out_specs=[whole(h2), whole(h2), gw_spec, pl.BlockSpec((1, step), lambda i: (0, i))],
        out_shape=[tokens, tokens, jax.ShapeDtypeStruct(shape, jnp.bfloat16), jax.ShapeDtypeStruct((1, width), jnp.float32)],
        scratch_shapes=[pltpu.VMEM((seqs * rows, step), jnp.bfloat16)] * 2,
        compiler_params=pltpu.CompilerParams(vmem_limit_bytes=LIMIT),
        cost_estimate=estimate(seqs * rows * D * width * 12, 20e6, seqs * rows * width * 2),
        name="ffn_tile",
    )(h2, og, w_in, w_back, bias, *(past or ()))


def rotary_blocks(length):
    half = HDIM // 2
    frequency = jnp.exp(jnp.arange(half, dtype=jnp.float32) * (-2.0 * math.log(10000.0) / HDIM))
    angles = jnp.arange(length, dtype=jnp.float32)[:, None] * frequency[None, :]
    cosine, sine = jnp.cos(angles), jnp.sin(angles)
    return jnp.tile(cosine, (1, 4)), jnp.tile(jnp.concatenate([-sine, sine], axis=1), (1, 2))


def projection_blocks(feature_proj):
    rows = jnp.arange(GF)[:, None] // FEAT
    columns = jnp.arange(GE)[None, :] // HDIM
    mask = (rows == columns).astype(jnp.float32)
    tall = jnp.tile(feature_proj.reshape(GROUPS, GF, HDIM), (1, 1, GROUP)) * mask
    high, low = halves(tall)
    square = jnp.broadcast_to(-0.5 * mask, tall.shape).astype(jnp.bfloat16)
    turned = [a.swapaxes(1, 2) for a in (high, high, low, square, square)]
    return jnp.concatenate(turned, axis=1), jnp.concatenate([high, high, low], axis=1)


def xor_pairs(size, mask):
    return [(index, index ^ mask) for index in range(size)]


def swap(value, axis_name, mask):
    return lax.ppermute(value, axis_name, xor_pairs(lax.axis_size(axis_name), mask))


def far_masks(axis_name):
    return [2 * m for m in range(1, lax.axis_size(axis_name) // 2)]


def gather_wide(piece):
    block = jnp.stack([piece] + [swap(piece, "wide", mask) for mask in far_masks("wide")])
    return jnp.stack([block, swap(block, "wide", 1)])


def gather_near(piece, far):
    block = gather_wide(piece)[None]
    if far:
        block = jnp.concatenate([block] + [swap(block, "narrow", mask) for mask in far_masks("narrow")])
    return block, swap(block, "narrow", 1)


def place_kernel(copies, me_ref, mine_ref, theirs_ref, out_ref, sems):
    started = []
    for side, ref in enumerate((mine_ref, theirs_ref)):
        for far in range(ref.shape[0]):
            for near in range(2):
                for m in range(ref.shape[2]):
                    wide = me_ref[0] ^ (2 * m + near)
                    narrow = me_ref[1] ^ (2 * far + side)
                    copy = pltpu.make_async_copy(
                        ref.at[far, near, m], copies(out_ref, wide, narrow), sems.at[len(started)]
                    )
                    copy.start()
                    started.append(copy)
    for copy in started:
        copy.wait()


def place(pair, target, shape, name):
    mine, theirs = pair
    me = jnp.stack([lax.axis_index("wide"), lax.axis_index("narrow")]).astype(jnp.int32)
    anywhere = pl.BlockSpec(memory_space=pl.ANY)
    return pl.pallas_call(
        partial(place_kernel, target),
        out_shape=jax.ShapeDtypeStruct(shape, mine.dtype),
        in_specs=[pl.BlockSpec(memory_space=pltpu.SMEM), anywhere, anywhere],
        out_specs=pl.BlockSpec(memory_space=pltpu.VMEM),
        compiler_params=pltpu.CompilerParams(vmem_limit_bytes=LIMIT),
        scratch_shapes=[pltpu.SemaphoreType.DMA((2 * math.prod(mine.shape[:3]),))],
        cost_estimate=pl.CostEstimate(flops=0, bytes_accessed=2 * math.prod(shape) * 2, transcendentals=0),
        name=name,
    )(me, mine, theirs)


def in_order(pair):
    both = jnp.stack(pair)
    sides, fars, unused_two, ms = both.shape[:4]
    piece = both.shape[4:]
    flat = both.reshape((sides * fars * 2 * ms,) + piece)
    my_wide, my_narrow = lax.axis_index("wide"), lax.axis_index("narrow")
    ordered = []
    for wide_index in range(2 * ms):
        for narrow_index in range(sides * fars):
            wide_mask = wide_index ^ my_wide
            narrow_mask = (narrow_index ^ my_narrow) & (sides * fars - 1)
            at = ((narrow_mask & 1) * fars + (narrow_mask >> 1)) * 2 + (wide_mask & 1)
            ordered.append(pick(flat, at * ms + (wide_mask >> 1), 0))
    return jnp.stack(ordered).reshape((2 * ms, sides * fars) + piece)


def pick(value, index, axis):
    return lax.dynamic_index_in_dim(value, index, axis, keepdims=False)


def fold(value, axis_name, masks, shift):
    place = lax.axis_index(axis_name)
    here = pick(value, (place >> shift) & (value.shape[0] - 1), 0).astype(jnp.float32)
    for mask in masks:
        other = ((place ^ mask) >> shift) & (value.shape[0] - 1)
        here = here + swap(pick(value, other, 0), axis_name, mask).astype(jnp.float32)
    return here


def scatter_blocks(parts, wire, far_last):
    wide_size = lax.axis_size("wide")
    narrow_size = lax.axis_size("narrow")
    rest = parts.shape[2:]
    value = parts.astype(wire).reshape((narrow_size // 2, 2, wide_size) + rest).swapaxes(0, 1)
    value = fold(value, "narrow", [1], 0).astype(wire)
    if not far_last:
        value = fold(value, "narrow", far_masks("narrow"), 1).astype(wire)[None]
    held = value.shape[0]
    value = value.reshape((held, wide_size // 2, 2) + rest)
    value = fold(jnp.moveaxis(value, 2, 0), "wide", [1], 0).astype(wire)
    value = fold(jnp.moveaxis(value, 1, 0), "wide", far_masks("wide"), 1)
    if not far_last:
        return value[0]
    return fold(value.astype(wire), "narrow", far_masks("narrow"), 1)


def narrow_sum(value):
    mask = 1
    while mask < lax.axis_size("narrow"):
        value = value + swap(value, "narrow", mask)
        mask *= 2
    return value


def gram_of(matrices):
    return jnp.einsum("brc,bsc->brs", matrices, matrices, precision=PRECISE)


def bmm(left, right):
    return jnp.einsum("brs,bst->brt", left, right, precision=PRECISE)


def ortho_factor(gram_mat):
    count = gram_mat.shape[-1]
    identity = jnp.eye(count, dtype=jnp.float32)
    square_sum = jnp.trace(gram_mat, axis1=-2, axis2=-1)
    scale = (1.0 / (jnp.sqrt(square_sum) + ORTHO_EPS))[:, None, None]
    gram_mat = gram_mat * scale * scale
    factor = None
    for sweep_index in range(NS_ITERS):
        poly_mat = (
            LINEAR_COEF * identity + CUBIC_COEF * gram_mat + QUINTIC_COEF * bmm(gram_mat, gram_mat)
        )
        factor = poly_mat if factor is None else bmm(poly_mat, factor)
        if sweep_index < NS_ITERS - 1:
            gram_mat = bmm(poly_mat, bmm(gram_mat, poly_mat))
    return factor * scale


def adam_update(param, earlier_first, earlier_second, gradient):
    first_new = FIRST_DECAY * earlier_first + (1.0 - FIRST_DECAY) * gradient
    second_new = SECOND_DECAY * earlier_second + (1.0 - SECOND_DECAY) * gradient * gradient
    first_fix = 1.0 - FIRST_DECAY**ADAM_STEP
    second_fix = 1.0 - SECOND_DECAY**ADAM_STEP
    direction = first_new / first_fix / (jnp.sqrt(second_new / second_fix) + ADAM_EPS)
    return (first_new, second_new, param - VECTOR_RATE * (direction + WEIGHT_DECAY * param))


def per_device(
    block_in,
    out_grad,
    lengths,
    feature_proj,
    attn_in,
    attn_out,
    ffn_in,
    ffn_out,
    norm_params,
    bias_in,
    bias_out,
    mom_attn_in,
    mom_attn_out,
    mom_ffn_in,
    mom_ffn_out,
    first_norms,
    first_bias_in,
    first_bias_out,
    second_norms,
    second_bias_in,
    second_bias_out,
):
    seqs, length, unused_width = block_in.shape
    wide_size, narrow_size = lax.axis_size("wide"), lax.axis_size("narrow")
    column = lax.axis_index("narrow")
    own_rows, own_cols = D // wide_size, D // narrow_size
    ffn_rows = FF // wide_size
    tiles = ffn_rows // 128 if ffn_rows % 128 == 0 else 1
    unit = ffn_rows // tiles
    width = unit * wide_size
    copied = narrow_size == 4 and own_rows % 16 == 0 and unit % 32 == 0 and (width // narrow_size) % 128 == 0
    blocks = unit == 128 and width // narrow_size == 256 and own_cols == 2 * own_rows
    bf = jnp.bfloat16

    four = jnp.concatenate([attn_in.astype(bf), attn_out.astype(bf)[None]])
    low_in = ffn_in.astype(bf).reshape(own_rows, wide_size, tiles, unit).transpose(2, 0, 1, 3).reshape(tiles, own_rows, width)
    low_back = ffn_out.astype(bf).reshape(tiles, unit, D)
    small = jnp.concatenate([norm_params.reshape(-1), bias_in, bias_out]).astype(bf).astype(jnp.float32)
    small_size = small.shape[0]
    small = jnp.pad(small, (0, -small_size % 1024)).reshape(-1, 128)
    part = 4 * D // narrow_size
    four_pair = gather_near(
        lax.dynamic_slice_in_dim(four.transpose(1, 0, 2).reshape(own_rows, 4 * D), column * part, part, 1)
        if part != D
        else pick(four, column, 0),
        True,
    )
    in_part = width // narrow_size
    in_pair = gather_near(lax.dynamic_slice_in_dim(low_in, column * in_part, in_part, 2), True)
    back_part = unit // 2
    back_pair = gather_near(lax.dynamic_slice_in_dim(low_back, (column & 1) * back_part, back_part, 1), False)
    small_all = in_order((gather_wide(small)[None],))[:, 0].reshape(wide_size, -1)[:, :small_size]
    norm_all = small_all[:, : 4 * own_rows].reshape(wide_size, 4, own_rows).transpose(1, 0, 2).reshape(4, D)
    bias_in_all = small_all[:, 4 * own_rows : 4 * own_rows + ffn_rows].reshape(wide_size, tiles, unit)
    bias_in_all = bias_in_all.transpose(1, 0, 2).reshape(tiles, 1, width)
    bias_out_all = small_all[:, 4 * own_rows + ffn_rows :].reshape(1, D)
    vectors = jnp.concatenate([norm_all, bias_out_all, jnp.zeros((3, D), jnp.float32)])
    if copied:
        weights = place(four_pair, lambda out, w, n: out.at[n, pl.ds(w * own_rows, own_rows)], (4, D, D), "place_four")
        w_in = place(
            in_pair,
            lambda out, w, n: out.at[:, pl.ds(w * own_rows, own_rows), pl.ds(n * in_part, in_part)],
            (tiles, D, width),
            "place_in",
        )
        w_back = place(
            back_pair,
            lambda out, w, n: out.at[:, pl.ds(w * unit + (n & 1) * back_part, back_part)],
            (tiles, width, D),
            "place_back",
        )
    else:
        weights = in_order(four_pair).transpose(0, 2, 1, 3).reshape(D, 4, D).transpose(1, 0, 2)
        w_in = in_order(in_pair).transpose(2, 0, 3, 1, 4).reshape(tiles, D, width)
        w_back = in_order(back_pair).transpose(2, 0, 1, 3, 4).reshape(tiles, width, D)

    cosine, sine = rotary_blocks(length)
    proj, projt = projection_blocks(feature_proj)
    middle, h1, h2, *kept, mixed = attend(lengths, block_in, weights, vectors, proj, cosine, sine)
    past = None
    ffn_sums, bias_sums = [], []
    for tile in range(tiles):
        ffn, grad_h2, grad_tile, bias_sum = ffn_tile(
            tile, h2, out_grad, w_in, w_back, bias_in_all, past, wide_size, narrow_size, blocks
        )
        past = (ffn, grad_h2)
        bias_sums.append(bias_sum)
        if blocks:
            ffn_sums.append(scatter_blocks(grad_tile, bf, tile == 1))
        else:
            grad_in = grad_tile[0].reshape(wide_size, own_rows, narrow_size, in_part).transpose(2, 0, 1, 3)
            grad_back = grad_tile[1].reshape(narrow_size, own_cols, wide_size, unit).transpose(0, 2, 1, 3)
            ffn_sums.append((scatter_blocks(grad_in, bf, False), scatter_blocks(grad_back, bf, False)))
    block_out, grad_middle, gb, gq, gk, gv, sums_two = attend_back(
        lengths, out_grad, grad_h2, ffn, middle, weights, vectors, projt, cosine, sine, kept, narrow_size
    )
    grad_four = attn_weights(h1, mixed, (gq, gk, gv, gb), wide_size)
    input_grad, sums_one = input_back(block_in, grad_middle, (gq, gk, gv), weights, vectors)

    four_sum = jnp.concatenate(
        [
            scatter_blocks(grad_four[:, :, own_rows:], bf, False),
            scatter_blocks(grad_four[:, :, :own_rows], bf, True),
        ]
    )
    grad_qkv = jnp.stack([four_sum[own_rows:, :own_cols], four_sum[own_rows:, own_cols:], four_sum[:own_rows, :own_cols]])
    grad_out_w = four_sum[:own_rows, own_cols:]
    in_parts, back_parts = [], []
    for found in ffn_sums:
        if blocks:
            in_parts.append(found[:own_rows])
            back_parts.append(found[own_rows:].reshape(own_rows, 2, 128).transpose(1, 0, 2).reshape(own_cols, 128))
        else:
            in_parts.append(found[0])
            back_parts.append(found[1])
    grad_in_w = jnp.stack([a.reshape(own_rows, wide_size // narrow_size, unit) for a in in_parts], axis=2).reshape(own_rows, -1)
    grad_back_w = jnp.concatenate(back_parts, axis=1).T
    norm_sums = jnp.concatenate([sums_one[:2], sums_two[:2], sums_two[2:3]])
    inner_sums = jnp.concatenate(bias_sums).reshape(tiles, wide_size, unit).transpose(1, 0, 2)
    inner_sums = inner_sums.reshape(wide_size, narrow_size, ffn_rows // narrow_size)
    norm_part = own_rows // narrow_size
    norm_sums = norm_sums.reshape(5, wide_size, narrow_size, norm_part).transpose(1, 2, 0, 3).reshape(wide_size, narrow_size, -1)
    vector_sums = scatter_blocks(jnp.concatenate([norm_sums, inner_sums], axis=2).swapaxes(0, 1), jnp.float32, False)
    grad_norm_vals = vector_sums[: 4 * norm_part].reshape(4, norm_part)
    grad_bias_final = vector_sums[4 * norm_part : 5 * norm_part]
    grad_bias_inner = vector_sums[5 * norm_part :]

    def own_columns(weight):
        block_width = weight.shape[-1] // narrow_size
        return lax.dynamic_slice_in_dim(
            weight, column * block_width, block_width, axis=weight.ndim - 1
        )

    mom_qkv_new = MOMENT_DECAY * mom_attn_in + grad_qkv
    mom_out_new = MOMENT_DECAY * mom_attn_out + grad_out_w
    mom_in_new = MOMENT_DECAY * mom_ffn_in + grad_in_w
    mom_back_new = MOMENT_DECAY * mom_ffn_out + grad_back_w
    stacks = (mom_qkv_new, mom_out_new[None], mom_in_new[None], mom_back_new[None])
    small = jnp.concatenate([gram_of(stacks[0]), gram_of(stacks[1]), gram_of(stacks[2])], axis=0)
    large = gram_of(stacks[3])
    small_factor = ortho_factor(narrow_sum(small))
    large_factor = ortho_factor(narrow_sum(large))
    iterates = (
        bmm(small_factor[:3], stacks[0]),
        bmm(small_factor[3:4], stacks[1]),
        bmm(small_factor[4:5], stacks[2]),
        bmm(large_factor, stacks[3]),
    )
    rate_qkv = MUON_SCALE
    rate_out = MUON_SCALE * math.sqrt(D / (D // 64))
    rate_in = MUON_SCALE * math.sqrt(FF / D)
    rate_back = MUON_SCALE * math.sqrt(D / FF)
    new_qkv = own_columns(attn_in) * (1.0 - rate_qkv * WEIGHT_DECAY) - rate_qkv * iterates[0]
    new_out = own_columns(attn_out) * (1.0 - rate_out * WEIGHT_DECAY) - rate_out * iterates[1][0]
    new_in = own_columns(ffn_in) * (1.0 - rate_in * WEIGHT_DECAY) - rate_in * iterates[2][0]
    new_back = own_columns(ffn_out) * (1.0 - rate_back * WEIGHT_DECAY) - rate_back * iterates[3][0]
    norm_first, norm_second, norm_new = adam_update(
        own_columns(norm_params), first_norms, second_norms, grad_norm_vals
    )
    inner_first, inner_second, inner_new = adam_update(
        own_columns(bias_in), first_bias_in, second_bias_in, grad_bias_inner
    )
    final_first, final_second, final_new = adam_update(
        own_columns(bias_out), first_bias_out, second_bias_out, grad_bias_final
    )
    return (
        block_out,
        input_grad,
        grad_qkv,
        grad_out_w,
        grad_in_w,
        grad_back_w,
        grad_norm_vals,
        grad_bias_inner,
        grad_bias_final,
        mom_qkv_new,
        mom_out_new,
        mom_in_new,
        mom_back_new,
        new_qkv,
        new_out,
        new_in,
        new_back,
        norm_first,
        inner_first,
        final_first,
        norm_second[:2],
        norm_second[2:],
        inner_second,
        final_second,
        norm_new,
        inner_new,
        final_new,
    )


def solution(mesh):
    in_specs = (
        P(("wide", "narrow"), None, None),
        P(("wide", "narrow"), None, None),
        P(("wide", "narrow")),
        P(),
        P(None, "wide", None),
        P("wide", None),
        P("wide", None),
        P("wide", None),
        P(None, "wide"),
        P("wide"),
        P("wide"),
        P(None, "wide", "narrow"),
        P("wide", "narrow"),
        P("wide", "narrow"),
        P("wide", "narrow"),
        P(None, ("wide", "narrow")),
        P(("wide", "narrow")),
        P(("wide", "narrow")),
        P(None, ("wide", "narrow")),
        P(("wide", "narrow")),
        P(("wide", "narrow")),
    )
    out_specs = (
        P(("wide", "narrow"), None, None),
        P(("wide", "narrow"), None, None),
        P(None, "wide", "narrow"),
        P("wide", "narrow"),
        P("wide", "narrow"),
        P("wide", "narrow"),
        P(None, ("wide", "narrow")),
        P(("wide", "narrow")),
        P(("wide", "narrow")),
        P(None, "wide", "narrow"),
        P("wide", "narrow"),
        P("wide", "narrow"),
        P("wide", "narrow"),
        P(None, "wide", "narrow"),
        P("wide", "narrow"),
        P("wide", "narrow"),
        P("wide", "narrow"),
        P(None, ("wide", "narrow")),
        P(("wide", "narrow")),
        P(("wide", "narrow")),
        P(None, ("wide", "narrow")),
        P(None, ("wide", "narrow")),
        P(("wide", "narrow")),
        P(("wide", "narrow")),
        P(None, ("wide", "narrow")),
        P(("wide", "narrow")),
        P(("wide", "narrow")),
    )
    return jax.shard_map(
        per_device, mesh=mesh, in_specs=in_specs, out_specs=out_specs, check_vma=False
    )
```

time: 792 us -> 487 us (0.61)
  local copies, waits for them, and re-layouts: 226 us -> 33.5 us
  Pallas kernels: 0 us -> 133 us
  matrix products: 158 us -> 38.5 us
  blocking collectives: 102 us -> 0 us
  other arithmetic: 71.3 us -> 40.1 us
  starting transfers between devices: 58.8 us -> 80.5 us
  waiting for transfers between devices: 166 us -> 151 us
    pallas_call x0 -> x10, Pallas kernels: none -> 133 us  [the longest x3 56.6 us: ffn_tile(): pl.pallas_call(partial(ffn_kernel, past is not None, blocks), grid=(width...]
    dot_general x24 -> x0, matrix products: 119 us -> none  [the longest x1 29.7 us: forward(): jnp.dot(hidden_two, w_in, preferred_element_type=jnp.float32)]
    unnamed x376 -> x85, local copies, waits for them, and re-layouts: 52.5 us -> 2.41 us
    all_gather x2 -> x0, blocking collectives: 44.5 us -> none  [the longest x1 26.7 us: per_device(): lax.all_gather(low_bias_in, 'wide', axis=0, tiled=True)]
    another operation x13 -> x15, local copies, waits for them, and re-layouts: 44.6 us -> 4.86 us  [the longest x3 2.99 us: projection_blocks(): jnp.tile(feature_proj.reshape(GROUPS, GF, HDIM), (1, 1, GROUP)) * mask]
    psum x1 -> x0, blocking collectives: 39.5 us -> none  [per_device(): lax.psum(gradients[4:], ('wide', 'narrow'))]
    convert_element_type x15 -> x0, local copies, waits for them, and re-layouts: 39.5 us -> none  [the longest x7 23.5 us: blocks_of(): return gradient.astype(jnp.bfloat16).reshape(shape).transpose(2, 0, 1, 3)]
    slice x7 -> x9, local copies, waits for them, and re-layouts: 34.2 us -> 5.87 us  [the longest x1 4.45 us: per_device(): grad_four[:, :, :own_rows]]
  transfers between devices with their start and end apart: 52 -> 61, of which waited for: 21 -> 27; matrix products, arithmetic and copies ran while one was open for 28% -> 16% of each run, Pallas kernels for 0% -> 23%
where the time goes in v2:
time: 487 us; the launch traced here: 479 us
  waiting for transfers between devices  151 us (31%)
  Pallas kernels  133 us (27%)
  starting transfers between devices  80.5 us (17%)
  other arithmetic  40.1 us (8%)
  matrix products  38.5 us (8%)
  local copies, waits for them, and re-layouts  33.5 us (7%)
    ppermute x61, waiting for transfers between devices, swap(): lax.ppermute(value, axis_name, xor_pairs(lax.axis_size(axis_name), mask))  151 us
    ppermute x61, starting transfers between devices, swap(): lax.ppermute(value, axis_name, xor_pairs(lax.axis_size(axis_name), mask))  80.5 us
    pallas_call x3, Pallas kernels, ffn_tile(): pl.pallas_call(partial(ffn_kernel, past is not None, blocks), grid=(width...  56.6 us
    dot_general x38, matrix products, bmm(): return jnp.einsum('brs,bst->brt', left, right, precision=PRECISE)  36.6 us
    pallas_call x1, Pallas kernels, attend_back(): pl.pallas_call(attend_back_kernel, grid_spec=pltpu.PrefetchScalarGridSpec...  19.2 us
    pallas_call x1, Pallas kernels, attend(): pl.pallas_call(attend_kernel, grid_spec=pltpu.PrefetchScalarGridSpec(num_...  18.9 us
    pallas_call x3, Pallas kernels, place(): pl.pallas_call(partial(place_kernel, target), out_shape=jax.ShapeDtypeStr...  16.4 us
    squeeze x24, local copies, waits for them, and re-layouts, pick(): return lax.dynamic_index_in_dim(value, index, axis, keepdims=False)  12.7 us
  transfers between devices with their start and end apart: 61, of which 27 were waited for; matrix products, arithmetic and copies ran while one was open for 16% of the time, Pallas kernels for 23%

profile of v2, /device:TPU:0, one launch (start us, length us, event | category | flops | bytes accessed | tf_op | source)
XLA Modules:
  0.0 479.2 jit_solution(11063278650043462278)
XLA Ops:
  4.0 3.1 collective-permute-start.10
  7.1 2.6 collective-permute-start.11
  10.3 3.9 collective-permute-start.2
  16.0 3.7 collective-permute-done
  19.7 3.4 collective-permute-start.12
  23.1 7.3 %collective-permute-done.1 = bf16[96,768]{1,0:T(8,128)(2,1)S(1)} collective-permute-done((bf16[96,768]{1,0:T(8,128)(2,1)S(1)}, bf16[96,768]{1,0:T(8,128)(2,1)S(1)}, u32[]{:S(2)}, u32[]{:S(2)}) %collective-permute-start.1) | collective-permute-done | bytes 147488 | tf_op jit(solution)/shard_map/ppermute | solution.py:475
  34.4 4.9 %collective-permute-start.17 = (bf16[3,64,768]{2,1,0:T(8,128)(2,1)S(1)}, bf16[3,64,768]{2,1,0:T(8,128)(2,1)S(1)}, u32[]{:S(2)}, u32[]{:S(2)}) collective-permute-start(bf16[3,64,768]{2,1,0:T(8,128)(2,1)S(1)} %constant_dynamic-slice_fusion.12), channel_id=1, source_target_pairs={{0,16},{4,20},{8,24},{12,28},{16,0},{20,4},{24,8},{28,12},{1,17},{... | collective-permute-start | bytes 884744 | tf_op jit(solution)/shard_map/ppermute | solution.py:475
  42.4 3.2 collective-permute-start.7
  45.6 12.4 %collective-permute-done.17 = bf16[3,64,768]{2,1,0:T(8,128)(2,1)S(1)} collective-permute-done((bf16[3,64,768]{2,1,0:T(8,128)(2,1)S(1)}, bf16[3,64,768]{2,1,0:T(8,128)(2,1)S(1)}, u32[]{:S(2)}, u32[]{:S(2)}) %collective-permute-start.17) | collective-permute-done | bytes 294944 | tf_op jit(solution)/shard_map/ppermute | solution.py:475
  67.9 6.7 %collective-permute-done.13 = bf16[4,3,96,256]{3,2,1,0:T(8,128)(2,1)} collective-permute-done((bf16[4,3,96,256]{3,2,1,0:T(8,128)(2,1)}, bf16[4,3,96,256]{3,2,1,0:T(8,128)(2,1)}, u32[]{:S(2)}, u32[]{:S(2)}) %collective-permute-start.13) | collective-permute-done | bytes 589856 | tf_op jit(solution)/shard_map/ppermute | solution.py:475
  78.7 17.3 %collective-permute-done.19 = bf16[4,3,64,768]{3,2,1,0:T(8,128)(2,1)} collective-permute-done((bf16[4,3,64,768]{3,2,1,0:T(8,128)(2,1)}, bf16[4,3,64,768]{3,2,1,0:T(8,128)(2,1)}, u32[]{:S(2)}, u32[]{:S(2)}) %collective-permute-start.19) | collective-permute-done | bytes 1179680 | tf_op jit(solution)/shard_map/ppermute | solution.py:475
  97.6 4.1 pad_maximum_fusion.mine_ref
  103.4 9.0 %collective-permute-done.14 = bf16[1,2,4,3,96,256]{5,4,3,2,1,0:T(8,128)(2,1)S(1)} collective-permute-done((bf16[1,2,4,3,96,256]{5,4,3,2,1,0:T(8,128)(2,1)S(1)}, bf16[1,2,4,3,96,256]{5,4,3,2,1,0:T(8,128)(2,1)S(1)}, u32[]{:S(2)}, u32[]{:S(2)}) %collective-permute-start.14) | collective-permute-done | bytes 1179680 | tf_op jit(solution)/shard_map/ppermute | solution.py:475
  116.5 4.6 collective-permute-done.8
  123.2 2.2 copy.83.proj_ref
  128.9 5.4 %place_back.1.wback_ref = bf16[3,1024,768]{2,1,0:T(8,128)(2,1)} custom-call(s32[2]{0:T(128)} %pad_add_fusion.me_ref, bf16[1,2,4,3,64,768]{5,4,3,2,1,0:T(8,128)(2,1)} %copy-done, bf16[1,2,4,3,64,768]{5,4,3,2,1,0:T(8,128)(2,1)} %collective-permute-done.20.theirs_ref), custom_call_target="tpu_custom_call" | custom-call | bytes 9437184 | tf_op jit(solution)/shard_map/place_back/pallas_call | solution.py:515
  134.3 5.5 %place_four.1.w_ref = bf16[4,768,768]{2,1,0:T(8,128)(2,1)} custom-call(s32[2]{0:T(128)} %pad_add_fusion.me_ref, bf16[2,2,4,96,768]{4,3,2,1,0:T(8,128)(2,1)} %pad_maximum_fusion.mine_ref, bf16[2,2,4,96,768]{4,3,2,1,0:T(8,128)(2,1)} %collective-permute-done.5.theirs_ref), custom_call_target="tpu_custom_call" | custom-call | bytes 9437184 | tf_op jit(solution)/shard_map/place_four/pallas_call | solution.py:515
  139.8 18.9 %attend.1 = (f32[4,208,768]{2,1,0:T(8,128)}, bf16[4,208,768]{2,1,0:T(8,128)(2,1)}, bf16[4,208,768]{2,1,0:T(8,128)(2,1)}, f32[4,208,768]{2,1,0:T(8,128)}, f32[4,2...) custom-call(s32[4]{0:T(128)} %lengths_ref.3, ...), custom_call_target="tpu_custom_call" | custom-call | flops 5888802816 | bytes 40000000 | tf_op jit(solution)/shard_map/attend/pallas_call | solution.py:345
  158.7 5.6 %place_in.1.win_ref = bf16[3,768,1024]{2,1,0:T(8,128)(2,1)} custom-call(s32[2]{0:T(128)} %pad_add_fusion.me_ref, bf16[2,2,4,3,96,256]{5,4,3,2,1,0:T(8,128)(2,1)} %pad_maximum_fusion.1.mine_ref, bf16[2,2,4,3,96,256]{5,4,3,2,1,0:T(8,128)(2,1)} %collective-permute-done.15.theirs_ref), custom_call_target="tpu_custom_call" | custom-call | bytes 9437184 | tf_op jit(solution)/shard_map/place_in/pallas_call | solution.py:515
  164.3 18.1 %ffn_tile.3 = (f32[4,208,768]{2,1,0:T(8,128)}, f32[4,208,768]{2,1,0:T(8,128)}, bf16[4,8,192,256]{3,2,1,0:T(8,128)(2,1)}, f32[1,1024]{1,0:T(1,128)}) custom-call(bf16[4,208,768]{2,1,0:T(8,128)(2,1)} %get-tuple-element.61.h2_ref, bf16[4,208,768]{2,1,0:T(8,128)(2,1)} %og_ref.7, bf16[3,768,1024]{2,1,0:T(8,128)(2,1)} %place_in.1.win_ref, ...), custom_call_target="tpu_custom_call" | custom-call | flops 7851737088 | bytes 20000000 | tf_op jit(solution)/shard_map/ffn_tile/pallas_call | solution.py:431
  182.4 2.7 dynamic-slice_bitcast_fusion.2
  185.1 19.2 %ffn_tile.4 = (f32[4,208,768]{2,1,0:T(8,128)}, f32[4,208,768]{2,1,0:T(8,128)}, bf16[4,8,192,256]{3,2,1,0:T(8,128)(2,1)}, f32[1,1024]{1,0:T(1,128)}) custom-call(bf16[4,208,768]{2,1,0:T(8,128)(2,1)} %get-tuple-element.61.h2_ref, bf16[4,208,768]{2,1,0:T(8,128)(2,1)} %og_ref.7, bf16[3,768,1024]{2,1,0:T(8,128)(2,1)} %place_in.1.win_ref, ...), custom_call_target="tpu_custom_call" | custom-call | flops 7851737088 | bytes 20000000 | tf_op jit(solution)/shard_map/ffn_tile/pallas_call | solution.py:431
  204.3 19.3 %ffn_tile.5 = (f32[4,208,768]{2,1,0:T(8,128)}, f32[4,208,768]{2,1,0:T(8,128)}, bf16[4,8,192,256]{3,2,1,0:T(8,128)(2,1)}, f32[1,1024]{1,0:T(1,128)}) custom-call(bf16[4,208,768]{2,1,0:T(8,128)(2,1)} %get-tuple-element.61.h2_ref, bf16[4,208,768]{2,1,0:T(8,128)(2,1)} %og_ref.7, bf16[3,768,1024]{2,1,0:T(8,128)(2,1)} %place_in.1.win_ref, ...), custom_call_target="tpu_custom_call" | custom-call | flops 7851737088 | bytes 20000000 | tf_op jit(solution)/shard_map/ffn_tile/pallas_call | solution.py:431
  223.6 19.2 %attend_back.1 = (f32[4,208,768]{2,1,0:T(8,128)}, f32[4,208,768]{2,1,0:T(8,128)}, bf16[4,4,208,192]{3,2,1,0:T(8,128)(2,1)}, bf16[4,4,208,192]{3,2,1,0:T(8,128)(2...) custom-call(s32[4]{0:T(128)} %lengths_ref.3, ...), custom_call_target="tpu_custom_call" | custom-call | flops 3925868544 | bytes 50000000 | tf_op jit(solution)/shard_map/attend_back/pallas_call | solution.py:371
  242.9 11.1 %attn_weights.1 = bf16[4,8,192,384]{3,2,1,0:T(8,128)(2,1)} custom-call(bf16[832,768]{1,0:T(8,128)(2,1)} %bitcast.461, bf16[832,768]{1,0:T(8,128)(2,1)} %bitcast.462, bf16[4,832,192]{2,1,0:T(8,128)(2,1)} %bitcast.418, bf16[4,832,192]{2,1,0:T(8,128)(2,1)} %bitcast.419, bf16[4,832,192]{2,1,0:T(8,128)(2,1)} %bitcast.420, bf16[4,832,192]{2,1,0:T(8,128)(2,1)} %bitcast.460), custom_call_target="tpu_custom_call" | custom-call | flops 3925868544 | bytes 15000000 | tf_op jit(solution)/shard_map/attn_weights/pallas_call | solution.py:408
  254.0 4.4 fusion.93
  258.4 10.6 %input_back.1 = (f32[4,208,768]{2,1,0:T(8,128)}, f32[8,768]{1,0:T(8,128)}) custom-call(bf16[4,208,768]{2,1,0:T(8,128)(2,1)} %x_ref.3, f32[4,208,768]{2,1,0:T(8,128)} %get-tuple-element.79.gm_ref, bf16[4,4,208,192]{3,2,1,0:T(8,128)(2,1)} %get-tuple-element.80.gq_ref, bf16[4,4,208,192]{3,2,1,0:T(8,128)(2,1)} %get-tuple-element.81.gk_ref, ...), custom_call_target="tpu_custom_call" | custom-call | flops 2944401408 | bytes 15000000 | tf_op jit(solution)/shard_map/input_back/pallas_call | solution.py:390
  270.9 2.9 dynamic-slice_bitcast_fusion
  279.0 2.4 dynamic-slice_bitcast_fusion.4
  281.6 4.6 collective-permute-start.54
  286.1 2.4 collective-permute-start.56
  309.1 2.2 collective-permute-done.22
  311.6 3.0 collective-permute-start.24
  317.0 2.5 collective-permute-done.23
  320.5 5.2 %collective-permute-done.24 = bf16[2,96,384]{2,1,0:T(8,128)(2,1)S(1)} collective-permute-done((bf16[2,96,384]{2,1,0:T(8,128)(2,1)S(1)}, bf16[2,96,384]{2,1,0:T(8,128)(2,1)S(1)}, u32[]{:S(2)}, u32[]{:S(2)}) %collective-permute-start.24) | collective-permute-done | bytes 147488 | tf_op jit(solution)/shard_map/ppermute | solution.py:475
  327.4 22.4 %collective-permute-done.26 = bf16[96,384]{1,0:T(8,128)(2,1)S(1)} collective-permute-done((bf16[96,384]{1,0:T(8,128)(2,1)S(1)}, bf16[96,384]{1,0:T(8,128)(2,1)S(1)}, u32[]{:S(2)}, u32[]{:S(2)}) %collective-permute-start.26) | collective-permute-done | bytes 73760 | tf_op jit(solution)/shard_map/ppermute | solution.py:475
  356.2 3.0 collective-permute-done.31
  363.4 12.3 %collective-permute-done.40 = bf16[2,4,192,256]{3,2,1,0:T(8,128)(2,1)S(1)} collective-permute-done((bf16[2,4,192,256]{3,2,1,0:T(8,128)(2,1)S(1)}, bf16[2,4,192,256]{3,2,1,0:T(8,128)(2,1)S(1)}, u32[]{:S(2)}, u32[]{:S(2)}) %collective-permute-start.40) | collective-permute-done | bytes 786464 | tf_op jit(solution)/shard_map/ppermute | solution.py:475
  378.1 2.4 collective-permute-start.43
  382.6 6.0 %collective-permute-done.42 = bf16[2,192,256]{2,1,0:T(8,128)(2,1)S(1)} collective-permute-done((bf16[2,192,256]{2,1,0:T(8,128)(2,1)S(1)}, bf16[2,192,256]{2,1,0:T(8,128)(2,1)S(1)}, u32[]{:S(2)}, u32[]{:S(2)}) %collective-permute-start.42) | collective-permute-done | bytes 196640 | tf_op jit(solution)/shard_map/ppermute | solution.py:475
  393.5 5.6 %collective-permute-done.47 = bf16[1,4,192,256]{3,2,1,0:T(8,128)(2,1)} collective-permute-done((bf16[1,4,192,256]{3,2,1,0:T(8,128)(2,1)}, bf16[1,4,192,256]{3,2,1,0:T(8,128)(2,1)}, u32[]{:S(2)}, u32[]{:S(2)}) %collective-permute-start.47) | collective-permute-done | bytes 393248 | tf_op jit(solution)/shard_map/ppermute | solution.py:475
  400.4 3.1 collective-permute-start.36
  407.5 2.4 collective-permute-start.49
  409.9 2.4 collective-permute-start.50
  414.4 6.0 %collective-permute-done.49 = bf16[1,192,256]{2,1,0:T(8,128)(2,1)S(1)} collective-permute-done((bf16[1,192,256]{2,1,0:T(8,128)(2,1)S(1)}, bf16[1,192,256]{2,1,0:T(8,128)(2,1)S(1)}, u32[]{:S(2)}, u32[]{:S(2)}) %collective-permute-start.49) | collective-permute-done | bytes 98336 | tf_op jit(solution)/shard_map/ppermute | solution.py:475
  425.7 5.9 %collective-permute-done.58 = f32[5,96,96]{2,1,0:T(8,128)S(1)} collective-permute-done((f32[5,96,96]{2,1,0:T(8,128)S(1)}, f32[5,96,96]{2,1,0:T(8,128)S(1)}, u32[]{:S(2)}, u32[]{:S(2)}) %collective-permute-start.58) | collective-permute-done | bytes 184352 | tf_op jit(solution)/shard_map/ppermute | solution.py:475
  443.3 2.1 fusion.15
  445.4 8.4 %collective-permute-done.60 = f32[1,384,384]{2,1,0:T(8,128)S(1)} collective-permute-done((f32[1,384,384]{2,1,0:T(8,128)S(1)}, f32[1,384,384]{2,1,0:T(8,128)S(1)}, u32[]{:S(2)}, u32[]{:S(2)}) %collective-permute-start.60) | collective-permute-done | bytes 589856 | tf_op jit(solution)/shard_map/ppermute | solution.py:475
  (362 shorter events, 140.6 us)
Async XLA Ops:
  4.0 30.4 %collective-permute-start.10 = (bf16[3,96,256]{2,1,0:T(8,128)(2,1)}, bf16[3,96,256]{2,1,0:T(8,128)(2,1)S(1)}, u32[]{:S(2)}, u32[]{:S(2)}) collective-permute-start(bf16[3,96,256]{2,1,0:T(8,128)(2,1)} %constant_dynamic-slice_fusion.13), channel_id=1, source_target_pairs={{0,8},{4,12},{8,0},{12,4},{16,24},{20,28},{24,16},{28,20},{1,9},{5... | collective-permute-start | bytes 442376 | tf_op jit(solution)/shard_map/ppermute | solution.py:475
  7.1 32.2 %collective-permute-start.11 = (bf16[3,96,256]{2,1,0:T(8,128)(2,1)}, bf16[3,96,256]{2,1,0:T(8,128)(2,1)}, u32[]{:S(2)}, u32[]{:S(2)}) collective-permute-start(bf16[3,96,256]{2,1,0:T(8,128)(2,1)} %constant_dynamic-slice_fusion.13), channel_id=1, source_target_pairs={{0,16},{4,20},{8,24},{12,28},{16,0},{20,4},{24,8},{28,12},{1,17},{... | collective-permute-start | bytes 442376 | tf_op jit(solution)/shard_map/ppermute | solution.py:475
  9.8 9.9 %collective-permute-start = (bf16[96,768]{1,0:T(8,128)(2,1)S(1)}, bf16[96,768]{1,0:T(8,128)(2,1)S(1)}, u32[]{:S(2)}, u32[]{:S(2)}) collective-permute-start(bf16[96,768]{1,0:T(8,128)(2,1)S(1)} %bitcast.422), channel_id=1, source_target_pairs={{0,8},{4,12},{8,0},{12,4},{16,24},{20,28},{24,16},{28,20},{1,9},{5... | collective-permute-start | bytes 442376 | tf_op jit(solution)/shard_map/ppermute | solution.py:475
  10.3 20.1 %collective-permute-start.1 = (bf16[96,768]{1,0:T(8,128)(2,1)S(1)}, bf16[96,768]{1,0:T(8,128)(2,1)S(1)}, u32[]{:S(2)}, u32[]{:S(2)}) collective-permute-start(bf16[96,768]{1,0:T(8,128)(2,1)S(1)} %bitcast.423), channel_id=1, source_target_pairs={{0,16},{4,20},{8,24},{12,28},{16,0},{20,4},{24,8},{28,12},{1,17},{... | collective-permute-start | bytes 442376 | tf_op jit(solution)/shard_map/ppermute | solution.py:475
  10.3 20.1 %collective-permute-start.2 = (bf16[96,768]{1,0:T(8,128)(2,1)S(1)}, bf16[96,768]{1,0:T(8,128)(2,1)S(1)}, u32[]{:S(2)}, u32[]{:S(2)}) collective-permute-start(bf16[96,768]{1,0:T(8,128)(2,1)S(1)} %bitcast.424), channel_id=1, source_target_pairs={{0,24},{4,28},{8,16},{12,20},{16,8},{20,12},{24,0},{28,4},{1,25},{... | collective-permute-start | bytes 442376 | tf_op jit(solution)/shard_map/ppermute | solution.py:475
  19.7 20.8 %collective-permute-start.12 = (bf16[3,96,256]{2,1,0:T(8,128)(2,1)}, bf16[3,96,256]{2,1,0:T(8,128)(2,1)S(1)}, u32[]{:S(2)}, u32[]{:S(2)}) collective-permute-start(bf16[3,96,256]{2,1,0:T(8,128)(2,1)} %constant_dynamic-slice_fusion.13), channel_id=1, source_target_pairs={{0,24},{4,28},{8,16},{12,20},{16,8},{20,12},{24,0},{28,4},{1,25},{... | collective-permute-start | bytes 442376 | tf_op jit(solution)/shard_map/ppermute | solution.py:475
  30.4 11.9 %collective-permute-start.16 = (bf16[3,64,768]{2,1,0:T(8,128)(2,1)S(1)}, bf16[3,64,768]{2,1,0:T(8,128)(2,1)S(1)}, u32[]{:S(2)}, u32[]{:S(2)}) collective-permute-start(bf16[3,64,768]{2,1,0:T(8,128)(2,1)S(1)} %constant_dynamic-slice_fusion.12), channel_id=1, source_target_pairs={{0,8},{4,12},{8,0},{12,4},{16,24},{20,28},{24,16},{28,20},{1,9},{5... | collective-permute-start | bytes 884744 | tf_op jit(solution)/shard_map/ppermute | solution.py:475
  32.2 29.0 %collective-permute-start.3 = (bf16[4,96,768]{2,1,0:T(8,128)(2,1)S(1)}, bf16[4,96,768]{2,1,0:T(8,128)(2,1)S(1)}, u32[]{:S(2)}, u32[]{:S(2)}) collective-permute-start(bf16[4,96,768]{2,1,0:T(8,128)(2,1)S(1)} %get-tuple-element.133), channel_id=1, source_target_pairs={{0,4},{4,0},{8,12},{12,8},{16,20},{20,16},{24,28},{28,24},{1,5},{5... | collective-permute-start | bytes 1769480 | tf_op jit(solution)/shard_map/ppermute | solution.py:475
  34.4 23.6 %collective-permute-start.17 = (bf16[3,64,768]{2,1,0:T(8,128)(2,1)S(1)}, bf16[3,64,768]{2,1,0:T(8,128)(2,1)S(1)}, u32[]{:S(2)}, u32[]{:S(2)}) collective-permute-start(bf16[3,64,768]{2,1,0:T(8,128)(2,1)S(1)} %constant_dynamic-slice_fusion.12), channel_id=1, source_target_pairs={{0,16},{4,20},{8,24},{12,28},{16,0},{20,4},{24,8},{28,12},{1,17},{... | collective-permute-start | bytes 884744 | tf_op jit(solution)/shard_map/ppermute | solution.py:475
  39.2 19.2 %collective-permute-start.18 = (bf16[3,64,768]{2,1,0:T(8,128)(2,1)S(1)}, bf16[3,64,768]{2,1,0:T(8,128)(2,1)S(1)}, u32[]{:S(2)}, u32[]{:S(2)}) collective-permute-start(bf16[3,64,768]{2,1,0:T(8,128)(2,1)S(1)} %constant_dynamic-slice_fusion.12), channel_id=1, source_target_pairs={{0,24},{4,28},{8,16},{12,20},{16,8},{20,12},{24,0},{28,4},{1,25},{... | collective-permute-start | bytes 884744 | tf_op jit(solution)/shard_map/ppermute | solution.py:475
  40.5 75.0 %collective-permute-start.6 = (f32[8,128]{1,0:T(8,128)}, f32[8,128]{1,0:T(8,128)S(1)}, u32[]{:S(2)}, u32[]{:S(2)}) collective-permute-start(f32[8,128]{1,0:T(8,128)} %get-tuple-element.168), channel_id=1, source_target_pairs={{0,8},{4,12},{8,0},{12,4},{16,24},{20,28},{24,16},{28,20},{1,9},{5... | collective-permute-start | bytes 12296 | tf_op jit(solution)/shard_map/ppermute | solution.py:475
  42.4 74.2 %collective-permute-start.7 = (f32[8,128]{1,0:T(8,128)}, f32[8,128]{1,0:T(8,128)}, u32[]{:S(2)}, u32[]{:S(2)}) collective-permute-start(f32[8,128]{1,0:T(8,128)} %get-tuple-element.168), channel_id=1, source_target_pairs={{0,16},{4,20},{8,24},{12,28},{16,0},{20,4},{24,8},{28,12},{1,17},{... | collective-permute-start | bytes 12296 | tf_op jit(solution)/shard_map/ppermute | solution.py:475
  58.0 16.6 %collective-permute-start.13 = (bf16[4,3,96,256]{3,2,1,0:T(8,128)(2,1)}, bf16[4,3,96,256]{3,2,1,0:T(8,128)(2,1)}, u32[]{:S(2)}, u32[]{:S(2)}) collective-permute-start(bf16[4,3,96,256]{3,2,1,0:T(8,128)(2,1)} %get-tuple-element.131), channel_id=1, source_target_pairs={{0,4},{4,0},{8,12},{12,8},{16,20},{20,16},{24,28},{28,24},{1,5},{5... | collective-permute-start | bytes 1769480 | tf_op jit(solution)/shard_map/ppermute | solution.py:475
  59.7 36.3 %collective-permute-start.19 = (bf16[4,3,64,768]{3,2,1,0:T(8,128)(2,1)}, bf16[4,3,64,768]{3,2,1,0:T(8,128)(2,1)}, u32[]{:S(2)}, u32[]{:S(2)}) collective-permute-start(bf16[4,3,64,768]{3,2,1,0:T(8,128)(2,1)} %get-tuple-element.123), channel_id=1, source_target_pairs={{0,4},{4,0},{8,12},{12,8},{16,20},{20,16},{24,28},{28,24},{1,5},{5... | collective-permute-start | bytes 3538952 | tf_op jit(solution)/shard_map/ppermute | solution.py:475
  62.3 35.3 %collective-permute-start.4 = (bf16[1,2,4,96,768]{4,3,2,1,0:T(8,128)(2,1)}, bf16[1,2,4,96,768]{4,3,2,1,0:T(8,128)(2,1)}, u32[]{:S(2)}, u32[]{:S(2)}) collective-permute-start(bf16[1,2,4,96,768]{4,3,2,1,0:T(8,128)(2,1)} %maximum_bitcast_fusion.1), channel_id=1, source_target_pairs={{0,2},{1,3},{2,0},{3,1},{4,6},{5,7},{6,4},{7,5},{8,10},{9,11},{10,... | collective-permute-start | bytes 3538952 | tf_op jit(solution)/shard_map/ppermute | solution.py:475
  75.7 36.6 %collective-permute-start.14 = (bf16[1,2,4,3,96,256]{5,4,3,2,1,0:T(8,128)(2,1)S(1)}, bf16[1,2,4,3,96,256]{5,4,3,2,1,0:T(8,128)(2,1)S(1)}, u32[]{:S(2)}, u32[]{:S(2)}) collective-permute-start(bf16[1,2,4,3,96,256]{5,4,3,2,1,0:T(8,128)(2,1)S(1)} %maximum_bitcast_fusion.2), channel_id=1, source_target_pairs={{0,2},{1,3},{2,0},{3,1},{4,6},{5,7},{6,4},{7,5},{8,10},{9,11},{10,... | collective-permute-start | bytes 3538952 | tf_op jit(solution)/shard_map/ppermute | solution.py:475
  97.5 31.4 %collective-permute-start.20 = (bf16[1,2,4,3,64,768]{5,4,3,2,1,0:T(8,128)(2,1)S(1)}, bf16[1,2,4,3,64,768]{5,4,3,2,1,0:T(8,128)(2,1)}, u32[]{:S(2)}, u32[]{:S(2)}) collective-permute-start(bf16[1,2,4,3,64,768]{5,4,3,2,1,0:T(8,128)(2,1)S(1)} %maximum_bitcast_fusion.mine_ref), channel_id=1, source_target_pairs={{0,1},{1,0},{2,3},{3,2},{4,5},{5,4},{6,7},{7,6},{8,9},{9,8},{10,11... | collective-permute-start | bytes 7077896 | tf_op jit(solution)/shard_map/ppermute | solution.py:475
  101.7 32.5 %collective-permute-start.5 = (bf16[2,2,4,96,768]{4,3,2,1,0:T(8,128)(2,1)}, bf16[2,2,4,96,768]{4,3,2,1,0:T(8,128)(2,1)}, u32[]{:S(2)}, u32[]{:S(2)}) collective-permute-start(bf16[2,2,4,96,768]{4,3,2,1,0:T(8,128)(2,1)} %pad_maximum_fusion.mine_ref), channel_id=1, source_target_pairs={{0,1},{1,0},{2,3},{3,2},{4,5},{5,4},{6,7},{7,6},{8,9},{9,8},{10,11... | collective-permute-start | bytes 7077896 | tf_op jit(solution)/shard_map/ppermute | solution.py:475
  114.0 44.8 %collective-permute-start.15 = (bf16[2,2,4,3,96,256]{5,4,3,2,1,0:T(8,128)(2,1)}, bf16[2,2,4,3,96,256]{5,4,3,2,1,0:T(8,128)(2,1)}, u32[]{:S(2)}, u32[]{:S(2)}) collective-permute-start(bf16[2,2,4,3,96,256]{5,4,3,2,1,0:T(8,128)(2,1)} %pad_maximum_fusion.1.mine_ref), channel_id=1, source_target_pairs={{0,1},{1,0},{2,3},{3,2},{4,5},{5,4},{6,7},{7,6},{8,9},{9,8},{10,11... | collective-permute-start | bytes 7077896 | tf_op jit(solution)/shard_map/ppermute | solution.py:475
  185.1 115.6 %collective-permute-start.33 = (bf16[2,8,192,256]{3,2,1,0:T(8,128)(2,1)}, bf16[2,8,192,256]{3,2,1,0:T(8,128)(2,1)}, u32[]{:S(2)}, u32[]{:S(2)}) collective-permute-start(bf16[2,8,192,256]{3,2,1,0:T(8,128)(2,1)} %dynamic-slice_bitcast_fusion.2), channel_id=1, source_target_pairs={{0,1},{1,0},{2,3},{3,2},{4,5},{5,4},{6,7},{7,6},{8,9},{9,8},{10,11... | collective-permute-start | bytes 4718600 | tf_op jit(solution)/shard_map/ppermute | solution.py:475
  281.4 12.1 %collective-permute-start.21 = (bf16[2,8,96,384]{3,2,1,0:T(8,128)(2,1)}, bf16[2,8,96,384]{3,2,1,0:T(8,128)(2,1)}, u32[]{:S(2)}, u32[]{:S(2)}) collective-permute-start(bf16[2,8,96,384]{3,2,1,0:T(8,128)(2,1)} %dynamic-slice_bitcast_fusion.4), channel_id=1, source_target_pairs={{0,1},{1,0},{2,3},{3,2},{4,5},{5,4},{6,7},{7,6},{8,9},{9,8},{10,11... | collective-permute-start | bytes 3538952 | tf_op jit(solution)/shard_map/ppermute | solution.py:475
  281.6 8.2 %collective-permute-start.54 = (f32[1,216]{1,0:T(1,128)S(1)}, f32[1,216]{1,0:T(1,128)S(1)}, u32[]{:S(2)}, u32[]{:S(2)}) collective-permute-start(f32[1,216]{1,0:T(1,128)S(1)} %get-tuple-element.164), channel_id=1, source_target_pairs={{0,8},{4,12},{8,0},{12,4},{16,24},{20,28},{24,16},{28,20},{1,9},{5... | collective-permute-start | bytes 2600 | tf_op jit(solution)/shard_map/ppermute | solution.py:475
  289.8 13.6 %collective-permute-start.45 = (bf16[2,8,192,256]{3,2,1,0:T(8,128)(2,1)}, bf16[2,8,192,256]{3,2,1,0:T(8,128)(2,1)}, u32[]{:S(2)}, u32[]{:S(2)}) collective-permute-start(bf16[2,8,192,256]{3,2,1,0:T(8,128)(2,1)} %dynamic-slice_bitcast_fusion), channel_id=1, source_target_pairs={{0,1},{1,0},{2,3},{3,2},{4,5},{5,4},{6,7},{7,6},{8,9},{9,8},{10,11... | collective-permute-start | bytes 4718600 | tf_op jit(solution)/shard_map/ppermute | solution.py:475
  290.6 16.6 %collective-permute-start.39 = (bf16[2,8,192,256]{3,2,1,0:T(8,128)(2,1)}, bf16[2,8,192,256]{3,2,1,0:T(8,128)(2,1)}, u32[]{:S(2)}, u32[]{:S(2)}) collective-permute-start(bf16[2,8,192,256]{3,2,1,0:T(8,128)(2,1)} %dynamic-slice_bitcast_fusion.1), channel_id=1, source_target_pairs={{0,1},{1,0},{2,3},{3,2},{4,5},{5,4},{6,7},{7,6},{8,9},{9,8},{10,11... | collective-permute-start | bytes 4718600 | tf_op jit(solution)/shard_map/ppermute | solution.py:475
  295.5 15.8 %collective-permute-start.22 = (bf16[2,4,96,384]{3,2,1,0:T(8,128)(2,1)S(1)}, bf16[2,4,96,384]{3,2,1,0:T(8,128)(2,1)S(1)}, u32[]{:S(2)}, u32[]{:S(2)}) collective-permute-start(bf16[2,4,96,384]{3,2,1,0:T(8,128)(2,1)S(1)} %dynamic-slice_bitcast_fusion.9), channel_id=1, source_target_pairs={{0,4},{4,0},{8,12},{12,8},{16,20},{20,16},{24,28},{28,24},{1,5},{5... | collective-permute-start | bytes 1769480 | tf_op jit(solution)/shard_map/ppermute | solution.py:475
  299.1 16.2 %collective-permute-start.28 = (bf16[8,96,384]{2,1,0:T(8,128)(2,1)S(1)}, bf16[8,96,384]{2,1,0:T(8,128)(2,1)S(1)}, u32[]{:S(2)}, u32[]{:S(2)}) collective-permute-start(bf16[8,96,384]{2,1,0:T(8,128)(2,1)S(1)} %dynamic-slice_bitcast_fusion.8), channel_id=1, source_target_pairs={{0,2},{1,3},{2,0},{3,1},{4,6},{5,7},{6,4},{7,5},{8,10},{9,11},{10,... | collective-permute-start | bytes 1769480 | tf_op jit(solution)/shard_map/ppermute | solution.py:475
  302.9 58.6 %collective-permute-start.34 = (bf16[8,192,256]{2,1,0:T(8,128)(2,1)S(1)}, bf16[8,192,256]{2,1,0:T(8,128)(2,1)S(1)}, u32[]{:S(2)}, u32[]{:S(2)}) collective-permute-start(bf16[8,192,256]{2,1,0:T(8,128)(2,1)S(1)} %dynamic-slice_bitcast_fusion.7), channel_id=1, source_target_pairs={{0,2},{1,3},{2,0},{3,1},{4,6},{5,7},{6,4},{7,5},{8,10},{9,11},{10,... | collective-permute-start | bytes 2359304 | tf_op jit(solution)/shard_map/ppermute | solution.py:475
  305.6 74.8 %collective-permute-start.46 = (bf16[8,192,256]{2,1,0:T(8,128)(2,1)S(1)}, bf16[8,192,256]{2,1,0:T(8,128)(2,1)S(1)}, u32[]{:S(2)}, u32[]{:S(2)}) collective-permute-start(bf16[8,192,256]{2,1,0:T(8,128)(2,1)S(1)} %dynamic-slice_bitcast_fusion.5), channel_id=1, source_target_pairs={{0,2},{1,3},{2,0},{3,1},{4,6},{5,7},{6,4},{7,5},{8,10},{9,11},{10,... | collective-permute-start | bytes 2359304 | tf_op jit(solution)/shard_map/ppermute | solution.py:475
  311.5 8.0 %collective-permute-start.23 = (bf16[2,96,384]{2,1,0:T(8,128)(2,1)S(1)}, bf16[2,96,384]{2,1,0:T(8,128)(2,1)S(1)}, u32[]{:S(2)}, u32[]{:S(2)}) collective-permute-start(bf16[2,96,384]{2,1,0:T(8,128)(2,1)S(1)} %get-tuple-element.127), channel_id=1, source_target_pairs={{0,8},{4,12},{8,0},{12,4},{16,24},{20,28},{24,16},{28,20},{1,9},{5... | collective-permute-start | bytes 442376 | tf_op jit(solution)/shard_map/ppermute | solution.py:475
  311.6 14.0 %collective-permute-start.24 = (bf16[2,96,384]{2,1,0:T(8,128)(2,1)S(1)}, bf16[2,96,384]{2,1,0:T(8,128)(2,1)S(1)}, u32[]{:S(2)}, u32[]{:S(2)}) collective-permute-start(bf16[2,96,384]{2,1,0:T(8,128)(2,1)S(1)} %get-tuple-element.129), channel_id=1, source_target_pairs={{0,16},{4,20},{8,24},{12,28},{16,0},{20,4},{24,8},{28,12},{1,17},{... | collective-permute-start | bytes 442376 | tf_op jit(solution)/shard_map/ppermute | solution.py:475
  315.4 10.3 %collective-permute-start.25 = (bf16[2,96,384]{2,1,0:T(8,128)(2,1)S(1)}, bf16[2,96,384]{2,1,0:T(8,128)(2,1)S(1)}, u32[]{:S(2)}, u32[]{:S(2)}) collective-permute-start(bf16[2,96,384]{2,1,0:T(8,128)(2,1)S(1)} %get-tuple-element.128), channel_id=1, source_target_pairs={{0,24},{4,28},{8,16},{12,20},{16,8},{20,12},{24,0},{28,4},{1,25},{... | collective-permute-start | bytes 442376 | tf_op jit(solution)/shard_map/ppermute | solution.py:475
  319.5 30.4 %collective-permute-start.29 = (bf16[1,4,96,384]{3,2,1,0:T(8,128)(2,1)S(1)}, bf16[1,4,96,384]{3,2,1,0:T(8,128)(2,1)S(1)}, u32[]{:S(2)}, u32[]{:S(2)}) collective-permute-start(bf16[1,4,96,384]{3,2,1,0:T(8,128)(2,1)S(1)} %dynamic-slice_bitcast_fusion.12), channel_id=1, source_target_pairs={{0,4},{4,0},{8,12},{12,8},{16,20},{20,16},{24,28},{28,24},{1,5},{5... | collective-permute-start | bytes 884744 | tf_op jit(solution)/shard_map/ppermute | solution.py:475
  325.8 24.1 %collective-permute-start.26 = (bf16[96,384]{1,0:T(8,128)(2,1)S(1)}, bf16[96,384]{1,0:T(8,128)(2,1)S(1)}, u32[]{:S(2)}, u32[]{:S(2)}) collective-permute-start(bf16[96,384]{1,0:T(8,128)(2,1)S(1)} %dynamic-slice_bitcast_fusion.29), channel_id=1, source_target_pairs={{0,2},{1,3},{2,0},{3,1},{4,6},{5,7},{6,4},{7,5},{8,10},{9,11},{10,... | collective-permute-start | bytes 221192 | tf_op jit(solution)/shard_map/ppermute | solution.py:475
  351.1 8.1 %collective-permute-start.31 = (bf16[1,96,384]{2,1,0:T(8,128)(2,1)S(1)}, bf16[1,96,384]{2,1,0:T(8,128)(2,1)S(1)}, u32[]{:S(2)}, u32[]{:S(2)}) collective-permute-start(bf16[1,96,384]{2,1,0:T(8,128)(2,1)S(1)} %get-tuple-element.142), channel_id=1, source_target_pairs={{0,16},{4,20},{8,24},{12,28},{16,0},{20,4},{24,8},{28,12},{1,17},{... | collective-permute-start | bytes 221192 | tf_op jit(solution)/shard_map/ppermute | solution.py:475
  355.2 20.5 %collective-permute-start.40 = (bf16[2,4,192,256]{3,2,1,0:T(8,128)(2,1)S(1)}, bf16[2,4,192,256]{3,2,1,0:T(8,128)(2,1)S(1)}, u32[]{:S(2)}, u32[]{:S(2)}) collective-permute-start(bf16[2,4,192,256]{3,2,1,0:T(8,128)(2,1)S(1)} %dynamic-slice_bitcast_fusion.6), channel_id=1, source_target_pairs={{0,4},{4,0},{8,12},{12,8},{16,20},{20,16},{24,28},{28,24},{1,5},{5... | collective-permute-start | bytes 2359304 | tf_op jit(solution)/shard_map/ppermute | solution.py:475
  362.5 31.0 %collective-permute-start.35 = (bf16[1,4,192,256]{3,2,1,0:T(8,128)(2,1)}, bf16[1,4,192,256]{3,2,1,0:T(8,128)(2,1)S(1)}, u32[]{:S(2)}, u32[]{:S(2)}) collective-permute-start(bf16[1,4,192,256]{3,2,1,0:T(8,128)(2,1)} %dynamic-slice_bitcast_fusion.11), channel_id=1, source_target_pairs={{0,4},{4,0},{8,12},{12,8},{16,20},{20,16},{24,28},{28,24},{1,5},{5... | collective-permute-start | bytes 1179656 | tf_op jit(solution)/shard_map/ppermute | solution.py:475
  376.9 11.6 %collective-permute-start.42 = (bf16[2,192,256]{2,1,0:T(8,128)(2,1)S(1)}, bf16[2,192,256]{2,1,0:T(8,128)(2,1)S(1)}, u32[]{:S(2)}, u32[]{:S(2)}) collective-permute-start(bf16[2,192,256]{2,1,0:T(8,128)(2,1)S(1)} %get-tuple-element.126), channel_id=1, source_target_pairs={{0,16},{4,20},{8,24},{12,28},{16,0},{20,4},{24,8},{28,12},{1,17},{... | collective-permute-start | bytes 589832 | tf_op jit(solution)/shard_map/ppermute | solution.py:475
  378.1 10.5 %collective-permute-start.43 = (bf16[2,192,256]{2,1,0:T(8,128)(2,1)S(1)}, bf16[2,192,256]{2,1,0:T(8,128)(2,1)S(1)}, u32[]{:S(2)}, u32[]{:S(2)}) collective-permute-start(bf16[2,192,256]{2,1,0:T(8,128)(2,1)S(1)} %get-tuple-element.125), channel_id=1, source_target_pairs={{0,24},{4,28},{8,16},{12,20},{16,8},{20,12},{24,0},{28,4},{1,25},{... | collective-permute-start | bytes 589832 | tf_op jit(solution)/shard_map/ppermute | solution.py:475
  391.1 8.1 %collective-permute-start.47 = (bf16[1,4,192,256]{3,2,1,0:T(8,128)(2,1)}, bf16[1,4,192,256]{3,2,1,0:T(8,128)(2,1)}, u32[]{:S(2)}, u32[]{:S(2)}) collective-permute-start(bf16[1,4,192,256]{3,2,1,0:T(8,128)(2,1)} %dynamic-slice_bitcast_fusion.10), channel_id=1, source_target_pairs={{0,4},{4,0},{8,12},{12,8},{16,20},{20,16},{24,28},{28,24},{1,5},{5... | collective-permute-start | bytes 1179656 | tf_op jit(solution)/shard_map/ppermute | solution.py:475
  400.4 9.6 %collective-permute-start.36 = (bf16[1,192,256]{2,1,0:T(8,128)(2,1)S(1)}, bf16[1,192,256]{2,1,0:T(8,128)(2,1)S(1)}, u32[]{:S(2)}, u32[]{:S(2)}) collective-permute-start(bf16[1,192,256]{2,1,0:T(8,128)(2,1)S(1)} %get-tuple-element.134), channel_id=1, source_target_pairs={{0,8},{4,12},{8,0},{12,4},{16,24},{20,28},{24,16},{28,20},{1,9},{5... | collective-permute-start | bytes 294920 | tf_op jit(solution)/shard_map/ppermute | solution.py:475
  403.5 10.8 %collective-permute-start.37 = (bf16[1,192,256]{2,1,0:T(8,128)(2,1)S(1)}, bf16[1,192,256]{2,1,0:T(8,128)(2,1)S(1)}, u32[]{:S(2)}, u32[]{:S(2)}) collective-permute-start(bf16[1,192,256]{2,1,0:T(8,128)(2,1)S(1)} %get-tuple-element.136), channel_id=1, source_target_pairs={{0,16},{4,20},{8,24},{12,28},{16,0},{20,4},{24,8},{28,12},{1,17},{... | collective-permute-start | bytes 294920 | tf_op jit(solution)/shard_map/ppermute | solution.py:475
  405.5 8.8 %collective-permute-start.38 = (bf16[1,192,256]{2,1,0:T(8,128)(2,1)S(1)}, bf16[1,192,256]{2,1,0:T(8,128)(2,1)S(1)}, u32[]{:S(2)}, u32[]{:S(2)}) collective-permute-start(bf16[1,192,256]{2,1,0:T(8,128)(2,1)S(1)} %get-tuple-element.135), channel_id=1, source_target_pairs={{0,24},{4,28},{8,16},{12,20},{16,8},{20,12},{24,0},{28,4},{1,25},{... | collective-permute-start | bytes 294920 | tf_op jit(solution)/shard_map/ppermute | solution.py:475
  406.9 7.5 %collective-permute-start.48 = (bf16[1,192,256]{2,1,0:T(8,128)(2,1)S(1)}, bf16[1,192,256]{2,1,0:T(8,128)(2,1)S(1)}, u32[]{:S(2)}, u32[]{:S(2)}) collective-permute-start(bf16[1,192,256]{2,1,0:T(8,128)(2,1)S(1)} %get-tuple-element.137), channel_id=1, source_target_pairs={{0,8},{4,12},{8,0},{12,4},{16,24},{20,28},{24,16},{28,20},{1,9},{5... | collective-permute-start | bytes 294920 | tf_op jit(solution)/shard_map/ppermute | solution.py:475
  407.5 12.8 %collective-permute-start.49 = (bf16[1,192,256]{2,1,0:T(8,128)(2,1)S(1)}, bf16[1,192,256]{2,1,0:T(8,128)(2,1)S(1)}, u32[]{:S(2)}, u32[]{:S(2)}) collective-permute-start(bf16[1,192,256]{2,1,0:T(8,128)(2,1)S(1)} %get-tuple-element.139), channel_id=1, source_target_pairs={{0,16},{4,20},{8,24},{12,28},{16,0},{20,4},{24,8},{28,12},{1,17},{... | collective-permute-start | bytes 294920 | tf_op jit(solution)/shard_map/ppermute | solution.py:475
  409.9 10.4 %collective-permute-start.50 = (bf16[1,192,256]{2,1,0:T(8,128)(2,1)S(1)}, bf16[1,192,256]{2,1,0:T(8,128)(2,1)S(1)}, u32[]{:S(2)}, u32[]{:S(2)}) collective-permute-start(bf16[1,192,256]{2,1,0:T(8,128)(2,1)S(1)} %get-tuple-element.138), channel_id=1, source_target_pairs={{0,24},{4,28},{8,16},{12,20},{16,8},{20,12},{24,0},{28,4},{1,25},{... | collective-permute-start | bytes 294920 | tf_op jit(solution)/shard_map/ppermute | solution.py:475
  423.2 8.4 %collective-permute-start.58 = (f32[5,96,96]{2,1,0:T(8,128)S(1)}, f32[5,96,96]{2,1,0:T(8,128)S(1)}, u32[]{:S(2)}, u32[]{:S(2)}) collective-permute-start(f32[5,96,96]{2,1,0:T(8,128)S(1)} %fusion.86), channel_id=1, source_target_pairs={{0,2},{1,3},{2,0},{3,1},{4,6},{5,7},{6,4},{7,5},{8,10},{9,11},{10,... | collective-permute-start | bytes 552968 | tf_op jit(solution)/shard_map/ppermute | solution.py:475
  425.4 13.3 %collective-permute-start.59 = (f32[1,384,384]{2,1,0:T(8,128)S(1)}, f32[1,384,384]{2,1,0:T(8,128)S(1)}, u32[]{:S(2)}, u32[]{:S(2)}) collective-permute-start(f32[1,384,384]{2,1,0:T(8,128)S(1)} %convolution_bitcast_fusion), channel_id=1, source_target_pairs={{0,1},{1,0},{2,3},{3,2},{4,5},{5,4},{6,7},{7,6},{8,9},{9,8},{10,11... | collective-permute-start | bytes 1769480 | tf_op jit(solution)/shard_map/ppermute | solution.py:475
  438.8 15.0 %collective-permute-start.60 = (f32[1,384,384]{2,1,0:T(8,128)S(1)}, f32[1,384,384]{2,1,0:T(8,128)S(1)}, u32[]{:S(2)}, u32[]{:S(2)}) collective-permute-start(f32[1,384,384]{2,1,0:T(8,128)S(1)} %add.557), channel_id=1, source_target_pairs={{0,2},{1,3},{2,0},{3,1},{4,6},{5,7},{6,4},{7,5},{8,10},{9,11},{10,... | collective-permute-start | bytes 1769480 | tf_op jit(solution)/shard_map/ppermute | solution.py:475
  (54 other events, 634.4 us)

commit v3 on v2

v3 whole, which is shorter than its diff:
```python
from functools import partial
import math

import jax
import jax.numpy as jnp
from jax import lax
from jax.experimental import pallas as pl
from jax.experimental.pallas import tpu as pltpu
from jax.sharding import PartitionSpec as P

D = 768
FF = 3072
HEADS = 12
HDIM = 64
FEAT = 32
NS_ITERS = 5
ADAM_STEP = 10


PRECISE = lax.Precision.HIGHEST
NORM_EPS = 1e-05
ORTHO_EPS = 1e-07
ADAM_EPS = 1e-08
LINEAR_COEF = 3.4445
CUBIC_COEF = -4.775
QUINTIC_COEF = 2.0315
MOMENT_DECAY = 0.5
FIRST_DECAY = 0.5
SECOND_DECAY = 0.5
MUON_SCALE = 0.6
WEIGHT_DECAY = 0.01
VECTOR_RATE = 0.4
GROUP = 4
GROUPS = HEADS // GROUP
GE = GROUP * HDIM
GF = GROUP * FEAT


def mm(left, right):
    return jnp.dot(left, right, preferred_element_type=jnp.float32)


def mm_nt(left, right):
    return lax.dot_general(left, right, (((1,), (1,)), ((), ())), preferred_element_type=jnp.float32)


def mm_tn(left, right):
    return lax.dot_general(left, right, (((0,), (0,)), ((), ())), preferred_element_type=jnp.float32)


def halves(value):
    high = value.astype(jnp.bfloat16)
    return high, (value - high.astype(jnp.float32)).astype(jnp.bfloat16)


def normalise(rows):
    centered = rows - jnp.mean(rows, axis=-1, keepdims=True)
    inverse = lax.rsqrt(jnp.mean(centered * centered, axis=-1, keepdims=True) + NORM_EPS)
    return centered * inverse, inverse


def norm_pull(normed, inverse, grad, gain):
    scaled = grad * gain
    mean_plain = jnp.mean(scaled, axis=-1, keepdims=True)
    mean_prod = jnp.mean(scaled * normed, axis=-1, keepdims=True)
    return inverse * (scaled - mean_plain - normed * mean_prod)


def partner_of(values):
    lane = lax.broadcasted_iota(jnp.int32, (values.shape[0], 128), 1)
    first = (lane & (HDIM - 1)) < HDIM // 2
    parts = []
    for at in range(0, values.shape[1], 128):
        block = values[:, at : at + 128]
        ahead = pltpu.roll(block, 128 - HDIM // 2, 1)
        behind = pltpu.roll(block, HDIM // 2, 1)
        parts.append(jnp.where(first, ahead, behind))
    return jnp.concatenate(parts, axis=1)


def head_mask(rows, columns, row_width, column_width):
    row = lax.broadcasted_iota(jnp.int32, (rows, columns), 0) // row_width
    column = lax.broadcasted_iota(jnp.int32, (rows, columns), 1) // column_width
    return row == column


def store_columns(ref, values):
    width = ref.shape[3]
    for n in range(ref.shape[0]):
        ref[n, 0] = values[:, width * n : width * (n + 1)].astype(ref.dtype)


def load_columns(ref):
    return jnp.concatenate([ref[n, 0] for n in range(ref.shape[0])], axis=1)


def attend_kernel(
    first, lengths_ref, x_ref, w_ref, vec_ref, proj_ref, cos_ref, sin_ref,
    middle_ref, h1_ref, h2_ref, wq_ref, wk_ref, pq_ref, pk_ref, v_ref, state_ref, total_ref, att_ref, rden_ref, mixed_ref,
):
    rows = x_ref.shape[1]
    x = x_ref[0].astype(jnp.float32)
    h1 = (normalise(x)[0] * vec_ref[0:1, :] + vec_ref[1:2, :]).astype(jnp.bfloat16)
    h1_ref[0] = h1
    live = lax.broadcasted_iota(jnp.int32, (rows, 1), 0) < lengths_ref[pl.program_id(0) + first]
    live = live.astype(jnp.float32)
    cosine = jnp.concatenate([cos_ref[...]] * (D // 128), axis=1)
    sine = jnp.concatenate([sin_ref[...]] * (D // 128), axis=1)
    values = mm(h1, w_ref[2]).astype(jnp.bfloat16)
    v_ref[0] = values
    feats = []
    for j, (w_out, p_out) in enumerate(((wq_ref, pq_ref), (wk_ref, pk_ref))):
        heads = mm(h1, w_ref[j])
        unit = (heads * cosine + partner_of(heads) * sine) * HDIM ** (-0.25)
        w_out[0] = unit
        high, low = halves(unit)
        sq_high, sq_low = halves(unit * unit)
        parts = []
        for g in range(GROUPS):
            cut = slice(GE * g, GE * (g + 1))
            left = jnp.concatenate([high[:, cut], low[:, cut], high[:, cut], sq_high[:, cut], sq_low[:, cut]], axis=1)
            parts.append(jnp.exp(mm(left, proj_ref[g])) * FEAT ** (-0.5))
        phi = jnp.concatenate(parts, axis=1)
        p_out[0] = phi
        feats.append(phi)
    query_low = feats[0].astype(jnp.bfloat16)
    key_vals = feats[1].astype(jnp.bfloat16).astype(jnp.float32) * live
    key_low = key_vals.astype(jnp.bfloat16)
    total_ref[0] = jnp.sum(key_vals, axis=0, keepdims=True)
    mask = head_mask(GF, GE, FEAT, HDIM)
    ones = jnp.ones((rows, GE), jnp.bfloat16)
    attended, inverse_den = [], []
    for g in range(GROUPS):
        cut = slice(GE * g, GE * (g + 1))
        fcut = slice(GF * g, GF * (g + 1))
        both = mm_tn(key_low[:, fcut], jnp.concatenate([values[:, cut], ones], axis=1))
        state = jnp.where(mask, both[:, :GE], 0.0).astype(jnp.bfloat16)
        state_ref[0, g] = state
        tot_high, tot_low = halves(jnp.where(mask, both[:, GE:], 0.0))
        query = query_low[:, fcut]
        numer = mm(query, state)
        denom = mm(jnp.concatenate([query, query], axis=1), jnp.concatenate([tot_high, tot_low], axis=0))
        inverse = 1.0 / denom
        attended.append(numer * inverse)
        inverse_den.append(inverse)
    attended = jnp.concatenate(attended, axis=1)
    att_ref[0] = attended
    rden_ref[0] = jnp.concatenate(inverse_den, axis=1)
    mixed = attended.astype(jnp.bfloat16)
    mixed_ref[0] = mixed
    middle = x + mm(mixed, w_ref[3])
    middle_ref[0] = middle
    h2_ref[0] = (normalise(middle)[0] * vec_ref[2:3, :] + vec_ref[3:4, :]).astype(jnp.bfloat16)


def middle_back_kernel(og_ref, gh2_ref, ffn_ref, middle_ref, vec_ref, out_ref, gm_ref, gb_ref, sums_ref):
    og = og_ref[0].astype(jnp.float32)
    middle = middle_ref[0]
    out_ref[0] = middle + (ffn_ref[0] + vec_ref[4:5, :])
    grad_h2 = gh2_ref[0]
    normed, inverse = normalise(middle)
    grad_middle = og + norm_pull(normed, inverse, grad_h2, vec_ref[2:3, :])
    gm_ref[0] = grad_middle
    store_columns(gb_ref, grad_middle)

    @pl.when(pl.program_id(0) == 0)
    def _():
        sums_ref[...] = jnp.zeros_like(sums_ref)

    sums_ref[0:1, :] += jnp.sum(grad_h2 * normed, axis=0, keepdims=True)
    sums_ref[1:2, :] += jnp.sum(grad_h2, axis=0, keepdims=True)
    sums_ref[2:3, :] += jnp.sum(og, axis=0, keepdims=True)


def attend_back_kernel(
    lengths_ref, gm_ref, w_ref, projt_ref, cos_ref, sin_ref,
    wq_ref, wk_ref, pq_ref, pk_ref, v_ref, state_ref, total_ref, att_ref, rden_ref,
    gq_ref, gk_ref, gv_ref,
):
    rows = gm_ref.shape[1]
    branch = gm_ref[0].astype(jnp.bfloat16)
    grad_numer = mm_nt(branch, w_ref[0]) * rden_ref[0]
    gn_high, gn_low = halves(grad_numer)
    pr_high, pr_low = halves(grad_numer * att_ref[0])
    live = (lax.broadcasted_iota(jnp.int32, (rows, 1), 0) < lengths_ref[pl.program_id(0)]).astype(jnp.float32)
    query_low = pq_ref[0].astype(jnp.bfloat16)
    key_low = (pk_ref[0].astype(jnp.bfloat16).astype(jnp.float32) * live).astype(jnp.bfloat16)
    mask = head_mask(GF, GE, FEAT, HDIM)
    spread = head_mask(GE, GF, HDIM, FEAT).astype(jnp.float32).astype(jnp.bfloat16)
    spread2 = jnp.concatenate([spread, spread], axis=0)
    gather = mask.astype(jnp.float32).astype(jnp.bfloat16)
    gather2 = jnp.concatenate([gather, gather], axis=0)
    grad_u = ([], [])
    grad_v = []
    for g in range(GROUPS):
        cut = slice(GE * g, GE * (g + 1))
        fcut = slice(GF * g, GF * (g + 1))
        query, key, values = query_low[:, fcut], key_low[:, fcut], v_ref[0, :, cut]
        state = state_ref[0, g]
        grad_denom = -mm(jnp.concatenate([pr_high[:, cut], pr_low[:, cut]], axis=1), spread2)
        two = jnp.concatenate([gn_high[:, cut], gn_low[:, cut]], axis=1)
        grad_qfeat = mm_nt(two, jnp.concatenate([state, state], axis=1)) + grad_denom * total_ref[0, :, fcut]
        pair = mm_tn(query, two)
        grad_state = jnp.where(mask, pair[:, :GE] + pair[:, GE:], 0.0)
        grad_total = jnp.sum(grad_denom * query.astype(jnp.float32), axis=0, keepdims=True)
        gs_high, gs_low = halves(grad_state)
        grad_kfeat = mm_nt(
            jnp.concatenate([values, values], axis=1), jnp.concatenate([gs_high, gs_low], axis=1)
        )
        grad_kfeat = (grad_kfeat + grad_total) * live
        grad_v.append(mm(jnp.concatenate([key, key], axis=1), jnp.concatenate([gs_high, gs_low], axis=0)))
        for j, (grad_feat, p_in, w_in) in enumerate(((grad_qfeat, pq_ref, wq_ref), (grad_kfeat, pk_ref, wk_ref))):
            t_high, t_low = halves(grad_feat * p_in[0, :, fcut])
            pulled = mm(jnp.concatenate([t_high, t_low, t_high], axis=1), projt_ref[g])
            weight = mm(jnp.concatenate([t_high, t_low], axis=1), gather2)
            grad_u[j].append((pulled - weight * w_in[0, :, cut]) * HDIM ** (-0.25))
    cosine = jnp.concatenate([cos_ref[...]] * (D // 128), axis=1)
    sine = jnp.concatenate([sin_ref[...]] * (D // 128), axis=1)
    for grads, ref in zip(grad_u, (gq_ref, gk_ref)):
        turned = jnp.concatenate(grads, axis=1)
        store_columns(ref, turned * cosine - partner_of(turned) * sine)
    store_columns(gv_ref, jnp.concatenate(grad_v, axis=1))


def input_back_kernel(x_ref, gm_ref, gq_ref, gk_ref, gv_ref, w_ref, vec_ref, out_ref, sums_ref):
    grad_h1 = sum(mm_nt(load_columns(ref), w_ref[j]) for j, ref in enumerate((gq_ref, gk_ref, gv_ref)))
    normed, inverse = normalise(x_ref[0].astype(jnp.float32))
    out_ref[0] = gm_ref[0] + norm_pull(normed, inverse, grad_h1, vec_ref[0:1, :])

    @pl.when(pl.program_id(0) == 0)
    def _():
        sums_ref[...] = jnp.zeros_like(sums_ref)

    sums_ref[0:1, :] += jnp.sum(grad_h1 * normed, axis=0, keepdims=True)
    sums_ref[1:2, :] += jnp.sum(grad_h1, axis=0, keepdims=True)


def attn_weight_kernel(me_ref, h1_ref, mixed_ref, gq_ref, gk_ref, gv_ref, gb_ref, *out_refs):
    width, rows = out_refs[0].shape[1], out_refs[0].shape[2] // 2
    h1 = h1_ref[...]
    left = mm_tn(h1, jnp.concatenate([gq_ref[...], gk_ref[...]], axis=1)).astype(jnp.bfloat16)
    right = jnp.concatenate([mm_tn(h1, gv_ref[...]), mm_tn(mixed_ref[...], gb_ref[...])], axis=1).astype(jnp.bfloat16)
    for w in range(width * len(out_refs)):
        out_refs[w // width][0, w % width, :rows] = left[rows * w : rows * (w + 1)]
        out_refs[w // width][0, w % width, rows:] = right[rows * w : rows * (w + 1)]


def ffn_kernel(has_past, blocks, h2_ref, og_ref, win_ref, wback_ref, bias_ref, me_ref, *rest):
    if has_past:
        out_past_ref, gh2_past_ref, *rest = rest
    if blocks:
        out_ref, gh2_ref, bsum_ref, keep_ref, *send_refs, act_ref, gi_ref, gw_ref = rest
    else:
        out_ref, gh2_ref, bsum_ref, gw_ref, act_ref, gi_ref = rest
    seqs, rows = out_ref.shape[0], out_ref.shape[1]
    step = pl.program_id(0)
    win, wback = win_ref[...], wback_ref[...]
    bias = bias_ref[...]

    def part(s, carry):
        span = pl.ds(pl.multiple_of(s * rows, rows), rows)
        inner = mm(h2_ref[s], win) + bias
        grad_act = mm_nt(og_ref[s], wback)
        cdf = 0.5 * (1.0 + lax.erf(inner * (2.0**-0.5)))
        pdf = jnp.exp(-0.5 * inner * inner) * (2.0 * math.pi) ** -0.5
        act = (inner * cdf).astype(jnp.bfloat16)
        grad_inner = (grad_act * (cdf + inner * pdf)).astype(jnp.bfloat16)
        act_ref[span, :] = act
        gi_ref[span, :] = grad_inner
        out_part = mm(act, wback)
        gh2_part = mm_nt(grad_inner, win)

        @pl.when(step == 0)
        def _():
            if has_past:
                out_ref[s] = out_past_ref[s] + out_part
                gh2_ref[s] = gh2_past_ref[s] + gh2_part
            else:
                out_ref[s] = out_part
                gh2_ref[s] = gh2_part

        @pl.when(step > 0)
        def _():
            out_ref[s] += out_part
            gh2_ref[s] += gh2_part

        return carry + jnp.sum(grad_inner.astype(jnp.float32), axis=0, keepdims=True)

    bsum_ref[...] = lax.fori_loop(0, seqs, part, jnp.zeros(bias.shape, jnp.float32))
    h2 = h2_ref[...].reshape(seqs * rows, D)
    og = og_ref[...].reshape(seqs * rows, D)
    grad_in = mm_tn(h2, gi_ref[...]).astype(jnp.bfloat16)
    grad_back = mm_tn(og, act_ref[...]).astype(jnp.bfloat16)
    if not blocks:
        gw_ref[0] = grad_in
        gw_ref[1] = grad_back
        return
    narrow, wide = gw_ref.shape[0], gw_ref.shape[1]
    in_rows, in_cols = D // wide, gw_ref.shape[3]
    width = grad_in.shape[1]
    for k in range(width // in_cols):
        for w in range(wide):
            gw_ref[step * (width // in_cols) + k, w, :in_rows, :] = grad_in[
                in_rows * w : in_rows * (w + 1), in_cols * k : in_cols * (k + 1)
            ]
    back_rows = D // narrow
    half = back_rows // 2
    for k in range(width // 128):
        for n in range(narrow):
            for h in range(2):
                gw_ref[n, step * (width // 128) + k, in_rows:, 128 * h : 128 * (h + 1)] = grad_back[
                    back_rows * n + half * h : back_rows * n + half * (h + 1), 128 * k : 128 * (k + 1)
                ]

    @pl.when(step == pl.num_programs(0) - 1)
    def _():
        side = me_ref[1] & 1
        for far in range(narrow // 2):
            for w in range(wide):
                keep_ref[far, w] = gw_ref[2 * far + side, w]
                width = wide // len(send_refs)
                send_refs[w // width][far, w % width] = gw_ref[2 * far + (1 - side), w]


def spec(shape, index):
    return pl.BlockSpec(shape, index)


LIMIT = 60 * 1024 * 1024
ANYWHERE = pl.BlockSpec(memory_space=pl.ANY)


def skipping(kernel, before, extra):
    def run(*refs):
        return kernel(*refs[:before], *refs[before + extra :])

    return run


def estimate(flops, moved, transcendentals=0):
    return pl.CostEstimate(flops=int(flops), bytes_accessed=int(moved), transcendentals=int(transcendentals))


def whole(array):
    rank = array.ndim
    return pl.BlockSpec(array.shape, lambda *unused: (0,) * rank)


def by_seq(shape):
    rank = len(shape)
    return pl.BlockSpec((1,) + tuple(shape[1:]), lambda s, *unused: (s,) + (0,) * (rank - 1))


def by_seq_second(shape):
    rank = len(shape)
    return pl.BlockSpec((shape[0], 1) + tuple(shape[2:]), lambda s, *unused: (0, s) + (0,) * (rank - 2))


def attend(lengths, x, weights, vectors, proj, cosine, sine, before, after):
    seqs, rows, unused_width = x.shape
    bf, f4 = jnp.bfloat16, jnp.float32
    shapes = [
        ((seqs, rows, D), f4), ((seqs, rows, D), bf), ((seqs, rows, D), bf), ((seqs, rows, D), f4), ((seqs, rows, D), f4),
        ((seqs, rows, HEADS * FEAT), f4), ((seqs, rows, HEADS * FEAT), f4), ((seqs, rows, D), bf),
        ((seqs, GROUPS, GF, GE), bf), ((seqs, 1, HEADS * FEAT), f4), ((seqs, rows, D), f4), ((seqs, rows, D), f4),
        ((seqs, rows, D), bf),
    ]
    half = seqs // 2
    first = 0 if before is None else half
    before = list(before or [])

    def part(shape):
        rank = len(shape)
        return pl.BlockSpec((1,) + tuple(shape[1:]), lambda s, *unused: (s + first,) + (0,) * (rank - 1))

    return pl.pallas_call(
        skipping(partial(attend_kernel, first), 7, len(after) + len(before)),
        grid_spec=pltpu.PrefetchScalarGridSpec(
            num_scalar_prefetch=1,
            grid=(half if first == 0 else seqs - half,),
            in_specs=[part(x.shape)] + [whole(a) for a in (weights, vectors, proj, cosine, sine)]
            + [ANYWHERE] * (len(after) + len(before)),
            out_specs=[part(shape) for shape, unused in shapes],
        ),
        out_shape=[jax.ShapeDtypeStruct(shape, dtype) for shape, dtype in shapes],
        input_output_aliases={7 + len(after) + k: k for k in range(len(before))},
        compiler_params=pltpu.CompilerParams(vmem_limit_bytes=LIMIT),
        cost_estimate=estimate(seqs * rows * D * D * 6, 20e6),
        name="attend",
    )(lengths, x, weights, vectors, proj, cosine, sine, *after, *before)


def middle_back(og, grad_h2, ffn, middle, vectors, narrow_size):
    seqs, rows, unused_width = og.shape
    blocked = (narrow_size, seqs, rows, D // narrow_size)
    full = jax.ShapeDtypeStruct(og.shape, jnp.float32)
    return pl.pallas_call(
        middle_back_kernel,
        grid=(seqs,),
        in_specs=[by_seq(og.shape)] * 4 + [whole(vectors)],
        out_specs=[by_seq(og.shape)] * 2 + [by_seq_second(blocked), pl.BlockSpec((8, D), lambda s: (0, 0))],
        out_shape=[full, full, jax.ShapeDtypeStruct(blocked, jnp.bfloat16), jax.ShapeDtypeStruct((8, D), jnp.float32)],
        compiler_params=pltpu.CompilerParams(vmem_limit_bytes=LIMIT),
        cost_estimate=estimate(1e7, 16e6),
        name="middle_back",
    )(og, grad_h2, ffn, middle, vectors)


def attend_back(lengths, grad_middle, weights, projt, cosine, sine, kept, narrow_size, after):
    seqs, rows, unused_width = grad_middle.shape
    blocked = (narrow_size, seqs, rows, D // narrow_size)
    count = 6 + len(kept)
    return pl.pallas_call(
        skipping(attend_back_kernel, count, len(after)),
        grid_spec=pltpu.PrefetchScalarGridSpec(
            num_scalar_prefetch=1,
            grid=(seqs,),
            in_specs=[by_seq(grad_middle.shape), pl.BlockSpec((1, D, D), lambda s, *unused: (3, 0, 0))]
            + [whole(a) for a in (projt, cosine, sine)]
            + [by_seq(a.shape) for a in kept]
            + [ANYWHERE] * len(after),
            out_specs=[by_seq_second(blocked)] * 3,
        ),
        out_shape=[jax.ShapeDtypeStruct(blocked, jnp.bfloat16)] * 3,
        compiler_params=pltpu.CompilerParams(vmem_limit_bytes=LIMIT),
        cost_estimate=estimate(seqs * rows * D * D * 8, 40e6),
        name="attend_back",
    )(lengths, grad_middle, weights, projt, cosine, sine, *kept, *after)


def input_back(x, grad_middle, grads, weights, vectors, after):
    seqs, rows, unused_width = x.shape
    return pl.pallas_call(
        skipping(input_back_kernel, 4 + len(grads), len(after)),
        grid=(seqs,),
        in_specs=[by_seq(x.shape), by_seq(x.shape)] + [by_seq_second(a.shape) for a in grads] + [whole(weights), whole(vectors)] + [ANYWHERE] * len(after),
        out_specs=[by_seq(x.shape), pl.BlockSpec((8, D), lambda s: (0, 0))],
        out_shape=[jax.ShapeDtypeStruct(x.shape, jnp.float32), jax.ShapeDtypeStruct((8, D), jnp.float32)],
        compiler_params=pltpu.CompilerParams(vmem_limit_bytes=LIMIT),
        cost_estimate=estimate(seqs * rows * D * D * 6, 15e6),
        name="input_back",
    )(x, grad_middle, *grads, weights, vectors, *after)


def attn_weights(me, h1, mixed, grads, wide_size, side, after):
    narrow_size, seqs, rows, width = grads[0].shape
    tokens = seqs * rows
    flat = [a.reshape(narrow_size, tokens, width) for a in grads]
    h1, mixed = h1.reshape(tokens, D), mixed.reshape(tokens, D)
    count = min(4, wide_size // 2) if side else 1
    shape = (narrow_size // 2, wide_size // count, 2 * D // wide_size, 2 * width)

    def block_at(i, me_ref):
        return (2 * i + ((me_ref[1] & 1) ^ side), 0, 0)

    return pl.pallas_call(
        skipping(attn_weight_kernel, 7, len(after)),
        grid_spec=pltpu.PrefetchScalarGridSpec(
            num_scalar_prefetch=1,
            grid=(narrow_size // 2,),
            in_specs=[whole(h1), whole(mixed)] + [pl.BlockSpec((None, tokens, width), block_at)] * 4 + [ANYWHERE] * len(after),
            out_specs=[pl.BlockSpec((1,) + shape[1:], lambda i, *unused: (i, 0, 0, 0))] * count,
        ),
        out_shape=[jax.ShapeDtypeStruct(shape, jnp.bfloat16)] * count,
        compiler_params=pltpu.CompilerParams(vmem_limit_bytes=LIMIT),
        cost_estimate=estimate(tokens * D * D * 4, 8e6),
        name="attn_weights",
    )(me, h1, mixed, *flat, *after)


def ffn_tile(tile, h2, og, w_in, w_back, bias, me, past, wide_size, narrow_size, blocks, after):
    seqs, rows, unused_width = h2.shape
    width = w_in.shape[2]
    step = 512 if width % 512 == 0 else width
    tokens = jax.ShapeDtypeStruct(h2.shape, jnp.float32)
    out_specs = [whole(h2), whole(h2), pl.BlockSpec((1, step), lambda i: (0, i))]
    out_shape = [tokens, tokens, jax.ShapeDtypeStruct((1, width), jnp.float32)]
    scratch = [pltpu.VMEM((seqs * rows, step), jnp.bfloat16)] * 2
    if blocks:
        block = (2 * D // wide_size, width // narrow_size)
        half = jax.ShapeDtypeStruct((narrow_size // 2, wide_size) + block, jnp.bfloat16)
        part = jax.ShapeDtypeStruct((narrow_size // 2, wide_size // 4) + block, jnp.bfloat16)
        out_specs += [whole(half)] + [whole(part)] * 4
        out_shape += [half] + [part] * 4
        scratch.append(pltpu.VMEM((narrow_size, wide_size) + block, jnp.bfloat16))
    else:
        out_specs.append(pl.BlockSpec((2, D, step), lambda i: (0, 0, i)))
        out_shape.append(jax.ShapeDtypeStruct((2, D, width), jnp.bfloat16))
    return pl.pallas_call(
        skipping(partial(ffn_kernel, past is not None, blocks), 6 + len(past or ()), len(after)),
        grid=(width // step,),
        in_specs=[
            whole(h2),
            whole(og),
            pl.BlockSpec((None, D, step), lambda i: (tile, 0, i)),
            pl.BlockSpec((None, step, D), lambda i: (tile, i, 0)),
            pl.BlockSpec((None, 1, step), lambda i: (0, 0, i)),
            pl.BlockSpec(memory_space=pltpu.SMEM),
        ]
        + [whole(a) for a in past or ()]
        + [ANYWHERE] * len(after),
        out_specs=out_specs,
        out_shape=out_shape,
        scratch_shapes=scratch,
        compiler_params=pltpu.CompilerParams(vmem_limit_bytes=LIMIT),
        cost_estimate=estimate(seqs * rows * D * width * 12, 20e6, seqs * rows * width * 2),
        name="ffn_tile",
    )(h2, og, w_in, w_back, bias, me, *(past or ()), *after)


def rotary_blocks(length):
    half = HDIM // 2
    frequency = jnp.exp(jnp.arange(half, dtype=jnp.float32) * (-2.0 * math.log(10000.0) / HDIM))
    angles = jnp.arange(length, dtype=jnp.float32)[:, None] * frequency[None, :]
    cosine, sine = jnp.cos(angles), jnp.sin(angles)
    return jnp.tile(cosine, (1, 4)), jnp.tile(jnp.concatenate([-sine, sine], axis=1), (1, 2))


def projection_blocks(feature_proj):
    rows = jnp.arange(GF)[:, None] // FEAT
    columns = jnp.arange(GE)[None, :] // HDIM
    mask = (rows == columns).astype(jnp.float32)
    tall = jnp.tile(feature_proj.reshape(GROUPS, GF, HDIM), (1, 1, GROUP)) * mask
    high, low = halves(tall)
    square = jnp.broadcast_to(-0.5 * mask, tall.shape).astype(jnp.bfloat16)
    turned = [a.swapaxes(1, 2) for a in (high, high, low, square, square)]
    return jnp.concatenate(turned, axis=1), jnp.concatenate([high, high, low], axis=1)


def xor_pairs(size, mask):
    return [(index, index ^ mask) for index in range(size)]


def tie(value, *earlier):
    return lax.optimization_barrier((value, earlier))[0]


def swap(value, axis_name, mask):
    return lax.ppermute(value, axis_name, xor_pairs(lax.axis_size(axis_name), mask))


def far_masks(axis_name):
    return [2 * m for m in range(1, lax.axis_size(axis_name) // 2)]


class Gather:
    def __init__(self, pieces, cut):
        self.cut = cut
        self.pieces = pieces

    def near(self, *earlier):
        self.pieces = [tie(piece, *earlier) for piece in self.pieces] if earlier else self.pieces
        self.first = jnp.stack([piece[..., : -self.cut, :] for piece in self.pieces])
        self.second = jnp.stack([piece[..., -self.cut :, :] for piece in self.pieces])
        self.first_in = swap(self.first, "wide", 1)
        self.second_in = [swap(self.second, "narrow", mask) for mask in far_masks("narrow")]
        return [self.first_in] + self.second_in

    def far(self, *earlier):
        if earlier:
            self.first_in = tie(self.first_in, *earlier)
        self.first = jnp.stack([self.first, self.first_in])
        self.extra = self.first[..., self.cut :, :]
        self.first = self.first[..., : self.cut, :]
        self.second = jnp.stack([self.second] + (list(tie(tuple(self.second_in), *earlier)) if earlier else self.second_in))
        self.first_in = [swap(self.first, "narrow", mask) for mask in far_masks("narrow")]
        self.second_in = swap(self.second, "wide", 1)
        return self.first_in + [self.second_in]

    def core(self):
        self.mine = [self.first] + self.first_in + [self.second, self.second_in]
        self.theirs = [swap(part, "narrow", 1) for part in self.mine]
        return self.theirs


def far_wide(piece):
    return [piece] + [swap(piece, "wide", mask) for mask in far_masks("wide")]


def gathered_at(part, index, side, fars, ms):
    m, index = index % ms, index // ms
    half, near, far = (0, index, part) if part < fars else (1, part - fars, index)
    return half, 2 * m + near, 2 * far + side


def place_kernel(copies, fars, ms, me_ref, *rest):
    count = 2 * (fars + 2)
    refs, outs, sems = rest[:count], rest[count:-1], rest[-1]
    started = []
    for k, ref in enumerate(refs):
        side, part = divmod(k, count // 2)
        for index in range(ref.shape[0] * ms):
            half, wide_mask, narrow_mask = gathered_at(part, index, side, fars, ms)
            wide, narrow = me_ref[0] ^ wide_mask, me_ref[1] ^ narrow_mask
            for source, target in copies(ref.at[index // ms, index % ms], outs, half, wide, narrow):
                copy = pltpu.make_async_copy(source, target, sems.at[len(started)])
                copy.start()
                started.append(copy)
    for copy in started:
        copy.wait()


def place(me, parts, copies, shapes, each, name):
    fars, ms = lax.axis_size("narrow") // 2, lax.axis_size("wide") // 2
    return pl.pallas_call(
        partial(place_kernel, copies, fars, ms),
        out_shape=[jax.ShapeDtypeStruct(shape, parts[0].dtype) for shape in shapes],
        in_specs=[pl.BlockSpec(memory_space=pltpu.SMEM)] + [ANYWHERE] * len(parts),
        out_specs=[pl.BlockSpec(memory_space=pltpu.VMEM)] * len(shapes),
        compiler_params=pltpu.CompilerParams(vmem_limit_bytes=LIMIT),
        scratch_shapes=[pltpu.SemaphoreType.DMA((4 * fars * ms * (1 + each),))],
        cost_estimate=estimate(0, 4 * sum(math.prod(shape) for shape in shapes)),
        name=name,
    )(me, *parts)


def in_order(parts, wide_size, narrow_size, place_of):
    my_wide, my_narrow = lax.axis_index("wide"), lax.axis_index("narrow")
    ordered = [
        pick(parts, place_of(w ^ my_wide, n ^ my_narrow), 0) for w in range(wide_size) for n in range(narrow_size)
    ]
    return jnp.stack(ordered).reshape((wide_size, narrow_size) + parts.shape[1:])


def half_in_order(parts, half):
    wide_size, narrow_size = lax.axis_size("wide"), lax.axis_size("narrow")
    fars, ms = narrow_size // 2, wide_size // 2

    def place_of(wide_mask, narrow_mask):
        near, m, side, far = wide_mask & 1, wide_mask >> 1, narrow_mask & 1, narrow_mask >> 1
        outer = far * 2 + near if half == 0 else near * fars + far
        return side * (fars * 2 * ms) + outer * ms + m

    count = len(parts) // 2
    found = []
    for side in range(2):
        own = parts[side * count : (side + 1) * count]
        found += own[:fars] if half == 0 else own[fars:]
    found = [part.reshape((-1,) + part.shape[2:]) for part in found]
    return in_order(jnp.concatenate(found), wide_size, narrow_size, place_of)


def pick(value, index, axis):
    return lax.dynamic_index_in_dim(value, index, axis, keepdims=False)


def core_swap(send):
    return [swap(part, "narrow", 1) for part in send]


def cut_wide(send):
    count = min(4, send.shape[1] // 2)
    width = send.shape[1] // count
    return [lax.slice_in_dim(send, width * k, width * (k + 1), axis=1) for k in range(count)]


class Stream:
    def __init__(self, keep, arrived, order, window=None):
        rest = keep.shape[2:]
        self.quarters, self.wide = len(arrived), keep.shape[1]
        self.window = window or (0, rest[0])
        self.rest = (self.window[1] - self.window[0],) + rest[1:]
        self.order = list(order)
        self.dims = {"y": keep.shape[0], "z": keep.shape[1] // 2, "x": 2}
        self.parts = [part.reshape((1, -1) + rest) for part in [keep] + arrived]

    def plan(self):
        by_all = self.order[0] == "a"
        axis = "z" if by_all else self.order[0]
        names = [name for name in ("y", "z", "x") if name in self.dims]
        sizes = [self.dims[name] for name in names]
        cut = names.index(axis)
        stride = math.prod(sizes[cut + 1 :])
        places = [
            outer * sizes[cut] * stride + inner for outer in range(math.prod(sizes[:cut])) for inner in range(stride)
        ]
        return by_all, axis, sizes[cut], stride, places

    def outputs(self):
        by_all, unused_axis, size, unused_stride, places = self.plan()
        shape = (len(places),) + self.rest
        return [(size,) + shape] if by_all else [(1,) + shape] * size

    def sent(self, pieces):
        axis = self.order.pop(0)
        self.quarters = 0
        del self.dims["z" if axis == "a" else axis]
        self.window = (0, self.rest[0])
        if axis == "a":
            groups = [list(range(near, lax.axis_size("wide"), 2)) for near in range(2)]
            self.parts = [lax.all_to_all(pieces[0], "wide", 0, 0, axis_index_groups=groups)]
        else:
            name, scale = ("narrow", 2) if axis == "y" else ("wide", 1 if axis == "x" else 2)
            self.parts = [pieces[0]] + [swap(piece, name, scale * m) for m, piece in enumerate(pieces) if m]

    def last(self):
        return [part.reshape((-1,) + self.rest) for part in self.parts]


def fold_kernel(plans, counts, windows, quarters, me_ref, *refs):
    for (by_all, axis, size, stride, places), count, (low, high), parts in zip(plans, counts, windows, quarters):
        ins, refs = take(refs, count)
        outs, refs = take(refs, 1 if by_all else size)
        here = me_ref[1] >> 1 if axis == "y" else me_ref[0] & 1 if axis == "x" else me_ref[0] >> 1
        for step in range(size):
            at = step * stride if by_all else (here ^ step) * stride
            for k, base in enumerate(places):
                found = [(ref, source, base + at) for ref in (ins[:1] if parts else ins) for source in range(ref.shape[0])]
                if parts:
                    wide = parts[1]
                    width = wide // parts[0]
                    far, left = (here ^ step, base) if axis == "y" else (base // wide, base % wide)
                    inner = left % width if axis == "y" else left % width + at
                    found.append((ins[1 + left // width], 0, far * width + inner))
                total = sum(ref[source, place, low:high].astype(jnp.float32) for ref, source, place in found)
                out = outs[0].at[step, k] if by_all else outs[step].at[0, k]
                out[...] = total.astype(out.dtype)


def interleaved(kernel, before, extra, out_counts, counts):
    def run(*refs):
        ins, outs = refs[1:before], refs[before + extra :]
        turn = []
        for out_count, count in zip(out_counts, counts):
            part, ins = take(ins, count)
            turn += part
            part, outs = take(outs, out_count)
            turn += part
        return kernel(refs[0], *turn)

    return run


def fold_streams(streams, me, after):
    plans = [stream.plan() for stream in streams]
    counts = [len(stream.parts) for stream in streams]
    windows = [stream.window for stream in streams]
    out_shapes = [
        [jax.ShapeDtypeStruct(shape, stream.parts[0].dtype) for shape in stream.outputs()] for stream in streams
    ]
    operands = sum((stream.parts for stream in streams), [])
    quarters = [(stream.quarters, stream.wide) if stream.quarters else None for stream in streams]
    kernel = partial(fold_kernel, plans, counts, windows, quarters)
    found = pl.pallas_call(
        interleaved(kernel, 1 + len(operands), len(after), [len(shapes) for shapes in out_shapes], counts),
        in_specs=[pl.BlockSpec(memory_space=pltpu.SMEM)] + [whole_plain(a) for a in operands] + [ANYWHERE] * len(after),
        out_shape=sum(out_shapes, []),
        compiler_params=pltpu.CompilerParams(vmem_limit_bytes=LIMIT),
        cost_estimate=estimate(1e6, 6e6),
        name="fold",
    )(me, *operands, *after)
    token = found[0]
    for stream, shapes in zip(streams, out_shapes):
        part, found = take(found, len(shapes))
        stream.sent(part)
    return token


def narrow_sum(value):
    mask = 1
    while mask < lax.axis_size("narrow"):
        value = value + swap(value, "narrow", mask)
        mask *= 2
    return value


def exact(left, right, dims=(((1,), (0,)), ((), ()))):
    return lax.dot_general(left, right, dims, precision=PRECISE, preferred_element_type=jnp.float32)


def diagonal_of(shape):
    return lax.broadcasted_iota(jnp.int32, shape, 0) == lax.broadcasted_iota(jnp.int32, shape, 1)


def ortho_scale(gram_mat):
    square_sum = jnp.where(diagonal_of(gram_mat.shape), gram_mat, 0.0)
    square_sum = jnp.sum(jnp.sum(square_sum, axis=1, keepdims=True), axis=0, keepdims=True)
    return 1.0 / (jnp.sqrt(square_sum) + ORTHO_EPS)


def sweeps(grams, factors, count, last):
    for left in reversed(range(count)):
        polys = [CUBIC_COEF * gram + QUINTIC_COEF * exact(gram, gram) for gram in grams]
        polys = [jnp.where(diagonal_of(poly.shape), poly + LINEAR_COEF, poly) for poly in polys]
        factors = polys if factors is None else [exact(poly, factor) for poly, factor in zip(polys, factors)]
        if left or not last:
            grams = [exact(poly, gram) for poly, gram in zip(polys, grams)]
            grams = [exact(poly, gram) for poly, gram in zip(polys, grams)]
    return grams, factors


def ortho_start(grams):
    scales = [ortho_scale(gram) for gram in grams]
    return [gram * scale * scale for gram, scale in zip(grams, scales)], scales


def block_pairs(count):
    return [(row, column) for row in range(count) for column in range(row + 1)]


def packed_blocks(small, large, out_ref):
    size = out_ref.shape[1]
    pairs = block_pairs(large.shape[0] // size)
    for k, (row, column) in enumerate(pairs):
        out_ref[k] = large[size * row : size * (row + 1), size * column : size * (column + 1)]
    rows = small.shape[0]
    out_ref[len(pairs)] = jnp.zeros(out_ref.shape[1:], jnp.float32)
    out_ref[len(pairs), :rows, :rows] = small


def unpacked_blocks(blocks, rows, count):
    pairs = block_pairs(count)
    found = {}
    for k, (row, column) in enumerate(pairs):
        found[row, column] = blocks[k]
        if row != column:
            found[column, row] = blocks[k].T
    large = [jnp.concatenate([found[row, column] for column in range(count)], axis=1) for row in range(count)]
    return blocks[len(pairs)][:rows, :rows], jnp.concatenate(large, axis=0)


def sweep_kernel(count, rows, blocks_ref, small_ref, large_ref, small_factor_ref, large_factor_ref):
    size = blocks_ref.shape[1]
    grams = unpacked_blocks(blocks_ref[...], rows, large_ref.shape[0] // size)
    grams, scales = ortho_start(grams)
    grams, factors = sweeps(grams, None, count, False)
    for gram, factor, scale, gram_ref, factor_ref in zip(
        grams, factors, scales, (small_ref, large_ref), (small_factor_ref, large_factor_ref)
    ):
        gram_ref[...] = gram
        factor_ref[...] = factor * scale


def moment_step(gradient, moment_ref, grad_ref, new_ref, at=()):
    grad_ref[at + (slice(None), slice(None))] = gradient
    moment = MOMENT_DECAY * moment_ref[at + (slice(None), slice(None))] + gradient
    new_ref[at + (slice(None), slice(None))] = moment
    return exact(moment, moment, (((1,), (1,)), ((), ())))


def sum_of(refs):
    return sum(ref[k].astype(jnp.float32) for ref in refs for k in range(ref.shape[0]))


def take(refs, count):
    return refs[:count], refs[count:]


def attn_moment_kernel(counts, mqkv_ref, mout_ref, *refs):
    left, refs = take(refs, counts[0])
    right, refs = take(refs, counts[1])
    gqkv_ref, gout_ref, nqkv_ref, nout_ref, gram_ref = refs
    left, right = sum_of(left), sum_of(right)
    width = mout_ref.shape[1]
    gram_ref[0] = moment_step(left[:, :width], mqkv_ref, gqkv_ref, nqkv_ref, (0,))
    gram_ref[1] = moment_step(left[:, width:], mqkv_ref, gqkv_ref, nqkv_ref, (1,))
    gram_ref[2] = moment_step(right[:, :width], mqkv_ref, gqkv_ref, nqkv_ref, (2,))
    gram_ref[3] = moment_step(right[:, width:], mout_ref, gout_ref, nout_ref)


def ffn_moment_kernel(counts, unit, min_ref, mback_ref, *refs):
    found = []
    for count in counts:
        part, refs = take(refs, count)
        found.append(sum_of(part))
    gin_ref, gback_ref, nin_ref, nback_ref, blocks_ref = refs
    rows = min_ref.shape[0]
    if len(found) * 128 == mback_ref.shape[0]:
        grad_in = [part[:rows] for part in found]
        turned = [jnp.concatenate([part[rows:, :128], part[rows:, 128:]], axis=0) for part in found]
        turned = jnp.concatenate(turned, axis=1)
    else:
        grad_in, turned = [found[0]], found[1]
    pieces = [part[:, at : at + unit] for at in range(0, grad_in[0].shape[1], unit) for part in grad_in]
    small = moment_step(jnp.concatenate(pieces, axis=1), min_ref, gin_ref, nin_ref)
    packed_blocks(small, moment_step(turned.T, mback_ref, gback_ref, nback_ref), blocks_ref)


def attn_ortho_kernel(rates, gram_ref, nqkv_ref, nout_ref, wqkv_ref, wout_ref, vqkv_ref, vout_ref):
    grams, scales = ortho_start([gram_ref[j] for j in range(4)])
    factors = sweeps(grams, None, NS_ITERS, True)[1]
    for j in range(4):
        factor = factors[j] * scales[j]
        if j < 3:
            ortho = exact(factor, nqkv_ref[j])
            vqkv_ref[j] = wqkv_ref[j] * (1.0 - rates[0] * WEIGHT_DECAY) - rates[0] * ortho
        else:
            ortho = exact(factor, nout_ref[...])
            vout_ref[...] = wout_ref[...] * (1.0 - rates[1] * WEIGHT_DECAY) - rates[1] * ortho


def ffn_ortho_kernel(
    rates, count, gin_ref, gback_ref, fin_ref, fback_ref, nin_ref, nback_ref, win_ref, wback_ref, vin_ref, vback_ref
):
    grams, factors = [gin_ref[...], gback_ref[...]], [fin_ref[...], fback_ref[...]]
    factors = sweeps(grams, factors, count, True)[1]
    for rate, factor, new_ref, old_ref, out_ref in (
        (rates[0], factors[0], nin_ref, win_ref, vin_ref),
        (rates[1], factors[1], nback_ref, wback_ref, vback_ref),
    ):
        ortho = exact(factor, new_ref[...])
        out_ref[...] = old_ref[...] * (1.0 - rate * WEIGHT_DECAY) - rate * ortho


def simple_call(kernel, args, shapes, name, flops, after=()):
    def run(*refs):
        kernel(*refs[: len(args)], *refs[len(args) + len(after) :])

    return pl.pallas_call(
        run,
        in_specs=[whole_plain(a) for a in args] + [pl.BlockSpec(memory_space=pl.ANY)] * len(after),
        out_shape=[jax.ShapeDtypeStruct(shape, jnp.float32) for shape in shapes],
        compiler_params=pltpu.CompilerParams(vmem_limit_bytes=LIMIT),
        cost_estimate=estimate(flops, 4e6),
        name=name,
    )(*args, *after)


def whole_plain(unused_array):
    return pl.BlockSpec(memory_space=pltpu.VMEM)


def adam_update(param, earlier_first, earlier_second, gradient):
    first_new = FIRST_DECAY * earlier_first + (1.0 - FIRST_DECAY) * gradient
    second_new = SECOND_DECAY * earlier_second + (1.0 - SECOND_DECAY) * gradient * gradient
    first_fix = 1.0 - FIRST_DECAY**ADAM_STEP
    second_fix = 1.0 - SECOND_DECAY**ADAM_STEP
    direction = first_new / first_fix / (jnp.sqrt(second_new / second_fix) + ADAM_EPS)
    return (first_new, second_new, param - VECTOR_RATE * (direction + WEIGHT_DECAY * param))


def per_device(
    block_in,
    out_grad,
    lengths,
    feature_proj,
    attn_in,
    attn_out,
    ffn_in,
    ffn_out,
    norm_params,
    bias_in,
    bias_out,
    mom_attn_in,
    mom_attn_out,
    mom_ffn_in,
    mom_ffn_out,
    first_norms,
    first_bias_in,
    first_bias_out,
    second_norms,
    second_bias_in,
    second_bias_out,
):
    seqs, length, unused_width = block_in.shape
    wide_size, narrow_size = lax.axis_size("wide"), lax.axis_size("narrow")
    column = lax.axis_index("narrow")
    own_rows, own_cols = D // wide_size, D // narrow_size
    ffn_rows = FF // wide_size
    tiles = ffn_rows // 128 if ffn_rows % 128 == 0 else 1
    unit = ffn_rows // tiles
    width = unit * wide_size
    copied = narrow_size == 4 and own_rows % 16 == 0 and unit % 32 == 0 and (width // narrow_size) % 128 == 0
    blocks = unit == 128 and width // narrow_size == 256 and own_cols == 2 * own_rows
    bf = jnp.bfloat16

    me = jnp.stack([lax.axis_index("wide"), column]).astype(jnp.int32)

    small = jnp.concatenate([norm_params.reshape(-1), bias_in, bias_out]).astype(bf)
    small_size = small.shape[0]
    part = 4 * D // narrow_size
    four = jnp.concatenate([attn_in.astype(bf), attn_out.astype(bf)[None]])
    if part == D:
        four = pick(four, column, 0)
    else:
        four = lax.dynamic_slice_in_dim(four.transpose(1, 0, 2).reshape(own_rows, 4 * D), column * part, part, 1)
    small = jnp.pad(small, (0, -small_size % (8 * part))).reshape(-1, part)
    split = own_rows // 2
    four_gather = Gather(far_wide(jnp.concatenate([four[:split], small, four[split:]])), split)

    in_part = width // narrow_size
    back_part = unit // narrow_size
    folds = D // in_part
    low_in = ffn_in.astype(bf).reshape(own_rows, wide_size, tiles, unit).transpose(2, 0, 1, 3).reshape(tiles, own_rows, width)
    low_in = lax.dynamic_slice_in_dim(low_in, column * in_part, in_part, 2)
    low_back = lax.dynamic_slice_in_dim(ffn_out.reshape(tiles, unit, D), column * back_part, back_part, 1).astype(bf)
    low_back = low_back.reshape(tiles, back_part, folds, in_part).transpose(0, 2, 1, 3).reshape(tiles, own_rows, in_part)
    low_ffn = jnp.concatenate([low_in, low_back], axis=1)
    four_in = four_gather.near()
    ffn_gathers = [Gather(far_wide(tie(low_ffn[:1], *four_gather.pieces[1:])), own_rows)]
    four_far = four_gather.far(*ffn_gathers[0].pieces[1:])
    if tiles > 1:
        ffn_gathers.append(Gather(far_wide(tie(low_ffn[1:], *four_in)), own_rows))
    four_gather.core()
    ready = ffn_gathers[0].near(*four_far)
    for gather in ffn_gathers[1:]:
        ready += gather.pieces[1:]
    four_parts = four_gather.mine + list(tie(tuple(four_gather.theirs), *ready))
    ready = ffn_gathers[0].far(*four_gather.theirs)
    ms = wide_size // 2
    small_all = in_order(
        four_gather.extra.reshape((-1,) + small.shape), wide_size, 1, lambda w, n: (w & 1) * ms + (w >> 1)
    )
    small_all = small_all.reshape(wide_size, -1)[:, :small_size].astype(jnp.float32)
    norm_all = small_all[:, : 4 * own_rows].reshape(wide_size, 4, own_rows).transpose(1, 0, 2).reshape(4, D)
    bias_in_all = small_all[:, 4 * own_rows : 4 * own_rows + ffn_rows].reshape(wide_size, tiles, unit)
    bias_in_all = bias_in_all.transpose(1, 0, 2).reshape(tiles, 1, width)
    bias_out_all = small_all[:, 4 * own_rows + ffn_rows :].reshape(1, D)
    vectors = jnp.concatenate([norm_all, bias_out_all, jnp.zeros((3, D), jnp.float32)])

    def four_copies(piece, outs, half, w, n):
        return [(piece, outs[0].at[n, pl.ds(w * own_rows + half * split, split)])]

    def ffn_copies(piece, outs, half, w, n):
        if half == 0:
            return [(piece, outs[0].at[:, pl.ds(w * own_rows, own_rows), pl.ds(n * in_part, in_part)])]
        rows = pl.ds(w * unit + n * back_part, back_part)
        return [
            (piece.at[:, pl.ds(k * back_part, back_part)], outs[1].at[:, rows, pl.ds(k * in_part, in_part)])
            for k in range(folds)
        ]

    def ffn_weights(gather):
        parts = gather.mine + gather.theirs
        count = parts[0].shape[2]
        if copied:
            return place(me, parts, ffn_copies, [(count, D, width), (count, width, D)], folds, "place_ffn")
        w_in = half_in_order(parts, 0).transpose(2, 0, 3, 1, 4).reshape(count, D, width)
        w_back = half_in_order(parts, 1).reshape(wide_size, narrow_size, count, folds, back_part, in_part)
        return w_in, w_back.transpose(2, 0, 1, 4, 3, 5).reshape(count, width, D)

    if copied:
        (weights,) = place(me, four_parts, four_copies, [(4, D, D)], 1, "place_four")
    else:
        weights = jnp.stack([half_in_order(four_parts, half) for half in range(2)], axis=2)
        weights = weights.transpose(0, 2, 3, 1, 4).reshape(D, 4, D).transpose(1, 0, 2)

    cosine, sine = rotary_blocks(length)
    proj, projt = projection_blocks(feature_proj)
    found = attend(lengths, block_in, weights, vectors, proj, cosine, sine, None, ready)
    half_done = found[0]
    early = list(ffn_gathers[0].core())
    for gather in ffn_gathers[1:]:
        early += gather.near(*ready)
    found = attend(lengths, block_in, weights, vectors, proj, cosine, sine, found, early)
    middle, h1, h2, *kept, mixed = found
    tile_weights = [ffn_weights(ffn_gathers[0])]
    later = []
    for gather in ffn_gathers[1:]:
        later += gather.far(half_done)
        gather.core()
        tile_weights.append(ffn_weights(gather))
    past, token = None, later
    streams, bias_sums = [], []
    orders = ["yzx", "yxz", "xya"]
    for tile in range(tiles):
        ffn, grad_h2, bias_sum, *grad_tile = ffn_tile(
            max(tile - 1, 0), h2, out_grad, *tile_weights[min(tile, 1)], bias_in_all[tile : tile + 1], me, past, wide_size, narrow_size, blocks, token
        )
        past = (ffn, grad_h2)
        bias_sums.append(bias_sum)
        token = [fold_streams(streams[:1], me, [bias_sum])] if tile == 1 else []
        if blocks:
            keep, *send = grad_tile
            streams.append(Stream(keep, core_swap(send), orders[tile % 3]))
        else:
            grad_in = grad_tile[0][0].reshape(wide_size, own_rows, narrow_size, in_part).transpose(2, 0, 1, 3)
            grad_back = grad_tile[0][1].reshape(narrow_size, own_cols, wide_size, unit).transpose(0, 2, 1, 3)
            for found, order in ((grad_in, "yxz"), (grad_back, "xyz")):
                found = found.reshape((narrow_size // 2, 2) + found.shape[1:])
                arrived = core_swap(cut_wide(pick(found, 1 - (column & 1), 1)))
                streams.append(Stream(pick(found, column & 1, 1), arrived, order))
    ffn = tie(ffn, *streams[0].parts[1:])
    block_out, grad_middle, gb, sums_two = middle_back(out_grad, grad_h2, ffn, middle, vectors, narrow_size)

    def fold_open(more, after):
        found = more + [stream for stream in streams if stream.order]
        done = [part for stream in streams if not stream.order for part in stream.parts]
        return fold_streams(found, me, after + done)

    token = fold_open([], [sums_two])
    gq, gk, gv = attend_back(lengths, grad_middle, weights, projt, cosine, sine, kept, narrow_size, [token])
    token = fold_open([], [gq])
    send = attn_weights(me, h1, mixed, (gq, gk, gv, gb), wide_size, 1, [token])
    (keep,) = attn_weights(me, h1, mixed, (gq, gk, gv, gb), wide_size, 0, send[:1])
    arrived = core_swap(send)
    left = Stream(keep, arrived, "xzy", (0, own_rows))
    right = Stream(keep, arrived, "yxz", (own_rows, 2 * own_rows))
    token = fold_open([left, right], [keep])
    input_grad, sums_one = input_back(block_in, grad_middle, (gq, gk, gv), weights, vectors, [token])

    norm_sums = jnp.concatenate([sums_one[:2], sums_two[:2], sums_two[2:3]])
    inner_sums = jnp.concatenate(bias_sums).reshape(tiles, wide_size, unit).transpose(1, 0, 2)
    inner_sums = inner_sums.reshape(wide_size, narrow_size, ffn_rows // narrow_size)
    norm_part = own_rows // narrow_size
    norm_sums = norm_sums.reshape(5, wide_size, narrow_size, norm_part).transpose(1, 2, 0, 3).reshape(wide_size, narrow_size, -1)
    vector_parts = jnp.concatenate([norm_sums, inner_sums], axis=2).swapaxes(0, 1)
    vector_size = vector_parts.shape[2]
    vector_parts = jnp.pad(vector_parts, ((0, 0), (0, 0), (0, -vector_size % 128)))
    vector_parts = vector_parts.reshape(narrow_size // 2, 2, wide_size, 1, -1)
    vector_send = pick(vector_parts, 1 - (column & 1), 1)
    vector = Stream(pick(vector_parts, column & 1, 1), core_swap([vector_send]), "yxz")
    token = fold_open([left, right, vector], [sums_one])
    ffn_parts = [stream.last() for stream in streams]
    block_size = 128 if ffn_rows % 128 == 0 else ffn_rows
    block_count = len(block_pairs(ffn_rows // block_size)) + 1
    grad_in_w, grad_back_w, mom_in_new, mom_back_new, blocks_gram = simple_call(
        partial(ffn_moment_kernel, [len(parts) for parts in ffn_parts], unit),
        [mom_ffn_in, mom_ffn_out] + sum(ffn_parts, []),
        [mom_ffn_in.shape, mom_ffn_out.shape] * 2 + [(block_count, block_size, block_size)],
        "ffn_moment",
        1e9,
        [token],
    )
    blocks_gram = narrow_sum(blocks_gram)
    token = fold_streams([left, right, vector], me, [mom_in_new])
    sweep_in, sweep_back, factor_in, factor_back = simple_call(
        partial(sweep_kernel, 2, own_rows),
        [blocks_gram],
        [(own_rows, own_rows), (ffn_rows, ffn_rows)] * 2,
        "ffn_sweeps",
        1e10,
        [token],
    )
    left_parts, right_parts = left.last(), right.last()
    def own_columns(weight):
        block_width = weight.shape[-1] // narrow_size
        return lax.dynamic_slice_in_dim(
            weight, column * block_width, block_width, axis=weight.ndim - 1
        )

    rate_qkv = MUON_SCALE
    rate_out = MUON_SCALE * math.sqrt(D / (D // 64))
    rate_in = MUON_SCALE * math.sqrt(FF / D)
    rate_back = MUON_SCALE * math.sqrt(D / FF)
    shapes = [mom_attn_in.shape, mom_attn_out.shape]
    grad_qkv, grad_out_w, mom_qkv_new, mom_out_new, gram_four = simple_call(
        partial(attn_moment_kernel, (len(left_parts), len(right_parts))),
        [mom_attn_in, mom_attn_out] + left_parts + right_parts,
        shapes + shapes + [(4, own_rows, own_rows)],
        "attn_moment",
        1e9,
        [sweep_in],
    )
    fold_streams([vector], me, [gram_four])
    vector_sums = sum(jnp.sum(part, axis=0) for part in vector.last())[0, :vector_size]
    grad_norm_vals = vector_sums[: 4 * norm_part].reshape(4, norm_part)
    grad_bias_final = vector_sums[4 * norm_part : 5 * norm_part]
    grad_bias_inner = vector_sums[5 * norm_part :]
    new_in, new_back = simple_call(
        partial(ffn_ortho_kernel, (rate_in, rate_back), NS_ITERS - 2),
        [sweep_in, sweep_back, factor_in, factor_back, mom_in_new, mom_back_new, own_columns(ffn_in), own_columns(ffn_out)],
        [mom_ffn_in.shape, mom_ffn_out.shape],
        "ffn_ortho",
        1e10,
        [gram_four],
    )
    new_qkv, new_out = simple_call(
        partial(attn_ortho_kernel, (rate_qkv, rate_out)),
        [narrow_sum(gram_four), mom_qkv_new, mom_out_new, own_columns(attn_in), own_columns(attn_out)],
        shapes,
        "attn_ortho",
        5e9,
        [new_in],
    )
    norm_first, norm_second, norm_new = adam_update(
        own_columns(norm_params), first_norms, second_norms, grad_norm_vals
    )
    inner_first, inner_second, inner_new = adam_update(
        own_columns(bias_in), first_bias_in, second_bias_in, grad_bias_inner
    )
    final_first, final_second, final_new = adam_update(
        own_columns(bias_out), first_bias_out, second_bias_out, grad_bias_final
    )
    return (
        block_out,
        input_grad,
        grad_qkv,
        grad_out_w,
        grad_in_w,
        grad_back_w,
        grad_norm_vals,
        grad_bias_inner,
        grad_bias_final,
        mom_qkv_new,
        mom_out_new,
        mom_in_new,
        mom_back_new,
        new_qkv,
        new_out,
        new_in,
        new_back,
        norm_first,
        inner_first,
        final_first,
        norm_second[:2],
        norm_second[2:],
        inner_second,
        final_second,
        norm_new,
        inner_new,
        final_new,
    )


def solution(mesh):
    in_specs = (
        P(("wide", "narrow"), None, None),
        P(("wide", "narrow"), None, None),
        P(("wide", "narrow")),
        P(),
        P(None, "wide", None),
        P("wide", None),
        P("wide", None),
        P("wide", None),
        P(None, "wide"),
        P("wide"),
        P("wide"),
        P(None, "wide", "narrow"),
        P("wide", "narrow"),
        P("wide", "narrow"),
        P("wide", "narrow"),
        P(None, ("wide", "narrow")),
        P(("wide", "narrow")),
        P(("wide", "narrow")),
        P(None, ("wide", "narrow")),
        P(("wide", "narrow")),
        P(("wide", "narrow")),
    )
    out_specs = (
        P(("wide", "narrow"), None, None),
        P(("wide", "narrow"), None, None),
        P(None, "wide", "narrow"),
        P("wide", "narrow"),
        P("wide", "narrow"),
        P("wide", "narrow"),
        P(None, ("wide", "narrow")),
        P(("wide", "narrow")),
        P(("wide", "narrow")),
        P(None, "wide", "narrow"),
        P("wide", "narrow"),
        P("wide", "narrow"),
        P("wide", "narrow"),
        P(None, "wide", "narrow"),
        P("wide", "narrow"),
        P("wide", "narrow"),
        P("wide", "narrow"),
        P(None, ("wide", "narrow")),
        P(("wide", "narrow")),
        P(("wide", "narrow")),
        P(None, ("wide", "narrow")),
        P(None, ("wide", "narrow")),
        P(("wide", "narrow")),
        P(("wide", "narrow")),
        P(None, ("wide", "narrow")),
        P(("wide", "narrow")),
        P(("wide", "narrow")),
    )
    return jax.shard_map(
        per_device, mesh=mesh, in_specs=in_specs, out_specs=out_specs, check_vma=False
    )
```

time: 487 us -> 438 us (0.90)
  Pallas kernels: 133 us -> 229 us
  waiting for transfers between devices: 151 us -> 68.8 us
  matrix products: 38.5 us -> 0 us
  other arithmetic: 40.1 us -> 17.5 us
  local copies, waits for them, and re-layouts: 33.5 us -> 40.9 us
  starting transfers between devices: 80.5 us -> 75.4 us
    pallas_call x10 -> x25, Pallas kernels: 133 us -> 229 us  [the longest x3 71.9 us: ffn_tile(): pl.pallas_call(skipping(partial(ffn_kernel, past is not None, blocks), 6...]
    ppermute x61 -> x81, waiting for transfers between devices: 151 us -> 68.8 us  [swap(): lax.ppermute(value, axis_name, xor_pairs(lax.axis_size(axis_name), mask))]
    dot_general x42 -> x0, matrix products: 38.5 us -> none  [the longest x38 36.6 us: bmm(): return jnp.einsum('brs,bst->brt', left, right, precision=PRECISE)]
    unnamed x85 -> x183, local copies, waits for them, and re-layouts: 2.41 us -> 15.6 us
    squeeze x24 -> x1, local copies, waits for them, and re-layouts: 12.7 us -> 0.01 us  [pick(): return lax.dynamic_index_in_dim(value, index, axis, keepdims=False)]
    convert_element_type x15 -> x1, other arithmetic: 12 us -> 0.01 us  [per_device(): small_all.reshape(wide_size, -1)[:, :small_size].astype(jnp.float32)]
    ppermute x61 -> x81, starting transfers between devices: 80.5 us -> 71.9 us  [swap(): lax.ppermute(value, axis_name, xor_pairs(lax.axis_size(axis_name), mask))]
    another operation x8 -> x13, local copies, waits for them, and re-layouts: 0.36 us -> 8.42 us  [the longest x9 5.73 us: near(): jnp.stack([piece[..., -self.cut:, :] for piece in self.pieces])]
  transfers between devices with their start and end apart: 61 -> 82, of which waited for: 27 -> 18; matrix products, arithmetic and copies ran while one was open for 16% -> 9% of each run, Pallas kernels for 23% -> 46%
where the time goes in v3:
time: 438 us; the launch traced here: 434 us
  Pallas kernels  229 us (52%)
  starting transfers between devices  75.4 us (17%)
  waiting for transfers between devices  68.8 us (16%)
  local copies, waits for them, and re-layouts  40.9 us (9%)
  other arithmetic  17.5 us (4%)
    ppermute x81, starting transfers between devices, swap(): lax.ppermute(value, axis_name, xor_pairs(lax.axis_size(axis_name), mask))  71.9 us
    pallas_call x3, Pallas kernels, ffn_tile(): pl.pallas_call(skipping(partial(ffn_kernel, past is not None, blocks), 6...  71.9 us
    ppermute x81, waiting for transfers between devices, swap(): lax.ppermute(value, axis_name, xor_pairs(lax.axis_size(axis_name), mask))  68.8 us
    pallas_call x5, Pallas kernels, simple_call(): pl.pallas_call(run, in_specs=[whole_plain(a) for a in args] + [pl.BlockSp...  39.9 us
    pallas_call x7, Pallas kernels, fold_streams(): pl.pallas_call(interleaved(kernel, 1 + len(operands), len(after), [len(sh...  25.2 us
    pallas_call x2, Pallas kernels, attend(): pl.pallas_call(skipping(partial(attend_kernel, first), 7, len(after) + le...  24 us
    pallas_call x3, Pallas kernels, place(): pl.pallas_call(partial(place_kernel, copies, fars, ms), out_shape=[jax.Sh...  18.7 us
    pallas_call x2, Pallas kernels, attn_weights(): pl.pallas_call(skipping(attn_weight_kernel, 7, len(after)), grid_spec=plt...  15.7 us
  transfers between devices with their start and end apart: 82, of which 18 were waited for; matrix products, arithmetic and copies ran while one was open for 9% of the time, Pallas kernels for 46%

profile of v3, /device:TPU:0, one launch (start us, length us, event | category | flops | bytes accessed | tf_op | source)
XLA Modules:
  0.0 434.3 jit_solution(517787076559269385)
XLA Ops:
  4.6 5.0 %collective-permute-start.2 = (bf16[104,768]{1,0:T(8,128)(2,1)}, bf16[104,768]{1,0:T(8,128)(2,1)}, u32[]{:S(2)}, u32[]{:S(2)}) collective-permute-start(bf16[104,768]{1,0:T(8,128)(2,1)} %pad_maximum_fusion.13), channel_id=1, source_target_pairs={{0,24},{4,28},{8,16},{12,20},{16,8},{20,12},{24,0},{28,4},{1,25},{... | collective-permute-start | bytes 479240 | tf_op jit(solution)/shard_map/ppermute | solution.py:539
  19.7 3.8 collective-permute-done.1
  31.3 2.5 collective-permute-start.6
  33.8 1.9 collective-permute-start.5
  36.3 2.5 collective-permute-done.6
  43.0 12.1 %collective-permute-done.9.rest_3_ = bf16[2,4,48,768]{3,2,1,0:T(8,128)(2,1)S(1)} collective-permute-done((bf16[2,4,48,768]{3,2,1,0:T(8,128)(2,1)S(1)}, bf16[2,4,48,768]{3,2,1,0:T(8,128)(2,1)S(1)}, u32[]{:S(2)}, u32[]{:S(2)}) %collective-permute-start.9) | collective-permute-done | bytes 589856 | tf_op jit(solution)/shard_map/ppermute | solution.py:539
  55.1 2.8 collective-permute-done.7.rest_1_
  60.2 2.1 collective-permute-start.18
  62.3 3.1 collective-permute-done.14
  72.7 7.1 %collective-permute-done.20 = bf16[2,4,1,96,256]{4,3,1,2,0:T(8,128)(2,1)S(1)} collective-permute-done((bf16[2,4,1,96,256]{4,3,1,2,0:T(8,128)(2,1)S(1)}, bf16[2,4,1,96,256]{4,3,1,2,0:T(8,128)(2,1)S(1)}, u32[]{:S(2)}, u32[]{:S(2)}) %collective-permute-start.20) | collective-permute-done | bytes 393248 | tf_op jit(solution)/shard_map/ppermute | solution.py:539
  88.9 5.8 %place_four.1.refs_2_.refs_5_ = bf16[4,768,768]{2,1,0:T(8,128)(2,1)} custom-call(s32[2]{0:T(128)} %pad_add_fusion.me_ref.refs_5_.refs_0_, bf16[2,4,48,768]{3,2,1,0:T(8,128)(2,1)} %copy-done.3, bf16[2,4,48,768]{3,2,1,0:T(8,128)(2,1)} %copy-done.23, bf16[2,4,48,768]{3,2,1,0:T(8,128)(2,1)} %copy-done.4, bf16[2,4,48,768]{3,2,1,0:T(8,128)(2,1)} %copy-done.21, ...), custom_call_target="tpu_custom_call" | custom-call | bytes 9437184 | tf_op jit(solution)/shard_map/place_four/pallas_call | solution.py:605
  94.7 11.9 %attend.2 = (f32[4,208,768]{2,1,0:T(8,128)}, bf16[4,208,768]{2,1,0:T(8,128)(2,1)}, bf16[4,208,768]{2,1,0:T(8,128)(2,1)}, f32[4,208,768]{2,1,0:T(8,128)}, f32[4,2...) custom-call(s32[4]{0:T(128)} %refs_0_.8, ...), custom_call_target="tpu_custom_call" | custom-call | flops 2944401408 | bytes 20000000 | tf_op jit(solution)/shard_map/attend/pallas_call | solution.py:376
  111.4 12.5 %collective-permute-done.27.rest_1_.refs_6_ = bf16[2,4,2,96,256]{4,3,2,1,0:T(8,128)(2,1)} collective-permute-done((bf16[2,4,2,96,256]{4,3,2,1,0:T(8,128)(2,1)S(1)}, bf16[2,4,2,96,256]{4,3,2,1,0:T(8,128)(2,1)}, u32[]{:S(2)}, u32[]{:S(2)}) %collective-permute-start.27) | collective-permute-done | bytes 786464 | tf_op jit(solution)/shard_map/ppermute | solution.py:539
  125.1 12.1 %attend.3 = (f32[4,208,768]{2,1,0:T(8,128)}, bf16[4,208,768]{2,1,0:T(8,128)(2,1)}, bf16[4,208,768]{2,1,0:T(8,128)(2,1)}, f32[4,208,768]{2,1,0:T(8,128)}, f32[4,2...) custom-call(s32[4]{0:T(128)} %refs_0_.8, ...), custom_call_target="tpu_custom_call", output_to_operand_aliasing={{0}: (13, {}), {1}: (14, {}), {2}: (15, {}), {3}: (16, {}),... | custom-call | flops 2944401408 | bytes 20000000 | tf_op jit(solution)/shard_map/attend/pallas_call | solution.py:376
  137.2 5.4 %place_ffn.3 = (bf16[1,768,1024]{2,1,0:T(8,128)(2,1)}, bf16[1,1024,768]{2,1,0:T(8,128)(2,1)}) custom-call(s32[2]{0:T(128)} %pad_add_fusion.me_ref.refs_5_.refs_0_, bf16[2,4,1,96,256]{4,3,2,1,0:T(8,128)(2,1)} %get-tuple-element.427.rest_0_, bf16[2,4,1,96,256]{4,3,2,1,0:T(8,128)(2,1)} %bitcast.242, bf16[2,4,1,96,256]{4,3,2,1,0:T(8,128)(2,1)} %get-tuple-element.425.rest_2_, ...), custom_call_target="tpu_custom_call" | custom-call | bytes 6291456 | tf_op jit(solution)/shard_map/place_ffn/pallas_call | solution.py:605
  142.6 19.2 %ffn_tile.3 = (f32[4,208,768]{2,1,0:T(8,128)}, f32[4,208,768]{2,1,0:T(8,128)}, f32[1,1024]{1,0:T(1,128)}, bf16[2,8,192,256]{3,2,1,0:T(8,128)(2,1)}, bf16[2,2,192...) custom-call(bf16[4,208,768]{2,1,0:T(8,128)(2,1)} %get-tuple-element., ...), custom_call_target="tpu_custom_call" | custom-call | flops 7851737088 | bytes 20000000 | tf_op jit(solution)/shard_map/ffn_tile/pallas_call | solution.py:489
  163.0 7.5 %place_ffn.2 = (bf16[2,768,1024]{2,1,0:T(8,128)(2,1)}, bf16[2,1024,768]{2,1,0:T(8,128)(2,1)}) custom-call(s32[2]{0:T(128)} %pad_add_fusion.me_ref.refs_5_.refs_0_, bf16[2,4,2,96,256]{4,3,2,1,0:T(8,128)(2,1)} %copy-done.1, bf16[2,4,2,96,256]{4,3,2,1,0:T(8,128)(2,1)} %collective-permute-done.27.rest_1_.refs_6_, bf16[2,4,2,96,256]{4,3,2,1,0:T(8,128)(2,1)} %copy-done.2, ...), custom_call_target="tpu_custom_call" | custom-call | bytes 12582912 | tf_op jit(solution)/shard_map/place_ffn/pallas_call | solution.py:605
  170.5 21.2 %ffn_tile.4 = (f32[4,208,768]{2,1,0:T(8,128)}, f32[4,208,768]{2,1,0:T(8,128)}, f32[1,1024]{1,0:T(1,128)}, bf16[2,8,192,256]{3,2,1,0:T(8,128)(2,1)}, bf16[2,2,192...) custom-call(bf16[4,208,768]{2,1,0:T(8,128)(2,1)} %get-tuple-element., ...), custom_call_target="tpu_custom_call" | custom-call | flops 7851737088 | bytes 20000000 | tf_op jit(solution)/shard_map/ffn_tile/pallas_call | solution.py:489
  192.9 3.3 fold.7
  198.0 31.4 %ffn_tile.5 = (f32[4,208,768]{2,1,0:T(8,128)}, f32[4,208,768]{2,1,0:T(8,128)}, f32[1,1024]{1,0:T(1,128)}, bf16[2,8,192,256]{3,2,1,0:T(8,128)(2,1)}, bf16[2,2,192...) custom-call(bf16[4,208,768]{2,1,0:T(8,128)(2,1)} %get-tuple-element., ...), custom_call_target="tpu_custom_call" | custom-call | flops 7851737088 | bytes 20000000 | tf_op jit(solution)/shard_map/ffn_tile/pallas_call | solution.py:489
  230.6 7.7 %middle_back.1 = (f32[4,208,768]{2,1,0:T(8,128)}, f32[4,208,768]{2,1,0:T(8,128)}, bf16[4,4,208,192]{3,2,1,0:T(8,128)(2,1)}, f32[8,768]{1,0:T(8,128)}) custom-call(bf16[4,208,768]{2,1,0:T(8,128)(2,1)} %og_ref.1, f32[4,208,768]{2,1,0:T(8,128)} %get-tuple-element.227.gh2_ref, f32[4,208,768]{2,1,0:T(8,128)} %get-tuple-element.230.ffn_ref, ...), custom_call_target="tpu_custom_call" | custom-call | flops 10000000 | bytes 16000000 | tf_op jit(solution)/shard_map/middle_back/pallas_call | solution.py:397
  239.1 6.0 %fold.8 = (bf16[1,2,192,256]{3,2,1,0:T(8,128)(2,1)}, bf16[1,2,192,256]{3,2,1,0:T(8,128)(2,1)}, bf16[1,2,192,256]{3,2,1,0:T(8,128)(2,1)}, bf16[1,2,192,256]{3,2,1...) custom-call(s32[2]{0:T(128)} %pad_add_fusion.me_ref.refs_5_.refs_0_,, ...), custom_call_target="tpu_custom_call" | custom-call | flops 1000000 | bytes 6000000 | tf_op jit(solution)/shard_map/fold/pallas_call | solution.py:744
  248.0 1.9 collective-permute-start.47
  249.9 2.0 collective-permute-start.48
  251.9 15.2 %attend_back.1 = (bf16[4,4,208,192]{3,2,1,0:T(8,128)(2,1)}, bf16[4,4,208,192]{3,2,1,0:T(8,128)(2,1)}, bf16[4,4,208,192]{3,2,1,0:T(8,128)(2,1)}) custom-call(s32[4]{0:T(128)} %refs_0_.8, f32[4,208,768]{2,1,0:T(8,128)} %get-tuple-element.233.refs_1_, bf16[4,768,768]{2,1,0:T(8,128)(2,1)} %place_four.1.refs_2_.refs_5_, ...), custom_call_target="tpu_custom_call" | custom-call | flops 3925868544 | bytes 40000000 | tf_op jit(solution)/shard_map/attend_back/pallas_call | solution.py:413
  268.5 3.6 fold.9
  274.1 7.8 %attn_weights.2 = (bf16[2,2,192,384]{3,2,1,0:T(8,128)(2,1)}, bf16[2,2,192,384]{3,2,1,0:T(8,128)(2,1)}, bf16[2,2,192,384]{3,2,1,0:T(8,128)(2,1)}, bf16[2,2,192,384]{3,2,1,0:T(8,128)(2,1)}) custom-call(s32[2]{0:T(128)} %pad_add_fusion.me_ref.refs_5_.refs_0_, bf16[832,768]{1,0:T(8,128)(2,1)} %bitcast.191, bf16[832,768]{1,0:T(8,128)(2,1)} %bitcast.193, ...), custom_call_target="tpu_custom_call" | custom-call | flops 1962934272 | bytes 8000000 | tf_op jit(solution)/shard_map/attn_weights/pallas_call | solution.py:456
  289.2 7.9 %attn_weights.3.refs_15_ = bf16[2,8,192,384]{3,2,1,0:T(8,128)(2,1)} custom-call(s32[2]{0:T(128)} %pad_add_fusion.me_ref.refs_5_.refs_0_, bf16[832,768]{1,0:T(8,128)(2,1)} %bitcast.192, bf16[832,768]{1,0:T(8,128)(2,1)} %bitcast.194, bf16[4,832,192]{2,1,0:T(8,128)(2,1)} %bitcast.186, bf16[4,832,192]{2,1,0:T(8,128)(2,1)} %bitcast.188, ...), custom_call_target="tpu_custom_call" | custom-call | flops 1962934272 | bytes 8000000 | tf_op jit(solution)/shard_map/attn_weights/pallas_call | solution.py:456
  298.5 6.3 %fold.10 = (bf16[1,8,96,384]{3,2,1,0:T(8,128)(2,1)}, bf16[1,8,96,384]{3,2,1,0:T(8,128)(2,1)}, bf16[1,8,96,384]{3,2,1,0:T(8,128)(2,1)}, bf16[1,8,96,384]{3,2,1,0:...) custom-call(s32[2]{0:T(128)} %pad_add_fusion.me_ref.refs_5_.refs_0_,, ...), custom_call_target="tpu_custom_call" | custom-call | flops 1000000 | bytes 6000000 | tf_op jit(solution)/shard_map/fold/pallas_call | solution.py:744
  307.6 3.5 all-to-all-start
  311.1 10.9 %input_back.1 = (f32[4,208,768]{2,1,0:T(8,128)}, f32[8,768]{1,0:T(8,128)}) custom-call(bf16[4,208,768]{2,1,0:T(8,128)(2,1)} %refs_0_.9, f32[4,208,768]{2,1,0:T(8,128)} %get-tuple-element.233.refs_1_, bf16[4,4,208,192]{3,2,1,0:T(8,128)(2,1)} %get-tuple-element.255.refs_9_.refs_2_, bf16[4,4,208,192]{3,2,1,0:T(8,128)(2,1)} %get-tuple-element.256.refs_3_, ...), custom_call_target="tpu_custom_call" | custom-call | flops 2944401408 | bytes 15000000 | tf_op jit(solution)/shard_map/input_back/pallas_call | solution.py:433
  323.3 2.1 collective-permute-start.61
  325.4 2.4 collective-permute-start.62
  329.8 6.5 %collective-permute-done.62.refs_12_ = bf16[1,1,192,256]{3,2,1,0:T(8,128)(2,1)S(1)} collective-permute-done((bf16[1,1,192,256]{3,2,1,0:T(8,128)(2,1)}, bf16[1,1,192,256]{3,2,1,0:T(8,128)(2,1)S(1)}, u32[]{:S(2)}, u32[]{:S(2)}) %collective-permute-start.62) | collective-permute-done | bytes 98336 | tf_op jit(solution)/shard_map/ppermute | solution.py:539
  337.6 2.7 fold.11
  340.3 3.3 ffn_moment.1
  343.6 2.0 collective-permute-done.73
  347.6 1.9 constant_dynamic-slice_fusion.4.refs_3_
  355.8 3.7 collective-permute-done.68.refs_8_
  359.5 2.4 collective-permute-start.66
  367.9 2.1 fold.12
  370.9 3.5 collective-permute-start.70
  379.3 11.2 %ffn_sweeps.1 = (f32[96,96]{1,0:T(8,128)}, f32[384,384]{1,0:T(8,128)}, f32[96,96]{1,0:T(8,128)}, f32[384,384]{1,0:T(8,128)}) custom-call(f32[7,128,128]{2,1,0:T(8,128)} %add.212.refs_0_, bf16[1,1,96,384]{3,2,1,0:T(8,128)(2,1)} %get-tuple-element.300.refs_1_), custom_call_target="tpu_custom_call" | custom-call | flops 10000000000 | bytes 4000000 | tf_op jit(solution)/shard_map/ffn_sweeps/pallas_call | solution.py:909
  391.2 2.4 attn_moment.1
  395.4 2.3 collective-permute-start.78
  399.9 16.9 %ffn_ortho.1 = (f32[96,768]{1,0:T(8,128)}, f32[384,192]{1,0:T(8,128)}) custom-call(f32[96,96]{1,0:T(8,128)} %get-tuple-element.307.refs_8_.refs_0_, f32[384,384]{1,0:T(8,128)} %get-tuple-element.322.refs_1_, f32[96,96]{1,0:T(8,128)} %get-tuple-element.323.refs_2_, f32[384,384]{1,0:T(8,128)} %get-tuple-element.324.refs_3_, ...), custom_call_target="tpu_custom_call" | custom-call | flops 10000000000 | bytes 4000000 | tf_op jit(solution)/shard_map/ffn_ortho/pallas_call | solution.py:909
  423.2 4.0 collective-permute-done.80
  427.9 6.1 %attn_ortho.1 = (f32[3,96,192]{2,1,0:T(8,128)}, f32[96,192]{1,0:T(8,128)}) custom-call(f32[4,96,96]{2,1,0:T(8,128)} %add.218.refs_0_, f32[3,96,192]{2,1,0:T(8,128)} %get-tuple-element.392.refs_1_, f32[96,192]{1,0:T(8,128)} %get-tuple-element.393.refs_2_, f32[3,96,192]{2,1,0:T(8,128)} %constant_dynamic-slice_fusion.4.refs_3_, ...), custom_call_target="tpu_custom_call" | custom-call | flops 5000000000 | bytes 4000000 | tf_op jit(solution)/shard_map/attn_ortho/pallas_call | solution.py:909
  (431 shorter events, 110.4 us)
Async XLA Ops:
  4.6 14.2 %collective-permute-start.2 = (bf16[104,768]{1,0:T(8,128)(2,1)}, bf16[104,768]{1,0:T(8,128)(2,1)}, u32[]{:S(2)}, u32[]{:S(2)}) collective-permute-start(bf16[104,768]{1,0:T(8,128)(2,1)} %pad_maximum_fusion.13), channel_id=1, source_target_pairs={{0,24},{4,28},{8,16},{12,20},{16,8},{20,12},{24,0},{28,4},{1,25},{... | collective-permute-start | bytes 479240 | tf_op jit(solution)/shard_map/ppermute | solution.py:539
  9.7 14.7 %collective-permute-start = (bf16[104,768]{1,0:T(8,128)(2,1)}, bf16[104,768]{1,0:T(8,128)(2,1)}, u32[]{:S(2)}, u32[]{:S(2)}) collective-permute-start(bf16[104,768]{1,0:T(8,128)(2,1)} %pad_maximum_fusion.13), channel_id=1, source_target_pairs={{0,8},{4,12},{8,0},{12,4},{16,24},{20,28},{24,16},{28,20},{1,9},{5... | collective-permute-start | bytes 479240 | tf_op jit(solution)/shard_map/ppermute | solution.py:539
  25.3 16.0 %collective-permute-start.8 = (bf16[4,48,768]{2,1,0:T(8,128)(2,1)S(1)}, bf16[4,48,768]{2,1,0:T(8,128)(2,1)S(1)}, u32[]{:S(2)}, u32[]{:S(2)}) collective-permute-start(bf16[4,48,768]{2,1,0:T(8,128)(2,1)S(1)} %get-tuple-element.436), channel_id=1, source_target_pairs={{0,2},{1,3},{2,0},{3,1},{4,6},{5,7},{6,4},{7,5},{8,10},{9,11},{10,... | collective-permute-start | bytes 884744 | tf_op jit(solution)/shard_map/ppermute | solution.py:539
  42.0 17.6 %collective-permute-start.12 = (bf16[2,4,48,768]{3,2,1,0:T(8,128)(2,1)S(1)}, bf16[2,4,48,768]{3,2,1,0:T(8,128)(2,1)S(1)}, u32[]{:S(2)}, u32[]{:S(2)}) collective-permute-start(bf16[2,4,48,768]{3,2,1,0:T(8,128)(2,1)S(1)} %pad_maximum_fusion.2.rest_2_), channel_id=1, source_target_pairs={{0,1},{1,0},{2,3},{3,2},{4,5},{5,4},{6,7},{7,6},{8,9},{9,8},{10,11... | collective-permute-start | bytes 1769480 | tf_op jit(solution)/shard_map/ppermute | solution.py:539
  42.1 15.8 %collective-permute-start.7 = (bf16[2,4,48,768]{3,2,1,0:T(8,128)(2,1)S(1)}, bf16[2,4,48,768]{3,2,1,0:T(8,128)(2,1)S(1)}, u32[]{:S(2)}, u32[]{:S(2)}) collective-permute-start(bf16[2,4,48,768]{3,2,1,0:T(8,128)(2,1)S(1)} %fusion.rest_0_), channel_id=1, source_target_pairs={{0,2},{1,3},{2,0},{3,1},{4,6},{5,7},{6,4},{7,5},{8,10},{9,11},{10,... | collective-permute-start | bytes 1769480 | tf_op jit(solution)/shard_map/ppermute | solution.py:539
  42.7 17.6 %collective-permute-start.10 = (bf16[2,4,48,768]{3,2,1,0:T(8,128)(2,1)S(1)}, bf16[2,4,48,768]{3,2,1,0:T(8,128)(2,1)S(1)}, u32[]{:S(2)}, u32[]{:S(2)}) collective-permute-start(bf16[2,4,48,768]{3,2,1,0:T(8,128)(2,1)S(1)} %fusion.rest_0_), channel_id=1, source_target_pairs={{0,1},{1,0},{2,3},{3,2},{4,5},{5,4},{6,7},{7,6},{8,9},{9,8},{10,11... | collective-permute-start | bytes 1769480 | tf_op jit(solution)/shard_map/ppermute | solution.py:539
  65.4 16.6 %collective-permute-start.17 = (bf16[2,192,256]{2,1,0:T(8,128)(2,1)S(1)}, bf16[2,192,256]{2,1,0:T(8,128)(2,1)}, u32[]{:S(2)}, u32[]{:S(2)}) collective-permute-start(bf16[2,192,256]{2,1,0:T(8,128)(2,1)S(1)} %pad_maximum_fusion.10), channel_id=1, source_target_pairs={{0,16},{4,20},{8,24},{12,28},{16,0},{20,4},{24,8},{28,12},{1,17},{... | collective-permute-start | bytes 589832 | tf_op jit(solution)/shard_map/ppermute | solution.py:539
  66.2 16.7 %collective-permute-start.16 = (bf16[2,192,256]{2,1,0:T(8,128)(2,1)S(1)}, bf16[2,192,256]{2,1,0:T(8,128)(2,1)}, u32[]{:S(2)}, u32[]{:S(2)}) collective-permute-start(bf16[2,192,256]{2,1,0:T(8,128)(2,1)S(1)} %pad_maximum_fusion.10), channel_id=1, source_target_pairs={{0,8},{4,12},{8,0},{12,4},{16,24},{20,28},{24,16},{28,20},{1,9},{5... | collective-permute-start | bytes 589832 | tf_op jit(solution)/shard_map/ppermute | solution.py:539
  85.0 21.7 %collective-permute-start.26 = (bf16[4,2,96,256]{3,2,1,0:T(8,128)(2,1)}, bf16[4,2,96,256]{3,2,1,0:T(8,128)(2,1)S(1)}, u32[]{:S(2)}, u32[]{:S(2)}) collective-permute-start(bf16[4,2,96,256]{3,2,1,0:T(8,128)(2,1)} %get-tuple-element.430), channel_id=1, source_target_pairs={{0,2},{1,3},{2,0},{3,1},{4,6},{5,7},{6,4},{7,5},{8,10},{9,11},{10,... | collective-permute-start | bytes 1179656 | tf_op jit(solution)/shard_map/ppermute | solution.py:539
  86.6 20.1 %collective-permute-start.25 = (bf16[4,2,96,256]{3,2,1,0:T(8,128)(2,1)S(1)}, bf16[4,2,96,256]{3,2,1,0:T(8,128)(2,1)S(1)}, u32[]{:S(2)}, u32[]{:S(2)}) collective-permute-start(bf16[4,2,96,256]{3,2,1,0:T(8,128)(2,1)S(1)} %get-tuple-element.432), channel_id=1, source_target_pairs={{0,4},{4,0},{8,12},{12,8},{16,20},{20,16},{24,28},{28,24},{1,5},{5... | collective-permute-start | bytes 1179656 | tf_op jit(solution)/shard_map/ppermute | solution.py:539
  106.8 17.1 %collective-permute-start.27 = (bf16[2,4,2,96,256]{4,3,2,1,0:T(8,128)(2,1)S(1)}, bf16[2,4,2,96,256]{4,3,2,1,0:T(8,128)(2,1)}, u32[]{:S(2)}, u32[]{:S(2)}) collective-permute-start(bf16[2,4,2,96,256]{4,3,2,1,0:T(8,128)(2,1)S(1)} %pad_maximum_fusion.rest_0_), channel_id=1, source_target_pairs={{0,2},{1,3},{2,0},{3,1},{4,6},{5,7},{6,4},{7,5},{8,10},{9,11},{10,... | collective-permute-start | bytes 2359304 | tf_op jit(solution)/shard_map/ppermute | solution.py:539
  107.9 17.1 %collective-permute-start.28 = (bf16[2,4,2,96,256]{4,3,2,1,0:T(8,128)(2,1)S(1)}, bf16[2,4,2,96,256]{4,3,2,1,0:T(8,128)(2,1)}, u32[]{:S(2)}, u32[]{:S(2)}) collective-permute-start(bf16[2,4,2,96,256]{4,3,2,1,0:T(8,128)(2,1)S(1)} %pad_maximum_fusion.1.rest_2_), channel_id=1, source_target_pairs={{0,4},{4,0},{8,12},{12,8},{16,20},{20,16},{24,28},{28,24},{1,5},{5... | collective-permute-start | bytes 2359304 | tf_op jit(solution)/shard_map/ppermute | solution.py:539
  110.1 14.9 %collective-permute-start.24 = (bf16[2,4,1,96,256]{4,3,1,2,0:T(8,128)(2,1)S(1)}, bf16[2,4,1,96,256]{4,3,1,2,0:T(8,128)(2,1)}, u32[]{:S(2)}, u32[]{:S(2)}) collective-permute-start(bf16[2,4,1,96,256]{4,3,1,2,0:T(8,128)(2,1)S(1)} %copy-done.43), channel_id=1, source_target_pairs={{0,1},{1,0},{2,3},{3,2},{4,5},{5,4},{6,7},{7,6},{8,9},{9,8},{10,11... | collective-permute-start | bytes 1179656 | tf_op jit(solution)/shard_map/ppermute | solution.py:539
  110.9 51.5 %collective-permute-start.29 = (bf16[2,4,2,96,256]{4,3,2,1,0:T(8,128)(2,1)S(1)}, bf16[2,4,2,96,256]{4,3,2,1,0:T(8,128)(2,1)}, u32[]{:S(2)}, u32[]{:S(2)}) collective-permute-start(bf16[2,4,2,96,256]{4,3,2,1,0:T(8,128)(2,1)S(1)} %pad_maximum_fusion.rest_0_), channel_id=1, source_target_pairs={{0,1},{1,0},{2,3},{3,2},{4,5},{5,4},{6,7},{7,6},{8,9},{9,8},{10,11... | collective-permute-start | bytes 2359304 | tf_op jit(solution)/shard_map/ppermute | solution.py:539
  111.2 51.3 %collective-permute-start.31 = (bf16[2,4,2,96,256]{4,3,2,1,0:T(8,128)(2,1)S(1)}, bf16[2,4,2,96,256]{4,3,2,1,0:T(8,128)(2,1)}, u32[]{:S(2)}, u32[]{:S(2)}) collective-permute-start(bf16[2,4,2,96,256]{4,3,2,1,0:T(8,128)(2,1)S(1)} %pad_maximum_fusion.1.rest_2_), channel_id=1, source_target_pairs={{0,1},{1,0},{2,3},{3,2},{4,5},{5,4},{6,7},{7,6},{8,9},{9,8},{10,11... | collective-permute-start | bytes 2359304 | tf_op jit(solution)/shard_map/ppermute | solution.py:539
  123.9 39.0 %collective-permute-start.30 = (bf16[2,4,2,96,256]{4,3,2,1,0:T(8,128)(2,1)}, bf16[2,4,2,96,256]{4,3,2,1,0:T(8,128)(2,1)}, u32[]{:S(2)}, u32[]{:S(2)}) collective-permute-start(bf16[2,4,2,96,256]{4,3,2,1,0:T(8,128)(2,1)} %collective-permute-done.27.rest_1_.refs_6_), channel_id=1, source_target_pairs={{0,1},{1,0},{2,3},{3,2},{4,5},{5,4},{6,7},{7,6},{8,9},{9,8},{10,11... | collective-permute-start | bytes 2359304 | tf_op jit(solution)/shard_map/ppermute | solution.py:539
  125.0 38.0 %collective-permute-start.32 = (bf16[2,4,2,96,256]{4,3,2,1,0:T(8,128)(2,1)}, bf16[2,4,2,96,256]{4,3,2,1,0:T(8,128)(2,1)}, u32[]{:S(2)}, u32[]{:S(2)}) collective-permute-start(bf16[2,4,2,96,256]{4,3,2,1,0:T(8,128)(2,1)} %collective-permute-done.28.rest_3_.refs_7_), channel_id=1, source_target_pairs={{0,1},{1,0},{2,3},{3,2},{4,5},{5,4},{6,7},{7,6},{8,9},{9,8},{10,11... | collective-permute-start | bytes 2359304 | tf_op jit(solution)/shard_map/ppermute | solution.py:539
  161.9 29.9 %collective-permute-start.33 = (bf16[2,2,192,256]{3,2,1,0:T(8,128)(2,1)}, bf16[2,2,192,256]{3,2,1,0:T(8,128)(2,1)S(1)}, u32[]{:S(2)}, u32[]{:S(2)}) collective-permute-start(bf16[2,2,192,256]{3,2,1,0:T(8,128)(2,1)} %get-tuple-element.221), channel_id=1, source_target_pairs={{0,1},{1,0},{2,3},{3,2},{4,5},{5,4},{6,7},{7,6},{8,9},{9,8},{10,11... | collective-permute-start | bytes 1179656 | tf_op jit(solution)/shard_map/ppermute | solution.py:539
  162.4 29.4 %collective-permute-start.34 = (bf16[2,2,192,256]{3,2,1,0:T(8,128)(2,1)}, bf16[2,2,192,256]{3,2,1,0:T(8,128)(2,1)S(1)}, u32[]{:S(2)}, u32[]{:S(2)}) collective-permute-start(bf16[2,2,192,256]{3,2,1,0:T(8,128)(2,1)} %get-tuple-element.222), channel_id=1, source_target_pairs={{0,1},{1,0},{2,3},{3,2},{4,5},{5,4},{6,7},{7,6},{8,9},{9,8},{10,11... | collective-permute-start | bytes 1179656 | tf_op jit(solution)/shard_map/ppermute | solution.py:539
  162.5 29.3 %collective-permute-start.35 = (bf16[2,2,192,256]{3,2,1,0:T(8,128)(2,1)}, bf16[2,2,192,256]{3,2,1,0:T(8,128)(2,1)S(1)}, u32[]{:S(2)}, u32[]{:S(2)}) collective-permute-start(bf16[2,2,192,256]{3,2,1,0:T(8,128)(2,1)} %get-tuple-element.223), channel_id=1, source_target_pairs={{0,1},{1,0},{2,3},{3,2},{4,5},{5,4},{6,7},{7,6},{8,9},{9,8},{10,11... | collective-permute-start | bytes 1179656 | tf_op jit(solution)/shard_map/ppermute | solution.py:539
  162.9 28.9 %collective-permute-start.36 = (bf16[2,2,192,256]{3,2,1,0:T(8,128)(2,1)}, bf16[2,2,192,256]{3,2,1,0:T(8,128)(2,1)S(1)}, u32[]{:S(2)}, u32[]{:S(2)}) collective-permute-start(bf16[2,2,192,256]{3,2,1,0:T(8,128)(2,1)} %get-tuple-element.224), channel_id=1, source_target_pairs={{0,1},{1,0},{2,3},{3,2},{4,5},{5,4},{6,7},{7,6},{8,9},{9,8},{10,11... | collective-permute-start | bytes 1179656 | tf_op jit(solution)/shard_map/ppermute | solution.py:539
  196.2 34.1 %collective-permute-start.37 = (bf16[1,8,192,256]{3,2,1,0:T(8,128)(2,1)}, bf16[1,8,192,256]{3,2,1,0:T(8,128)(2,1)S(1)}, u32[]{:S(2)}, u32[]{:S(2)}) collective-permute-start(bf16[1,8,192,256]{3,2,1,0:T(8,128)(2,1)} %get-tuple-element.229), channel_id=1, source_target_pairs={{0,2},{1,3},{2,0},{3,1},{4,6},{5,7},{6,4},{7,5},{8,10},{9,11},{10,... | collective-permute-start | bytes 2359304 | tf_op jit(solution)/shard_map/ppermute | solution.py:539
  197.0 32.5 %collective-permute-start.38 = (bf16[2,2,192,256]{3,2,1,0:T(8,128)(2,1)}, bf16[2,2,192,256]{3,2,1,0:T(8,128)(2,1)S(1)}, u32[]{:S(2)}, u32[]{:S(2)}) collective-permute-start(bf16[2,2,192,256]{3,2,1,0:T(8,128)(2,1)} %get-tuple-element.244), channel_id=1, source_target_pairs={{0,1},{1,0},{2,3},{3,2},{4,5},{5,4},{6,7},{7,6},{8,9},{9,8},{10,11... | collective-permute-start | bytes 1179656 | tf_op jit(solution)/shard_map/ppermute | solution.py:539
  197.2 32.6 %collective-permute-start.39 = (bf16[2,2,192,256]{3,2,1,0:T(8,128)(2,1)}, bf16[2,2,192,256]{3,2,1,0:T(8,128)(2,1)S(1)}, u32[]{:S(2)}, u32[]{:S(2)}) collective-permute-start(bf16[2,2,192,256]{3,2,1,0:T(8,128)(2,1)} %get-tuple-element.245), channel_id=1, source_target_pairs={{0,1},{1,0},{2,3},{3,2},{4,5},{5,4},{6,7},{7,6},{8,9},{9,8},{10,11... | collective-permute-start | bytes 1179656 | tf_op jit(solution)/shard_map/ppermute | solution.py:539
  197.5 32.6 %collective-permute-start.40 = (bf16[2,2,192,256]{3,2,1,0:T(8,128)(2,1)}, bf16[2,2,192,256]{3,2,1,0:T(8,128)(2,1)S(1)}, u32[]{:S(2)}, u32[]{:S(2)}) collective-permute-start(bf16[2,2,192,256]{3,2,1,0:T(8,128)(2,1)} %get-tuple-element.246), channel_id=1, source_target_pairs={{0,1},{1,0},{2,3},{3,2},{4,5},{5,4},{6,7},{7,6},{8,9},{9,8},{10,11... | collective-permute-start | bytes 1179656 | tf_op jit(solution)/shard_map/ppermute | solution.py:539
  197.7 40.6 %collective-permute-start.41 = (bf16[2,2,192,256]{3,2,1,0:T(8,128)(2,1)}, bf16[2,2,192,256]{3,2,1,0:T(8,128)(2,1)S(1)}, u32[]{:S(2)}, u32[]{:S(2)}) collective-permute-start(bf16[2,2,192,256]{3,2,1,0:T(8,128)(2,1)} %get-tuple-element.247), channel_id=1, source_target_pairs={{0,1},{1,0},{2,3},{3,2},{4,5},{5,4},{6,7},{7,6},{8,9},{9,8},{10,11... | collective-permute-start | bytes 1179656 | tf_op jit(solution)/shard_map/ppermute | solution.py:539
  245.1 22.2 %collective-permute-start.49 = (bf16[1,8,192,256]{3,2,1,0:T(8,128)(2,1)}, bf16[1,8,192,256]{3,2,1,0:T(8,128)(2,1)S(1)}, u32[]{:S(2)}, u32[]{:S(2)}) collective-permute-start(bf16[1,8,192,256]{3,2,1,0:T(8,128)(2,1)} %get-tuple-element.265), channel_id=1, source_target_pairs={{0,2},{1,3},{2,0},{3,1},{4,6},{5,7},{6,4},{7,5},{8,10},{9,11},{10,... | collective-permute-start | bytes 2359304 | tf_op jit(solution)/shard_map/ppermute | solution.py:539
  246.3 21.0 %collective-permute-start.50 = (bf16[1,8,192,256]{3,2,1,0:T(8,128)(2,1)}, bf16[1,8,192,256]{3,2,1,0:T(8,128)(2,1)S(1)}, u32[]{:S(2)}, u32[]{:S(2)}) collective-permute-start(bf16[1,8,192,256]{3,2,1,0:T(8,128)(2,1)} %get-tuple-element.267), channel_id=1, source_target_pairs={{0,4},{4,0},{8,12},{12,8},{16,20},{20,16},{24,28},{28,24},{1,5},{5... | collective-permute-start | bytes 2359304 | tf_op jit(solution)/shard_map/ppermute | solution.py:539
  247.5 19.6 %collective-permute-start.46 = (bf16[1,2,192,256]{3,2,1,0:T(8,128)(2,1)}, bf16[1,2,192,256]{3,2,1,0:T(8,128)(2,1)S(1)}, u32[]{:S(2)}, u32[]{:S(2)}) collective-permute-start(bf16[1,2,192,256]{3,2,1,0:T(8,128)(2,1)} %get-tuple-element.261), channel_id=1, source_target_pairs={{0,8},{4,12},{8,0},{12,4},{16,24},{20,28},{24,16},{28,20},{1,9},{5... | collective-permute-start | bytes 589832 | tf_op jit(solution)/shard_map/ppermute | solution.py:539
  248.0 19.1 %collective-permute-start.47 = (bf16[1,2,192,256]{3,2,1,0:T(8,128)(2,1)}, bf16[1,2,192,256]{3,2,1,0:T(8,128)(2,1)S(1)}, u32[]{:S(2)}, u32[]{:S(2)}) collective-permute-start(bf16[1,2,192,256]{3,2,1,0:T(8,128)(2,1)} %get-tuple-element.262), channel_id=1, source_target_pairs={{0,16},{4,20},{8,24},{12,28},{16,0},{20,4},{24,8},{28,12},{1,17},{... | collective-permute-start | bytes 589832 | tf_op jit(solution)/shard_map/ppermute | solution.py:539
  249.9 17.3 %collective-permute-start.48 = (bf16[1,2,192,256]{3,2,1,0:T(8,128)(2,1)}, bf16[1,2,192,256]{3,2,1,0:T(8,128)(2,1)S(1)}, u32[]{:S(2)}, u32[]{:S(2)}) collective-permute-start(bf16[1,2,192,256]{3,2,1,0:T(8,128)(2,1)} %get-tuple-element.263), channel_id=1, source_target_pairs={{0,24},{4,28},{8,16},{12,20},{16,8},{20,12},{24,0},{28,4},{1,25},{... | collective-permute-start | bytes 589832 | tf_op jit(solution)/shard_map/ppermute | solution.py:539
  282.0 15.2 %collective-permute-start.51 = (bf16[2,2,192,384]{3,2,1,0:T(8,128)(2,1)}, bf16[2,2,192,384]{3,2,1,0:T(8,128)(2,1)S(1)}, u32[]{:S(2)}, u32[]{:S(2)}) collective-permute-start(bf16[2,2,192,384]{3,2,1,0:T(8,128)(2,1)} %get-tuple-element.269.refs_7_), channel_id=1, source_target_pairs={{0,1},{1,0},{2,3},{3,2},{4,5},{5,4},{6,7},{7,6},{8,9},{9,8},{10,11... | collective-permute-start | bytes 1769480 | tf_op jit(solution)/shard_map/ppermute | solution.py:539
  282.0 15.2 %collective-permute-start.52 = (bf16[2,2,192,384]{3,2,1,0:T(8,128)(2,1)}, bf16[2,2,192,384]{3,2,1,0:T(8,128)(2,1)S(1)}, u32[]{:S(2)}, u32[]{:S(2)}) collective-permute-start(bf16[2,2,192,384]{3,2,1,0:T(8,128)(2,1)} %get-tuple-element.270), channel_id=1, source_target_pairs={{0,1},{1,0},{2,3},{3,2},{4,5},{5,4},{6,7},{7,6},{8,9},{9,8},{10,11... | collective-permute-start | bytes 1769480 | tf_op jit(solution)/shard_map/ppermute | solution.py:539
  282.5 14.7 %collective-permute-start.53 = (bf16[2,2,192,384]{3,2,1,0:T(8,128)(2,1)}, bf16[2,2,192,384]{3,2,1,0:T(8,128)(2,1)S(1)}, u32[]{:S(2)}, u32[]{:S(2)}) collective-permute-start(bf16[2,2,192,384]{3,2,1,0:T(8,128)(2,1)} %get-tuple-element.271), channel_id=1, source_target_pairs={{0,1},{1,0},{2,3},{3,2},{4,5},{5,4},{6,7},{7,6},{8,9},{9,8},{10,11... | collective-permute-start | bytes 1769480 | tf_op jit(solution)/shard_map/ppermute | solution.py:539
  304.8 31.5 %collective-permute-start.58 = (bf16[1,8,96,384]{3,2,1,0:T(8,128)(2,1)}, bf16[1,8,96,384]{3,2,1,0:T(8,128)(2,1)S(1)}, u32[]{:S(2)}, u32[]{:S(2)}) collective-permute-start(bf16[1,8,96,384]{3,2,1,0:T(8,128)(2,1)} %get-tuple-element.280), channel_id=1, source_target_pairs={{0,4},{4,0},{8,12},{12,8},{16,20},{20,16},{24,28},{28,24},{1,5},{5... | collective-permute-start | bytes 1769480 | tf_op jit(solution)/shard_map/ppermute | solution.py:539
  306.4 29.9 %collective-permute-start.59 = (bf16[1,8,96,384]{3,2,1,0:T(8,128)(2,1)}, bf16[1,8,96,384]{3,2,1,0:T(8,128)(2,1)S(1)}, u32[]{:S(2)}, u32[]{:S(2)}) collective-permute-start(bf16[1,8,96,384]{3,2,1,0:T(8,128)(2,1)} %get-tuple-element.282), channel_id=1, source_target_pairs={{0,2},{1,3},{2,0},{3,1},{4,6},{5,7},{6,4},{7,5},{8,10},{9,11},{10,... | collective-permute-start | bytes 1769480 | tf_op jit(solution)/shard_map/ppermute | solution.py:539
  307.6 28.8 %all-to-all-start = ((bf16[4,1,192,256]{3,2,1,0:T(8,128)(2,1)}), bf16[4,1,192,256]{3,2,1,0:T(8,128)(2,1)S(1)}, u32[]{:S(2)}, u32[]{:S(2)}) async-start(bf16[4,1,192,256]{3,2,1,0:T(8,128)(2,1)} %get-tuple-element.290), calls=%async_computation | async-start | bytes 786432 | tf_op jit(solution)/shard_map/all_to_all | solution.py:691
  346.7 30.1 %collective-permute-start.74 = (f32[7,128,128]{2,1,0:T(8,128)S(1)}, f32[7,128,128]{2,1,0:T(8,128)S(1)}, u32[]{:S(2)}, u32[]{:S(2)}) collective-permute-start(f32[7,128,128]{2,1,0:T(8,128)S(1)} %add.211), channel_id=1, source_target_pairs={{0,2},{1,3},{2,0},{3,1},{4,6},{5,7},{6,4},{7,5},{8,10},{9,11},{10,... | collective-permute-start | bytes 1376264 | tf_op jit(solution)/shard_map/ppermute | solution.py:539
  349.5 17.7 %collective-permute-start.67 = (bf16[1,4,96,384]{3,2,1,0:T(8,128)(2,1)}, bf16[1,4,96,384]{3,2,1,0:T(8,128)(2,1)S(1)}, u32[]{:S(2)}, u32[]{:S(2)}) collective-permute-start(bf16[1,4,96,384]{3,2,1,0:T(8,128)(2,1)} %get-tuple-element.296), channel_id=1, source_target_pairs={{0,4},{4,0},{8,12},{12,8},{16,20},{20,16},{24,28},{28,24},{1,5},{5... | collective-permute-start | bytes 884744 | tf_op jit(solution)/shard_map/ppermute | solution.py:539
  370.0 20.4 %collective-permute-start.69 = (bf16[1,1,96,384]{3,2,1,0:T(8,128)(2,1)}, bf16[1,1,96,384]{3,2,1,0:T(8,128)(2,1)S(1)}, u32[]{:S(2)}, u32[]{:S(2)}) collective-permute-start(bf16[1,1,96,384]{3,2,1,0:T(8,128)(2,1)} %get-tuple-element.301), channel_id=1, source_target_pairs={{0,2},{1,3},{2,0},{3,1},{4,6},{5,7},{6,4},{7,5},{8,10},{9,11},{10,... | collective-permute-start | bytes 221192 | tf_op jit(solution)/shard_map/ppermute | solution.py:539
  370.9 19.5 %collective-permute-start.70 = (bf16[1,1,96,384]{3,2,1,0:T(8,128)(2,1)}, bf16[1,1,96,384]{3,2,1,0:T(8,128)(2,1)S(1)}, u32[]{:S(2)}, u32[]{:S(2)}) collective-permute-start(bf16[1,1,96,384]{3,2,1,0:T(8,128)(2,1)} %get-tuple-element.303), channel_id=1, source_target_pairs={{0,8},{4,12},{8,0},{12,4},{16,24},{20,28},{24,16},{28,20},{1,9},{5... | collective-permute-start | bytes 221192 | tf_op jit(solution)/shard_map/ppermute | solution.py:539
  374.5 16.0 %collective-permute-start.71 = (bf16[1,1,96,384]{3,2,1,0:T(8,128)(2,1)}, bf16[1,1,96,384]{3,2,1,0:T(8,128)(2,1)S(1)}, u32[]{:S(2)}, u32[]{:S(2)}) collective-permute-start(bf16[1,1,96,384]{3,2,1,0:T(8,128)(2,1)} %get-tuple-element.304), channel_id=1, source_target_pairs={{0,16},{4,20},{8,24},{12,28},{16,0},{20,4},{24,8},{28,12},{1,17},{... | collective-permute-start | bytes 221192 | tf_op jit(solution)/shard_map/ppermute | solution.py:539
  375.3 15.2 %collective-permute-start.72 = (bf16[1,1,96,384]{3,2,1,0:T(8,128)(2,1)}, bf16[1,1,96,384]{3,2,1,0:T(8,128)(2,1)S(1)}, u32[]{:S(2)}, u32[]{:S(2)}) collective-permute-start(bf16[1,1,96,384]{3,2,1,0:T(8,128)(2,1)} %get-tuple-element.305), channel_id=1, source_target_pairs={{0,24},{4,28},{8,16},{12,20},{16,8},{20,12},{24,0},{28,4},{1,25},{... | collective-permute-start | bytes 221192 | tf_op jit(solution)/shard_map/ppermute | solution.py:539
  376.8 16.7 %collective-permute-start.75 = (f32[1,4,1,256]{3,2,1,0:T(1,128)}, f32[1,4,1,256]{3,2,1,0:T(1,128)S(1)}, u32[]{:S(2)}, u32[]{:S(2)}) collective-permute-start(f32[1,4,1,256]{3,2,1,0:T(1,128)} %get-tuple-element.313), channel_id=1, source_target_pairs={{0,4},{4,0},{8,12},{12,8},{16,20},{20,16},{24,28},{28,24},{1,5},{5... | collective-permute-start | bytes 12296 | tf_op jit(solution)/shard_map/ppermute | solution.py:539
  393.5 27.1 %collective-permute-start.79 = (f32[4,96,96]{2,1,0:T(8,128)}, f32[4,96,96]{2,1,0:T(8,128)S(1)}, u32[]{:S(2)}, u32[]{:S(2)}) collective-permute-start(f32[4,96,96]{2,1,0:T(8,128)} %get-tuple-element.314.refs_3_.refs_8_), channel_id=1, source_target_pairs={{0,1},{1,0},{2,3},{3,2},{4,5},{5,4},{6,7},{7,6},{8,9},{9,8},{10,11... | collective-permute-start | bytes 442376 | tf_op jit(solution)/shard_map/ppermute | solution.py:539
  395.4 23.2 %collective-permute-start.78 = (f32[1,1,1,256]{3,2,1,0:T(1,128)}, f32[1,1,1,256]{3,2,1,0:T(1,128)S(1)}, u32[]{:S(2)}, u32[]{:S(2)}) collective-permute-start(f32[1,1,1,256]{3,2,1,0:T(1,128)} %get-tuple-element.318), channel_id=1, source_target_pairs={{0,24},{4,28},{8,16},{12,20},{16,8},{20,12},{24,0},{28,4},{1,25},{... | collective-permute-start | bytes 3080 | tf_op jit(solution)/shard_map/ppermute | solution.py:539
  397.8 20.9 %collective-permute-start.77 = (f32[1,1,1,256]{3,2,1,0:T(1,128)}, f32[1,1,1,256]{3,2,1,0:T(1,128)S(1)}, u32[]{:S(2)}, u32[]{:S(2)}) collective-permute-start(f32[1,1,1,256]{3,2,1,0:T(1,128)} %get-tuple-element.317), channel_id=1, source_target_pairs={{0,16},{4,20},{8,24},{12,28},{16,0},{20,4},{24,8},{28,12},{1,17},{... | collective-permute-start | bytes 3080 | tf_op jit(solution)/shard_map/ppermute | solution.py:539
  398.0 20.6 %collective-permute-start.76 = (f32[1,1,1,256]{3,2,1,0:T(1,128)}, f32[1,1,1,256]{3,2,1,0:T(1,128)S(1)}, u32[]{:S(2)}, u32[]{:S(2)}) collective-permute-start(f32[1,1,1,256]{3,2,1,0:T(1,128)} %get-tuple-element.316), channel_id=1, source_target_pairs={{0,8},{4,12},{8,0},{12,4},{16,24},{20,28},{24,16},{28,20},{1,9},{5... | collective-permute-start | bytes 3080 | tf_op jit(solution)/shard_map/ppermute | solution.py:539
  (118 other events, 992.7 us)
